TPU v7x, 128 devices: a whole 4x4x4 slice. The times are simulated.
128 devices in a mesh: expert: 8 (over x_hi, z), fsdp: 16 (over x_lo, y, core).
Axes of the slice: x: 4 (x_hi: 2, x_lo: 2; x = x_hi * 2 + x_lo), y: 4, z: 4, core: 2. Of those that a mesh axis runs over, the one named last changes fastest.
Arguments:
- tokens: bfloat16 [16384, 1536], P(('expert', 'fsdp')), may hold values from -6 to 6
- cotangent: bfloat16 [16384, 1536], P(('expert', 'fsdp')), may hold values from -6 to 6
- routes: int32 [16384, 8], P(('expert', 'fsdp')), may hold values from 0 to 39, all different within a row; in each aligned block of 128 rows (0 to 127, 128 to 255, ...) at most 32 rows name the same one
- norm_one: bfloat16 [1536], P('fsdp'), may hold values from 0.5 to 1.5
- w_query: bfloat16 [1536, 1536], P('fsdp'), may hold values from -0.15625 to 0.15625
- key_weight: bfloat16 [1536, 512], P('fsdp'), may hold values from -0.15625 to 0.15625
- value_weight: bfloat16 [1536, 512], P('fsdp'), may hold values from -0.15625 to 0.15625
- w_out: bfloat16 [1536, 1536], P('fsdp'), may hold values from -0.4375 to 0.4375
- norm_two: bfloat16 [1536], P('fsdp'), may hold values from 0.5 to 1.5
- w_router: bfloat16 [1536, 40], P('fsdp'), may hold values from -0.078125 to 0.078125
- w_gate: bfloat16 [40, 1536, 512], P('expert', 'fsdp'), may hold values from -0.15625 to 0.15625
- w_up: bfloat16 [40, 1536, 512], P('expert', 'fsdp'), may hold values from -0.15625 to 0.15625
- w_down: bfloat16 [40, 512, 1536], P('expert', None, 'fsdp'), may hold values from -0.75 to 0.75
Outputs:
- mixed_out: bfloat16 [16384, 1536], P(('expert', 'fsdp'))
- grad_tokens: float32 [16384, 1536], P(('expert', 'fsdp'))
- grad_norm_one: float32 [1536], P('fsdp')
- grad_query: float32 [1536, 1536], P('fsdp')
- grad_key: float32 [1536, 512], P('fsdp')
- grad_value: float32 [1536, 512], P('fsdp')
- grad_out: float32 [1536, 1536], P('fsdp')
- grad_norm_two: float32 [1536], P('fsdp')
- grad_router: float32 [1536, 40], P('fsdp')
- grad_gate: float32 [40, 1536, 512], P('expert', 'fsdp')
- grad_up: float32 [40, 1536, 512], P('expert', 'fsdp')
- grad_down: float32 [40, 512, 1536], P('expert', None, 'fsdp')
Inputs may be any that keep to these rules, and one draw needn't show every extreme that they name: In the rows of one device, no expert is named by more than 32 routes, a bound that some block reaches; the 8 experts of a token differ.
All inputs are finite; a program needn't handle non-finite values.
Results may differ from a plain program's by a relative error of at most 0.025.
Values may be sent and summed in bfloat16 or wider, within the bound.
No kernel may reach another device: no remote copies, remote signals or barrier semaphores. Data moves between devices by JAX's collectives and lax.ppermute only.
A program may use at most 192 MiB of HBM per device.

v0:
```python
import jax
import jax.numpy as jnp
from jax import lax
from jax.sharding import PartitionSpec as P

QUERY_HEADS = 24
KEY_VALUE_HEADS = 8
HEAD_DIM = 64
E = 40
TOPK = 8


NORM_EPSILON = 1e-05


def rope_tables(sequence_length):
    half_dim = HEAD_DIM // 2
    frequency = jnp.exp(
        -jnp.log(10000.0) * jnp.arange(half_dim, dtype=jnp.float32) * 2.0 / HEAD_DIM
    )
    angles = jnp.arange(sequence_length, dtype=jnp.float32)[:, None] * frequency[None, :]
    cosine_table = jnp.concatenate([jnp.cos(angles), jnp.cos(angles)], axis=1)[:, None, :]
    sines_lookup = jnp.concatenate([jnp.sin(angles), jnp.sin(angles)], axis=1)[:, None, :]
    return (cosine_table, sines_lookup)


def apply_rotary(values, cosine_table, sines_lookup):
    half_dim = values.shape[-1] // 2
    turned = jnp.concatenate([-values[..., half_dim:], values[..., :half_dim]], axis=-1)
    return values * cosine_table + turned * sines_lookup


def rotate_back(grad_values, cosine_table, sines_lookup):
    half_dim = grad_values.shape[-1] // 2
    scaled = grad_values * sines_lookup
    unturned = jnp.concatenate([scaled[..., half_dim:], -scaled[..., :half_dim]], axis=-1)
    return grad_values * cosine_table + unturned


def norm_back(grad_normed, normed, inverse_rms, gain):
    grad_gain = jnp.sum(grad_normed * normed, axis=0)
    scaled = grad_normed * gain
    grad_input = inverse_rms * (scaled - normed * jnp.mean(scaled * normed, axis=-1, keepdims=True))
    return (grad_input, grad_gain)


def masked_scores(query_block, key_rows, row_start, score_scale):
    rows_here = query_block.shape[0]
    scores = (
        jnp.einsum("qhgd,khd->hgqk", query_block, key_rows, preferred_element_type=jnp.float32)
        * score_scale
    )
    query_pos = row_start + jnp.arange(rows_here, dtype=jnp.int32)
    visible = query_pos[:, None] >= jnp.arange(key_rows.shape[0], dtype=jnp.int32)[None, :]
    return jnp.where(visible, scores, -jnp.inf)


def attend_forward(query_rows, key_rows, rows_of_value):
    sequence_length = query_rows.shape[0]
    block_rows = min(sequence_length, 512)
    score_scale = HEAD_DIM ** (-0.5)

    def one_block(row_start):
        scores = masked_scores(query_rows, key_rows, row_start, score_scale)
        row_peak = jnp.max(scores, axis=-1, keepdims=True)
        exponent = jnp.exp(scores - row_peak)
        row_total = jnp.sum(exponent, axis=-1, keepdims=True)
        probability = (exponent / row_total).astype(jnp.bfloat16)
        attended = jnp.einsum(
            "hgqk,khd->qhgd", probability, rows_of_value, preferred_element_type=jnp.float32
        )
        return (attended, (row_peak + jnp.log(row_total))[..., 0])

    starts = jnp.arange(sequence_length // block_rows, dtype=jnp.int32) * block_rows
    attended, log_total = lax.map(one_block, starts)
    return (attended.reshape((sequence_length,) + attended.shape[2:]), log_total)


def attend_backward(query_rows, key_rows, rows_of_value, log_total, attended_gradient):
    sequence_length = query_rows.shape[0]
    block_rows = min(sequence_length, 512)
    score_scale = HEAD_DIM ** (-0.5)

    def one_block(running, inputs):
        row_start, block_log = inputs
        scores = masked_scores(query_rows, key_rows, row_start, score_scale)
        probability = jnp.exp(scores - block_log[..., None])
        grad_prob = jnp.einsum(
            "qhgd,khd->hgqk", attended_gradient, rows_of_value, preferred_element_type=jnp.float32
        )
        row_inner = jnp.sum(probability * grad_prob, axis=-1, keepdims=True)
        grad_scores = (probability * (grad_prob - row_inner)).astype(jnp.bfloat16)
        grad_query = (
            jnp.einsum("hgqk,khd->qhgd", grad_scores, key_rows, preferred_element_type=jnp.float32)
            * score_scale
        )
        grad_keys = (
            running[0]
            + jnp.einsum(
                "hgqk,qhgd->khd", grad_scores, query_rows, preferred_element_type=jnp.float32
            )
            * score_scale
        )
        grad_values = running[1] + jnp.einsum(
            "hgqk,qhgd->khd",
            probability.astype(jnp.bfloat16),
            attended_gradient,
            preferred_element_type=jnp.float32,
        )
        return ((grad_keys, grad_values), grad_query)

    starts = jnp.arange(sequence_length // block_rows, dtype=jnp.int32) * block_rows
    zeros_kv = jnp.zeros(key_rows.shape, jnp.float32)
    (grad_keys, grad_values), grad_query = lax.scan(
        one_block, (zeros_kv, zeros_kv), (starts, log_total)
    )
    return (grad_query.reshape((sequence_length,) + grad_query.shape[2:]), grad_keys, grad_values)


def body(
    tokens,
    cotangent,
    routes,
    norm_one,
    w_query,
    key_weight,
    value_weight,
    w_out,
    norm_two,
    w_router,
    w_gate,
    w_up,
    w_down,
):
    sequence_length = tokens.shape[0]
    model_width = tokens.shape[1]
    grouped_heads = QUERY_HEADS // KEY_VALUE_HEADS
    slot_count = sequence_length // 4
    cosine_table, sines_lookup = rope_tables(sequence_length)
    attn_full = (
        lax.all_gather(norm_one, "fsdp", axis=0, tiled=True),
        lax.all_gather(w_query, "fsdp", axis=0, tiled=True),
        lax.all_gather(key_weight, "fsdp", axis=0, tiled=True),
        lax.all_gather(value_weight, "fsdp", axis=0, tiled=True),
        lax.all_gather(w_out, "fsdp", axis=0, tiled=True),
        lax.all_gather(norm_two, "fsdp", axis=0, tiled=True),
        lax.all_gather(w_router, "fsdp", axis=0, tiled=True),
    )
    gain_one, query_full, key_full, value_full, out_full, gain_two, router_full = attn_full
    gate_full, up_full, down_full = (
        lax.all_gather(w_gate, "fsdp", axis=1, tiled=True),
        lax.all_gather(w_up, "fsdp", axis=1, tiled=True),
        lax.all_gather(w_down, "fsdp", axis=2, tiled=True),
    )
    gain_one = gain_one.astype(jnp.float32)
    gain_two = gain_two.astype(jnp.float32)
    source = tokens.astype(jnp.float32)
    inverse_one = lax.rsqrt(jnp.mean(source * source, axis=-1, keepdims=True) + NORM_EPSILON)
    normed_one = source * inverse_one
    first_hidden = (normed_one * gain_one).astype(jnp.bfloat16)
    query_proj = jnp.dot(first_hidden, query_full, preferred_element_type=jnp.float32).reshape(
        sequence_length, QUERY_HEADS, HEAD_DIM
    )
    query_rows = (
        apply_rotary(query_proj, cosine_table, sines_lookup)
        .astype(jnp.bfloat16)
        .reshape(sequence_length, KEY_VALUE_HEADS, grouped_heads, HEAD_DIM)
    )
    key_proj = jnp.dot(first_hidden, key_full, preferred_element_type=jnp.float32).reshape(
        sequence_length, KEY_VALUE_HEADS, HEAD_DIM
    )
    key_rows = apply_rotary(key_proj, cosine_table, sines_lookup).astype(jnp.bfloat16)
    rows_of_value = (
        jnp.dot(first_hidden, value_full, preferred_element_type=jnp.float32)
        .astype(jnp.bfloat16)
        .reshape(sequence_length, KEY_VALUE_HEADS, HEAD_DIM)
    )
    attended, log_total = attend_forward(query_rows, key_rows, rows_of_value)
    attended_low = attended.reshape(sequence_length, QUERY_HEADS * HEAD_DIM).astype(jnp.bfloat16)
    residual = source + jnp.dot(attended_low, out_full, preferred_element_type=jnp.float32)
    inverse_two = lax.rsqrt(jnp.mean(residual * residual, axis=-1, keepdims=True) + NORM_EPSILON)
    normed_two = residual * inverse_two
    hidden_two = (normed_two * gain_two).astype(jnp.bfloat16)
    logits = jnp.dot(hidden_two, router_full, preferred_element_type=jnp.float32)
    member = routes[:, :, None] == jnp.arange(E, dtype=jnp.int32)[None, None, :]
    chosen = jnp.sum(jnp.where(member, logits[:, None, :], 0.0), axis=-1)
    gate_peak = jnp.max(chosen, axis=-1, keepdims=True)
    gate_exp = jnp.exp(chosen - gate_peak)
    gate_weights = gate_exp / jnp.sum(gate_exp, axis=-1, keepdims=True)
    route_flat = routes.reshape(-1)
    route_count = route_flat.shape[0]
    onehot = (route_flat[:, None] == jnp.arange(E, dtype=jnp.int32)[None, :]).astype(jnp.int32)
    place_slot = jnp.sum(onehot * (jnp.cumsum(onehot, axis=0) - 1), axis=1)
    destination = route_flat * slot_count + place_slot
    table_route = (
        jnp.full((E * slot_count,), route_count, jnp.int32)
        .at[destination]
        .set(jnp.arange(route_count, dtype=jnp.int32))
    )
    table_token = jnp.where(table_route < route_count, table_route // TOPK, sequence_length)
    padded_rows = jnp.concatenate([hidden_two, jnp.zeros((1, model_width), jnp.bfloat16)], axis=0)
    send_rows = padded_rows[table_token].reshape(E, slot_count, model_width)
    arrived = lax.all_to_all(send_rows, "expert", split_axis=0, concat_axis=1, tiled=True)
    gate_pre = jnp.einsum("esd,edh->esh", arrived, gate_full, preferred_element_type=jnp.float32)
    up_pre = jnp.einsum("esd,edh->esh", arrived, up_full, preferred_element_type=jnp.float32)
    sigmoid_gate = jax.nn.sigmoid(gate_pre)
    silu_gate = gate_pre * sigmoid_gate
    activated = (silu_gate * up_pre).astype(jnp.bfloat16)
    expert_result = jnp.einsum(
        "esh,ehd->esd", activated, down_full, preferred_element_type=jnp.float32
    ).astype(jnp.bfloat16)
    returned = lax.all_to_all(expert_result, "expert", split_axis=1, concat_axis=0, tiled=True)
    route_rows = (
        returned.reshape(E * slot_count, model_width)[destination]
        .reshape(sequence_length, TOPK, model_width)
        .astype(jnp.float32)
    )
    output = residual + jnp.sum(gate_weights[:, :, None] * route_rows, axis=1)
    mixed_out = output.astype(jnp.bfloat16)
    again = (
        lax.all_gather(w_query, "fsdp", axis=0, tiled=True),
        lax.all_gather(key_weight, "fsdp", axis=0, tiled=True),
        lax.all_gather(value_weight, "fsdp", axis=0, tiled=True),
        lax.all_gather(w_out, "fsdp", axis=0, tiled=True),
        lax.all_gather(w_router, "fsdp", axis=0, tiled=True),
    )
    query_back, key_back, value_back, out_back, router_back = again
    gate_back, up_back, down_back = (
        lax.all_gather(w_gate, "fsdp", axis=1, tiled=True),
        lax.all_gather(w_up, "fsdp", axis=1, tiled=True),
        lax.all_gather(w_down, "fsdp", axis=2, tiled=True),
    )
    grad_out_rows = cotangent.astype(jnp.float32)
    grad_routes = (gate_weights[:, :, None] * grad_out_rows[:, None, :]).reshape(
        route_count, model_width
    )
    grad_routes = jnp.concatenate([grad_routes, jnp.zeros((1, model_width), jnp.float32)], axis=0)
    grad_send = grad_routes[table_route].astype(jnp.bfloat16).reshape(E, slot_count, model_width)
    grad_arrived = lax.all_to_all(grad_send, "expert", split_axis=0, concat_axis=1, tiled=True)
    grad_gates = jnp.sum(grad_out_rows[:, None, :] * route_rows, axis=-1)
    grad_chosen = gate_weights * (
        grad_gates - jnp.sum(gate_weights * grad_gates, axis=-1, keepdims=True)
    )
    grad_logits = jnp.sum(jnp.where(member, grad_chosen[:, :, None], 0.0), axis=1).astype(
        jnp.bfloat16
    )
    grad_act = jnp.einsum(
        "esd,ehd->esh", grad_arrived, down_back, preferred_element_type=jnp.float32
    )
    grad_gate_pre = (
        grad_act * up_pre * sigmoid_gate * (1.0 + gate_pre * (1.0 - sigmoid_gate))
    ).astype(jnp.bfloat16)
    grad_up_pre = (grad_act * silu_gate).astype(jnp.bfloat16)
    grad_rows = jnp.einsum(
        "esh,edh->esd", grad_gate_pre, gate_back, preferred_element_type=jnp.float32
    )
    grad_rows = (
        grad_rows
        + jnp.einsum("esh,edh->esd", grad_up_pre, up_back, preferred_element_type=jnp.float32)
    ).astype(jnp.bfloat16)
    grad_back = lax.all_to_all(grad_rows, "expert", split_axis=1, concat_axis=0, tiled=True)
    grad_down_local = jnp.einsum(
        "esh,esd->ehd", activated, grad_arrived, preferred_element_type=jnp.float32
    )
    grad_gate_local = jnp.einsum(
        "esd,esh->edh", arrived, grad_gate_pre, preferred_element_type=jnp.float32
    )
    grad_up_local = jnp.einsum(
        "esd,esh->edh", arrived, grad_up_pre, preferred_element_type=jnp.float32
    )
    grad_gate_w, grad_up_w, grad_down_w = (
        lax.psum_scatter(
            grad_gate_local.astype(jnp.bfloat16), "fsdp", scatter_dimension=1, tiled=True
        ).astype(jnp.float32),
        lax.psum_scatter(
            grad_up_local.astype(jnp.bfloat16), "fsdp", scatter_dimension=1, tiled=True
        ).astype(jnp.float32),
        lax.psum_scatter(
            grad_down_local.astype(jnp.bfloat16), "fsdp", scatter_dimension=2, tiled=True
        ).astype(jnp.float32),
    )
    back_rows = (
        grad_back.reshape(E * slot_count, model_width)[destination]
        .reshape(sequence_length, TOPK, model_width)
        .astype(jnp.float32)
    )
    grad_hidden_two = jnp.sum(back_rows, axis=1) + jnp.dot(
        grad_logits, router_back.T, preferred_element_type=jnp.float32
    )
    grad_router_local = jnp.dot(hidden_two.T, grad_logits, preferred_element_type=jnp.float32)
    grad_from_two, grad_gain_two = norm_back(grad_hidden_two, normed_two, inverse_two, gain_two)
    grad_residual = grad_out_rows + grad_from_two
    grad_branch = grad_residual.astype(jnp.bfloat16)
    grad_out_local = jnp.dot(attended_low.T, grad_branch, preferred_element_type=jnp.float32)
    attended_gradient = jnp.dot(grad_branch, out_back.T, preferred_element_type=jnp.float32).astype(
        jnp.bfloat16
    )
    attended_gradient = attended_gradient.reshape(
        sequence_length, KEY_VALUE_HEADS, grouped_heads, HEAD_DIM
    )
    grad_query_rows, grad_key_rows, value_rows_gradient = attend_backward(
        query_rows, key_rows, rows_of_value, log_total, attended_gradient
    )
    grad_query_proj = (
        rotate_back(
            grad_query_rows.reshape(sequence_length, QUERY_HEADS, HEAD_DIM),
            cosine_table,
            sines_lookup,
        )
        .astype(jnp.bfloat16)
        .reshape(sequence_length, QUERY_HEADS * HEAD_DIM)
    )
    grad_key_proj = (
        rotate_back(grad_key_rows, cosine_table, sines_lookup)
        .astype(jnp.bfloat16)
        .reshape(sequence_length, KEY_VALUE_HEADS * HEAD_DIM)
    )
    value_projection_gradient = value_rows_gradient.astype(jnp.bfloat16).reshape(
        sequence_length, KEY_VALUE_HEADS * HEAD_DIM
    )
    grad_query_local = jnp.dot(first_hidden.T, grad_query_proj, preferred_element_type=jnp.float32)
    grad_key_local = jnp.dot(first_hidden.T, grad_key_proj, preferred_element_type=jnp.float32)
    grad_value_local = jnp.dot(
        first_hidden.T, value_projection_gradient, preferred_element_type=jnp.float32
    )
    grad_hidden_one = jnp.dot(grad_query_proj, query_back.T, preferred_element_type=jnp.float32)
    grad_hidden_one = grad_hidden_one + jnp.dot(
        grad_key_proj, key_back.T, preferred_element_type=jnp.float32
    )
    grad_hidden_one = grad_hidden_one + jnp.dot(
        value_projection_gradient, value_back.T, preferred_element_type=jnp.float32
    )
    grad_from_one, grad_gain_one = norm_back(grad_hidden_one, normed_one, inverse_one, gain_one)
    grad_tokens = grad_residual + grad_from_one
    weight_grads = (
        grad_gain_one,
        grad_query_local,
        grad_key_local,
        grad_value_local,
        grad_out_local,
        grad_gain_two,
        grad_router_local,
    )
    shares = (
        lax.psum_scatter(
            weight_grads[0].astype(jnp.bfloat16), "fsdp", scatter_dimension=0, tiled=True
        ).astype(jnp.float32),
        lax.psum_scatter(
            weight_grads[1].astype(jnp.bfloat16), "fsdp", scatter_dimension=0, tiled=True
        ).astype(jnp.float32),
        lax.psum_scatter(
            weight_grads[2].astype(jnp.bfloat16), "fsdp", scatter_dimension=0, tiled=True
        ).astype(jnp.float32),
        lax.psum_scatter(
            weight_grads[3].astype(jnp.bfloat16), "fsdp", scatter_dimension=0, tiled=True
        ).astype(jnp.float32),
        lax.psum_scatter(
            weight_grads[4].astype(jnp.bfloat16), "fsdp", scatter_dimension=0, tiled=True
        ).astype(jnp.float32),
        lax.psum_scatter(
            weight_grads[5].astype(jnp.bfloat16), "fsdp", scatter_dimension=0, tiled=True
        ).astype(jnp.float32),
        lax.psum_scatter(
            weight_grads[6].astype(jnp.bfloat16), "fsdp", scatter_dimension=0, tiled=True
        ).astype(jnp.float32),
    )
    totals = (
        lax.psum(shares[0].astype(jnp.bfloat16), "expert").astype(jnp.float32),
        lax.psum(shares[1].astype(jnp.bfloat16), "expert").astype(jnp.float32),
        lax.psum(shares[2].astype(jnp.bfloat16), "expert").astype(jnp.float32),
        lax.psum(shares[3].astype(jnp.bfloat16), "expert").astype(jnp.float32),
        lax.psum(shares[4].astype(jnp.bfloat16), "expert").astype(jnp.float32),
        lax.psum(shares[5].astype(jnp.bfloat16), "expert").astype(jnp.float32),
        lax.psum(shares[6].astype(jnp.bfloat16), "expert").astype(jnp.float32),
    )
    grad_norm_one, grad_query, grad_key, grad_value, grad_out, grad_norm_two, grad_router = totals
    return (
        mixed_out,
        grad_tokens,
        grad_norm_one,
        grad_query,
        grad_key,
        grad_value,
        grad_out,
        grad_norm_two,
        grad_router,
        grad_gate_w,
        grad_up_w,
        grad_down_w,
    )


def solution(mesh):
    return jax.shard_map(
        body,
        mesh=mesh,
        in_specs=(
            P(("expert", "fsdp"), None),
            P(("expert", "fsdp"), None),
            P(("expert", "fsdp"), None),
            P("fsdp"),
            P("fsdp", None),
            P("fsdp", None),
            P("fsdp", None),
            P("fsdp", None),
            P("fsdp"),
            P("fsdp", None),
            P("expert", "fsdp", None),
            P("expert", "fsdp", None),
            P("expert", None, "fsdp"),
        ),
        out_specs=(
            P(("expert", "fsdp"), None),
            P(("expert", "fsdp"), None),
            P("fsdp"),
            P("fsdp", None),
            P("fsdp", None),
            P("fsdp", None),
            P("fsdp", None),
            P("fsdp"),
            P("fsdp", None),
            P("expert", "fsdp", None),
            P("expert", "fsdp", None),
            P("expert", None, "fsdp"),
        ),
        check_vma=False,
    )
```

profile of v0, /device:TPU:0, one launch (start us, length us, event | category | flops | bytes accessed | tf_op | source)
XLA Modules:
  0.0 1247.1 jit_solution(4199540957345102978)
XLA Ops:
  17.3 31.3 %all-reduce.7 = (bf16[1536]{0:T(1024)(128)(2,1)S(1)}, bf16[1536]{0:T(1024)(128)(2,1)S(1)}) all-reduce(bf16[1536]{0:T(1024)(128)(2,1)S(1)} %dynamic-update-slice, bf16[1536]{0:T(1024)(128)(2,1)S(1)} %dynamic-update-slice.1), channel_id=1, replica_groups=mesh['expert'=8,'fsdp'=16] {'fsdp'}, use_global_device_ids=true, to_apply=%add.2 | all-reduce | flops 3072 | bytes 12288
  48.9 11.3 reduce-window.6
  60.6 16.6 %all-gather = bf16[16,96,40]{1,2,0:T(8,128)(2,1)S(1)} all-gather(bf16[1,96,40]{1,2,0:T(8,128)(2,1)S(1)} %bitcast.189), channel_id=1, replica_groups=mesh['expert'=8,'fsdp'=16] {'fsdp'}, dimensions={0}, use_global_device_ids=true | all-gather | bytes 130560 | tf_op jit(solution)/shard_map/all_gather | solution.py:147
  77.6 4.3 scatter_custom_fusion
  87.8 33.2 %all-gather.13.cloned.1.call-done = bf16[1536,1536]{1,0:T(8,128)(2,1)} async-done(((bf16[96,1536]{1,0:T(8,128)(2,1)}), bf16[1536,1536]{1,0:T(8,128)(2,1)}) %all-gather.13.cloned.1.call-update) | async-done | bytes 4718608 | tf_op jit(solution)/shard_map/all_gather | solution.py:142
  121.1 4.3 fusion.49
  128.5 32.8 %all-gather.15.cloned.1.call-done = bf16[1536,1536]{1,0:T(8,128)(2,1)} async-done(((bf16[96,1536]{1,0:T(8,128)(2,1)}), bf16[1536,1536]{1,0:T(8,128)(2,1)}) %all-gather.15.cloned.1.call-update) | async-done | bytes 4718608 | tf_op jit(solution)/shard_map/all_gather | solution.py:145
  168.1 5.4 gather_fusion.2
  173.5 6.7 all-to-all-start.2
  180.3 5.5 gather_fusion
  185.8 68.7 %all-to-all-done.2 = bf16[40,32,1536]{2,1,0:T(8,128)(2,1)} async-done(((bf16[40,32,1536]{2,1,0:T(8,128)(2,1)}), bf16[40,32,1536]{2,1,0:T(8,128)(2,1)}, u32[]{:S(2)}, u32[]{:S(2)}) %all-to-all-start.2) | async-done | bytes 3932192 | tf_op jit(solution)/shard_map/all_to_all | solution.py:239
  254.5 4.8 all-to-all-start
  259.3 4.6 copy.138
  263.9 71.9 %all-to-all-done = bf16[40,32,1536]{2,1,0:T(8,128)(2,1)} async-done(((bf16[40,32,1536]{2,1,0:T(8,128)(2,1)}), bf16[40,32,1536]{2,1,0:T(8,128)(2,1)}, u32[]{:S(2)}, u32[]{:S(2)}) %all-to-all-start) | async-done | bytes 3932192 | tf_op jit(solution)/shard_map/all_to_all | solution.py:203
  335.8 4.5 copy.134
  340.2 8.4 fusion.60
  348.6 8.4 fusion.59
  357.0 18.3 %all-gather.21.cloned.1.call-done = bf16[5,512,1536]{1,2,0:T(8,128)(2,1)} async-done(((bf16[5,512,96]{1,2,0:T(8,128)(2,1)}), bf16[5,512,1536]{1,2,0:T(8,128)(2,1)}) %all-gather.21.cloned.1.call-update) | async-done | bytes 7864336 | tf_op jit(solution)/shard_map/all_gather | solution.py:153
  375.3 9.8 multiply_convert_fusion
  387.4 7.7 add_convert_fusion
  395.1 7.2 copy.139
  402.2 19.7 %all-to-all-start.3 = ((bf16[5,256,1536]{2,0,1:T(8,128)(2,1)}), bf16[5,256,1536]{2,0,1:T(8,128)(2,1)}, u32[]{:S(2)}, u32[]{:S(2)}) async-start(bf16[5,256,1536]{2,0,1:T(8,128)(2,1)} %copy.139), calls=%async_computation.3 | async-start | bytes 12582912 | tf_op jit(solution)/shard_map/all_to_all | solution.py:261
  422.0 5.5 convolution_convert_fusion.5
  427.5 4.9 copy.135
  432.4 61.4 %all-to-all-done.3 = bf16[5,256,1536]{2,0,1:T(8,128)(2,1)} async-done(((bf16[5,256,1536]{2,0,1:T(8,128)(2,1)}), bf16[5,256,1536]{2,0,1:T(8,128)(2,1)}, u32[]{:S(2)}, u32[]{:S(2)}) %all-to-all-start.3) | async-done | bytes 3932192 | tf_op jit(solution)/shard_map/all_to_all | solution.py:261
  493.8 4.8 all-to-all-start.1
  499.2 6.2 copy.140
  505.4 9.3 gather_fusion.3
  517.7 52.5 %all-to-all-done.1 = bf16[5,256,1536]{2,0,1:T(8,128)(2,1)} async-done(((bf16[5,256,1536]{2,0,1:T(8,128)(2,1)}), bf16[5,256,1536]{2,0,1:T(8,128)(2,1)}, u32[]{:S(2)}, u32[]{:S(2)}) %all-to-all-start.1) | async-done | bytes 3932192 | tf_op jit(solution)/shard_map/all_to_all | solution.py:212
  570.2 6.3 copy.136
  576.5 10.0 gather_fusion.1
  586.5 4.0 fusion.1
  593.4 4.1 convolution_convert_fusion.8
  611.0 3.7 convolution_convert_fusion.1
  616.9 46.2 %reduce-scatter.15.cloned.1.call-done = bf16[96,512]{1,0:T(8,128)(2,1)} async-done(((bf16[1536,512]{1,0:T(8,128)(2,1)}), bf16[96,512]{1,0:T(8,128)(2,1)}) %reduce-scatter.15.cloned.1.call-update) | async-done | bytes 98320 | tf_op jit(solution)/shard_map/reduce_scatter | solution.py:354
  663.1 63.5 %reduce-scatter.13.cloned.1.call-done = bf16[96,512]{1,0:T(8,128)(2,1)} async-done(((bf16[1536,512]{1,0:T(8,128)(2,1)}), bf16[96,512]{1,0:T(8,128)(2,1)}) %reduce-scatter.13.cloned.1.call-update) | async-done | bytes 98320 | tf_op jit(solution)/shard_map/reduce_scatter | solution.py:351
  726.6 68.7 %reduce-scatter.17.cloned.1.call-done = bf16[96,1536]{1,0:T(8,128)(2,1)} async-done(((bf16[1536,1536]{1,0:T(8,128)(2,1)}), bf16[96,1536]{1,0:T(8,128)(2,1)}) %reduce-scatter.17.cloned.1.call-update) | async-done | bytes 294928 | tf_op jit(solution)/shard_map/reduce_scatter | solution.py:357
  795.3 68.9 %reduce-scatter.11.cloned.1.call-done = bf16[96,1536]{1,0:T(8,128)(2,1)} async-done(((bf16[1536,1536]{1,0:T(8,128)(2,1)}), bf16[96,1536]{1,0:T(8,128)(2,1)}) %reduce-scatter.11.cloned.1.call-update) | async-done | bytes 294928 | tf_op jit(solution)/shard_map/reduce_scatter | solution.py:348
  864.3 7.8 convolution_convert_fusion.2
  873.4 7.5 convolution_convert_fusion.3
  882.2 7.5 convolution_convert_fusion.4
  890.5 4.1 fusion.62
  896.2 27.9 %all-reduce.6 = (bf16[1536]{0:T(1024)(128)(2,1)S(1)}, bf16[1536]{0:T(1024)(128)(2,1)S(1)}) all-reduce(bf16[1536]{0:T(1024)(128)(2,1)S(1)} %get-tuple-element.61, bf16[1536]{0:T(1024)(128)(2,1)S(1)} %get-tuple-element.50), channel_id=2, replica_groups=mesh['expert'=8,'fsdp'=16] {'fsdp'}, use_global_device_ids=true, to_apply=%region_20.21.clone | all-reduce | flops 3072 | bytes 12288
  926.8 41.7 %all-reduce.8 = (bf16[96]{0:T(256)(128)(2,1)S(1)}, bf16[96]{0:T(256)(128)(2,1)S(1)}, bf16[96,40]{0,1:T(8,128)(2,1)S(1)}) all-reduce(bf16[96]{0:T(256)(128)(2,1)S(1)} %dynamic-slice.3, bf16[96]{0:T(256)(128)(2,1)S(1)} %dynamic-slice.5, bf16[96,40]{0,1:T(8,128)(2,1)S(1)} %copy.164), channel_id=1, replica_groups=mesh['expert'=8,'fsdp'=16] {'expert'}, use_global_device_ids=true, to_apply=%region_21.22 | all-reduce | flops 4032 | bytes 16128 | tf_op jit(solution)/shard_map/psum | solution.py:368
  970.2 44.3 %all-reduce.12.cloned.1.call-done = (bf16[96,1536]{1,0:T(8,128)(2,1)}, bf16[96,512]{1,0:T(8,128)(2,1)}, bf16[96,512]{1,0:T(8,128)(2,1)}, bf16[96,1536]{1,0:T(8,128)(2,1)}) async-done(((bf16[96,1536]{1,0:T(8,128)(2,1)}, bf16[96,512]{1,0:T(8,128)(2,1)}, bf16[96,512]{1,0:T(8,128)(2,1)}, bf16[96,1536]{1,0:T(8,128)(2,1)}), (bf16[96,1536]{1,0:T(8,128)(2,1)}, bf16[96,512]{1,0:T(8,128)(2,1)}, ...) | async-done | bytes 786448 | tf_op jit(solution)/shard_map/psum | solution.py:369
  1021.3 66.9 %reduce-scatter.23.cloned.1.call-done = bf16[5,512,96]{1,2,0:T(8,128)(2,1)} async-done(((bf16[5,512,1536]{1,2,0:T(8,128)(2,1)}), bf16[5,512,96]{1,2,0:T(8,128)(2,1)}) %reduce-scatter.23.cloned.1.call-update) | async-done | bytes 491536 | tf_op jit(solution)/shard_map/reduce_scatter | solution.py:278
  1090.4 72.9 %reduce-scatter.21.cloned.1.call-done = bf16[5,96,512]{2,1,0:T(8,128)(2,1)} async-done(((bf16[5,1536,512]{2,1,0:T(8,128)(2,1)}), bf16[5,96,512]{2,1,0:T(8,128)(2,1)}) %reduce-scatter.21.cloned.1.call-update) | async-done | bytes 491536 | tf_op jit(solution)/shard_map/reduce_scatter | solution.py:275
  1165.3 72.7 %reduce-scatter.19.cloned.1.call-done = bf16[5,96,512]{2,1,0:T(8,128)(2,1)} async-done(((bf16[5,1536,512]{2,1,0:T(8,128)(2,1)}), bf16[5,96,512]{2,1,0:T(8,128)(2,1)}) %reduce-scatter.19.cloned.1.call-update) | async-done | bytes 491536 | tf_op jit(solution)/shard_map/reduce_scatter | solution.py:272
  (256 shorter events, 71.4 us)
Async XLA Ops:
  7.2 53.4 %copy-start.53 = (bf16[96,40]{0,1:T(8,128)(2,1)S(1)}, bf16[96,40]{0,1:T(8,128)(2,1)}, u32[]{:S(2)}) copy-start(bf16[96,40]{0,1:T(8,128)(2,1)} %param.22) | copy-start | bytes 23044
  7.2 70.2 %copy-start.24 = (bf16[128,1536]{1,0:T(8,128)(2,1)S(1)}, bf16[128,1536]{1,0:T(8,128)(2,1)}, u32[]{:S(2)}) copy-start(bf16[128,1536]{1,0:T(8,128)(2,1)} %param.14) | copy-start | bytes 1179652
  7.2 76.3 %all-gather.9.cloned.1.call-start = ((), (), s32[]{:S(2)}) async-start(), calls=%async_computation.12 | async-start | bytes 1671168 | tf_op jit(solution)/shard_map/all_gather | solution.py:144
  7.9 77.6 %all-gather.11.cloned.1.call-start = ((), (), s32[]{:S(2)}) async-start(), calls=%async_computation.13 | async-start | bytes 1671168 | tf_op jit(solution)/shard_map/all_gather | solution.py:143
  8.7 74.7 %copy-start.3 = (bf16[128,1536]{1,0:T(8,128)(2,1)S(1)}, bf16[128,1536]{1,0:T(8,128)(2,1)}, u32[]{:S(2)}) copy-start(bf16[128,1536]{1,0:T(8,128)(2,1)} %param.13) | copy-start | bytes 1179652
  8.7 112.4 %all-gather.13.cloned.1.call-start = ((), (), s32[]{:S(2)}) async-start(), calls=%async_computation.14 | async-start | bytes 5013504 | tf_op jit(solution)/shard_map/all_gather | solution.py:142
  9.4 151.9 %all-gather.15.cloned.1.call-start = ((), (), s32[]{:S(2)}) async-start(), calls=%async_computation.15 | async-start | bytes 5013504 | tf_op jit(solution)/shard_map/all_gather | solution.py:145
  10.0 330.2 %all-gather.19.cloned.1.call-start = ((), (), s32[]{:S(2)}) async-start(), calls=%async_computation.17 | async-start | bytes 8355840 | tf_op jit(solution)/shard_map/all_gather | solution.py:152
  10.6 338.0 %all-gather.17.cloned.1.call-start = ((), (), s32[]{:S(2)}) async-start(), calls=%async_computation.16 | async-start | bytes 8355840 | tf_op jit(solution)/shard_map/all_gather | solution.py:151
  11.2 364.1 %all-gather.21.cloned.1.call-start = ((), (), s32[]{:S(2)}) async-start(), calls=%async_computation.18 | async-start | bytes 8355840 | tf_op jit(solution)/shard_map/all_gather | solution.py:153
  48.6 116.0 %copy-start.42 = (f32[1536]{0:T(1024)}, f32[1536]{0:T(1024)S(1)}, u32[]{:S(2)}) copy-start(f32[1536]{0:T(1024)S(1)} %convert_element_type.201) | copy-start | bytes 18436
  77.4 88.2 %copy-start.31 = (bf16[1536,40]{0,1:T(8,128)(2,1)}, bf16[1536,40]{0,1:T(8,128)(2,1)S(1)}, u32[]{:S(2)}) copy-start(bf16[1536,40]{0,1:T(8,128)(2,1)S(1)} %reshape.344) | copy-start | bytes 368644
  77.5 89.4 %copy-start.9 = (f32[128,1536]{1,0:T(8,128)}, f32[128,1536]{1,0:T(8,128)S(1)}, u32[]{:S(2)}) copy-start(f32[128,1536]{1,0:T(8,128)S(1)} %convert_element_type.209) | copy-start | bytes 2359300
  82.7 42.8 %copy-start.35 = (f32[128,64]{0,1:T(8,128)}, f32[128,64]{0,1:T(8,128)S(1)}, u32[]{:S(2)}) copy-start(f32[128,64]{0,1:T(8,128)S(1)} %get-tuple-element.88) | copy-start | bytes 98308
  83.3 42.2 %copy-start.37 = (f32[128,64]{0,1:T(8,128)}, f32[128,64]{0,1:T(8,128)S(1)}, u32[]{:S(2)}) copy-start(f32[128,64]{0,1:T(8,128)S(1)} %get-tuple-element.90) | copy-start | bytes 98308
  83.5 41.9 %copy-start.49 = (f32[128]{0:T(128)}, f32[128]{0:T(128)S(1)}, u32[]{:S(2)}) copy-start(f32[128]{0:T(128)S(1)} %add_rsqrt_fusion.1) | copy-start | bytes 1540
  85.5 41.7 %copy-start.39 = (bf16[128,512]{0,1:T(8,128)(2,1)}, bf16[128,512]{0,1:T(8,128)(2,1)S(1)}, u32[]{:S(2)}) copy-start(bf16[128,512]{0,1:T(8,128)(2,1)S(1)} %copy.122) | copy-start | bytes 393220
  87.8 37.8 %copy-start.29 = (bf16[128,8,64,1]{0,2,3,1:T(8,128)(2,1)}, bf16[128,8,64,1]{0,2,3,1:T(8,128)(2,1)S(1)}, u32[]{:S(2)}) copy-start(bf16[128,8,64,1]{0,2,3,1:T(8,128)(2,1)S(1)} %fusion.34) | copy-start | bytes 393220
  128.4 36.1 %copy-start.21 = (bf16[8,64,3,128]{3,1,2,0:T(8,128)(2,1)}, bf16[8,64,3,128]{3,1,2,0:T(8,128)(2,1)S(1)}, u32[]{:S(2)}) copy-start(bf16[8,64,3,128]{3,1,2,0:T(8,128)(2,1)S(1)} %convolution_convert_fusion.10) | copy-start | bytes 1179652
  161.3 5.2 copy-start.48
  173.5 6.7 copy-start.13
  173.5 81.0 %all-to-all-start.2 = ((bf16[40,32,1536]{2,1,0:T(8,128)(2,1)}), bf16[40,32,1536]{2,1,0:T(8,128)(2,1)}, u32[]{:S(2)}, u32[]{:S(2)}) async-start(bf16[40,32,1536]{2,1,0:T(8,128)(2,1)} %bitcast.167), calls=%async_computation.2 | async-start | bytes 7864320 | tf_op jit(solution)/shard_map/all_to_all | solution.py:239
  254.5 81.2 %all-to-all-start = ((bf16[40,32,1536]{2,1,0:T(8,128)(2,1)}), bf16[40,32,1536]{2,1,0:T(8,128)(2,1)}, u32[]{:S(2)}, u32[]{:S(2)}) async-start(bf16[40,32,1536]{2,1,0:T(8,128)(2,1)} %bitcast.166), calls=%async_computation | async-start | bytes 7864320 | tf_op jit(solution)/shard_map/all_to_all | solution.py:203
  375.3 9.8 copy-start
  402.2 19.8 %copy-start.17 = (bf16[5,256,512]{2,1,0:T(8,128)(2,1)S(1)}, bf16[5,256,512]{2,1,0:T(8,128)(2,1)}, u32[]{:S(2)}) copy-start(bf16[5,256,512]{2,1,0:T(8,128)(2,1)} %get-tuple-element.76) | copy-start | bytes 3932164
  402.2 91.6 %all-to-all-start.3 = ((bf16[5,256,1536]{2,0,1:T(8,128)(2,1)}), bf16[5,256,1536]{2,0,1:T(8,128)(2,1)}, u32[]{:S(2)}, u32[]{:S(2)}) async-start(bf16[5,256,1536]{2,0,1:T(8,128)(2,1)} %copy.139), calls=%async_computation.3 | async-start | bytes 12582912 | tf_op jit(solution)/shard_map/all_to_all | solution.py:261
  493.8 76.4 %all-to-all-start.1 = ((bf16[5,256,1536]{2,0,1:T(8,128)(2,1)}), bf16[5,256,1536]{2,0,1:T(8,128)(2,1)}, u32[]{:S(2)}, u32[]{:S(2)}) async-start(bf16[5,256,1536]{2,0,1:T(8,128)(2,1)} %copy.135), calls=%async_computation.1 | async-start | bytes 12582912 | tf_op jit(solution)/shard_map/all_to_all | solution.py:212
  498.6 164.5 %reduce-scatter.15.cloned.1.call-start = ((), (), s32[]{:S(2)}) async-start(), calls=%async_computation.21 | async-start | bytes 1671168 | tf_op jit(solution)/shard_map/reduce_scatter | solution.py:354
  576.5 10.0 copy-start.10
  576.5 10.0 copy-start.34
  586.5 4.3 copy-start.6
  586.5 4.3 copy-start.20
  593.4 4.4 copy-start.2
  593.4 6.3 copy-start.4
  593.4 6.3 copy-start.50
  601.6 125.0 %reduce-scatter.13.cloned.1.call-start = ((), (), s32[]{:S(2)}) async-start(), calls=%async_computation.20 | async-start | bytes 1671168 | tf_op jit(solution)/shard_map/reduce_scatter | solution.py:351
  603.9 5.6 copy-start.27
  605.7 189.6 %reduce-scatter.17.cloned.1.call-start = ((), (), s32[]{:S(2)}) async-start(), calls=%async_computation.22 | async-start | bytes 5013504 | tf_op jit(solution)/shard_map/reduce_scatter | solution.py:357
  609.5 254.7 %reduce-scatter.11.cloned.1.call-start = ((), (), s32[]{:S(2)}) async-start(), calls=%async_computation.19 | async-start | bytes 5013504 | tf_op jit(solution)/shard_map/reduce_scatter | solution.py:348
  614.7 311.3 %reduce-scatter.25.cloned.1.call-start = ((), (), s32[]{:S(2)}) async-start(), calls=%async_computation.26 | async-start | bytes 417792
  616.8 397.7 %all-reduce.12.cloned.1.call-start = ((), (), s32[]{:S(2)}) async-start(), calls=%async_computation.27 | async-start | bytes 1572864 | tf_op jit(solution)/shard_map/psum | solution.py:369
  864.2 224.0 %reduce-scatter.23.cloned.1.call-start = ((), (), s32[]{:S(2)}) async-start(), calls=%async_computation.25 | async-start | bytes 8355840 | tf_op jit(solution)/shard_map/reduce_scatter | solution.py:278
  872.1 291.1 %reduce-scatter.21.cloned.1.call-start = ((), (), s32[]{:S(2)}) async-start(), calls=%async_computation.24 | async-start | bytes 8355840 | tf_op jit(solution)/shard_map/reduce_scatter | solution.py:275
  880.9 357.1 %reduce-scatter.19.cloned.1.call-start = ((), (), s32[]{:S(2)}) async-start(), calls=%async_computation.23 | async-start | bytes 8355840 | tf_op jit(solution)/shard_map/reduce_scatter | solution.py:272
  889.7 5.0 copy-start.11
  889.7 5.0 copy-start.28
  890.5 4.8 copy-start.23
  890.5 4.8 copy-start.26
  (30 other events, 58.2 us)
Sparse Core Ops, SparseCore 0:
  9.7 35.7 all-gather.8
  47.2 33.5 all-gather.10
  82.6 38.4 all-gather.12
  122.7 38.5 all-gather.14
  162.8 78.8 all-gather.18
  243.2 81.0 all-gather.16
  326.0 49.3 all-gather.20
  601.7 61.3 reduce-scatter.14
  665.6 60.9 reduce-scatter.12
  728.9 66.3 reduce-scatter.16
  797.7 66.4 reduce-scatter.10
  867.0 58.9 reduce-scatter.24
  929.0 85.4 all-reduce.11
  1016.8 71.4 reduce-scatter.22
  1090.5 72.6 reduce-scatter.20
  1165.5 72.4 reduce-scatter.18
where the time goes:
time: 1260 us; the launch traced here: 1250 us
  waiting for transfers between devices  848 us (67%)
  blocking collectives  117 us (9%)
  matrix products  101 us (8%)
  local copies, waits for them, and re-layouts  84.2 us (7%)
  other arithmetic  42.2 us (3%)
  starting transfers between devices  37.1 us (3%)
  between operations  16.9 us (1%)
    reduce_scatter x1, waiting for transfers between devices, body(): lax.psum_scatter(grad_up_local.astype(jnp.bfloat16), 'fsdp', scatter_dime...  72.9 us
    reduce_scatter x1, waiting for transfers between devices, body(): lax.psum_scatter(grad_gate_local.astype(jnp.bfloat16), 'fsdp', scatter_di...  72.7 us
    all_to_all x1, waiting for transfers between devices, body(): lax.all_to_all(send_rows, 'expert', split_axis=0, concat_axis=1, tiled=True)  71.9 us
    reduce_scatter x1, waiting for transfers between devices, body(): lax.psum_scatter(weight_grads[1].astype(jnp.bfloat16), 'fsdp', scatter_di...  68.9 us
    all_to_all x1, waiting for transfers between devices, body(): lax.all_to_all(grad_send, 'expert', split_axis=0, concat_axis=1, tiled=True)  68.7 us
    reduce_scatter x1, waiting for transfers between devices, body(): lax.psum_scatter(weight_grads[4].astype(jnp.bfloat16), 'fsdp', scatter_di...  68.7 us
    reduce_scatter x1, waiting for transfers between devices, body(): lax.psum_scatter(grad_down_local.astype(jnp.bfloat16), 'fsdp', scatter_di...  66.9 us
    reduce_scatter x1, waiting for transfers between devices, body(): lax.psum_scatter(weight_grads[2].astype(jnp.bfloat16), 'fsdp', scatter_di...  63.5 us
  transfers between devices with their start and end apart: 20, of which 16 were waited for; matrix products, arithmetic and copies ran while one was open for 13% of the time, Pallas kernels for 0%

commit v1 on v0

v1 whole, which is shorter than its diff:
```python
import functools

import jax
import jax.numpy as jnp
import numpy as np
from jax import lax
from jax.experimental import pallas as pl
from jax.experimental.pallas import tpu as pltpu
from jax.sharding import PartitionSpec as P

QUERY_HEADS = 24
KEY_VALUE_HEADS = 8
GROUP = QUERY_HEADS // KEY_VALUE_HEADS
HEAD_DIM = 64
HALF = HEAD_DIM // 2
E = 40
H = 512
D = 1536
T = 128
CAP = 32
NORM_EPSILON = 1e-05
SCALE = HEAD_DIM ** (-0.5)

Z = 4
PEERS = 8
LOCAL = E // PEERS
SLOTS = LOCAL * CAP
LANES = 128
BLOCK = 512
PACK = 4096 + LANES
VMEM_LIMIT = 60 * 1024 * 1024

F32 = jnp.float32
BF16 = jnp.bfloat16


def peer(index, hop, back=False):
    shift = hop % Z
    turned = (index % Z + (Z - shift if back else shift)) % Z
    return (index // Z + hop // Z) % 2 * Z + turned


def send(value, hop, back=False):
    if hop == 0:
        return value
    return lax.ppermute(value, "expert", [(i, peer(i, hop, back)) for i in range(PEERS)])


def mm(left, right):
    return jnp.dot(left, right, preferred_element_type=F32)


def mm_nt(left, right):
    return lax.dot_general(left, right, (((1,), (1,)), ((), ())), preferred_element_type=F32)


def mm_tn(left, right):
    return lax.dot_general(left, right, (((0,), (0,)), ((), ())), preferred_element_type=F32)


def rope_tables():
    frequency = np.exp(-np.log(10000.0) * np.arange(HALF, dtype=np.float64) * 2.0 / HEAD_DIM)
    angles = np.arange(T, dtype=np.float64)[:, None] * frequency[None, :]
    cosine = np.tile(np.cos(angles), (1, 4)).astype(np.float32)
    sine = np.sin(angles)
    signed = np.tile(np.concatenate([-sine, sine], axis=1), (1, 2)).astype(np.float32)
    return cosine, signed


def swap_halves(values):
    width = values.shape[1]
    lane = lax.broadcasted_iota(jnp.int32, values.shape, 1)
    up = pltpu.roll(values, width - HALF, 1)
    down = pltpu.roll(values, HALF, 1)
    return jnp.where(lane % HEAD_DIM < HALF, up, down)


def wide(table, width):
    return jnp.concatenate([table] * (width // LANES), axis=1)


def rotate(values, cosine, signed):
    width = values.shape[1]
    return values * wide(cosine, width) + swap_halves(values) * wide(signed, width)


def rotate_back(values, cosine, signed):
    width = values.shape[1]
    return values * wide(cosine, width) + swap_halves(values * wide(signed, width))


def gain_rows(small):
    pick = lax.broadcasted_iota(jnp.int32, (16, LANES), 1) == (
        lax.broadcasted_iota(jnp.int32, (16, LANES), 0) + E
    )
    return mm_nt(pick.astype(BF16), small)


def norm_of(values):
    inverse = lax.rsqrt(jnp.mean(values * values, axis=-1, keepdims=True) + NORM_EPSILON)
    return values * inverse, inverse


def head(ref, index):
    return ref[:, index * HEAD_DIM : (index + 1) * HEAD_DIM]


def probabilities(query, key):
    scores = mm_nt(query, key) * SCALE
    rows = lax.broadcasted_iota(jnp.int32, scores.shape, 0)
    cols = lax.broadcasted_iota(jnp.int32, scores.shape, 1)
    scores = jnp.where(rows >= cols, scores, -jnp.inf)
    exponent = jnp.exp(scores - jnp.max(scores, axis=-1, keepdims=True))
    return exponent / jnp.sum(exponent, axis=-1, keepdims=True)


def attention_forward_kernel(
    x_ref, w_ref, small_ref, cos_ref, sin_ref, q_ref, k_ref, v_ref, ob_ref, x1_ref, h2_ref, h1
):
    step = pl.program_id(0)

    @pl.when(step == 0)
    def _():
        gain = gain_rows(small_ref[...])[0:1, :]
        normed, _ = norm_of(x_ref[...].astype(F32))
        h1[...] = (normed * gain).astype(BF16)

    @pl.when(step < 3)
    def _():
        columns = pl.ds(pl.multiple_of(step * BLOCK, BLOCK), BLOCK)
        q_ref[:, columns] = rotate(mm(h1[...], w_ref[...]), cos_ref[...], sin_ref[...]).astype(BF16)

    @pl.when(step == 3)
    def _():
        k_ref[...] = rotate(mm(h1[...], w_ref[...]), cos_ref[...], sin_ref[...]).astype(BF16)

    @pl.when(step == 4)
    def _():
        v_ref[...] = mm(h1[...], w_ref[...]).astype(BF16)
        for group in range(KEY_VALUE_HEADS):
            key, value = head(k_ref, group), head(v_ref, group)
            for index in range(group * GROUP, (group + 1) * GROUP):
                probability = probabilities(head(q_ref, index), key).astype(BF16)
                ob_ref[:, index * HEAD_DIM : (index + 1) * HEAD_DIM] = mm(
                    probability, value
                ).astype(BF16)

    @pl.when(step > 4)
    def _():
        columns = pl.ds(pl.multiple_of((step - 5) * BLOCK, BLOCK), BLOCK)
        x1_ref[:, columns] = x_ref[:, columns].astype(F32) + mm(ob_ref[...], w_ref[...])

    @pl.when(step == 7)
    def _():
        gain = gain_rows(small_ref[...])[1:2, :]
        normed, _ = norm_of(x1_ref[...])
        h2_ref[...] = (normed * gain).astype(BF16)


def whole(shape):
    return pl.BlockSpec(shape, lambda *_: (0,) * len(shape))


def params(**more):
    return pltpu.CompilerParams(vmem_limit_bytes=VMEM_LIMIT, **more)


def cost(flops, moved):
    return pl.CostEstimate(flops=flops, bytes_accessed=moved, transcendentals=0)


def attention_forward(x, pack, cosine, signed):
    shape = jax.ShapeDtypeStruct
    return pl.pallas_call(
        attention_forward_kernel,
        grid=(8,),
        in_specs=[
            whole((T, D)),
            pl.BlockSpec((D, BLOCK), lambda i: (0, i)),
            pl.BlockSpec((D, LANES), lambda i: (0, 4096 // LANES)),
            whole((T, LANES)),
            whole((T, LANES)),
        ],
        out_specs=[
            whole((T, D)),
            whole((T, BLOCK)),
            whole((T, BLOCK)),
            whole((T, D)),
            whole((T, D)),
            whole((T, D)),
        ],
        out_shape=[
            shape((T, D), BF16),
            shape((T, BLOCK), BF16),
            shape((T, BLOCK), BF16),
            shape((T, D), BF16),
            shape((T, D), F32),
            shape((T, D), BF16),
        ],
        scratch_shapes=[pltpu.VMEM((T, D), BF16)],
        compiler_params=params(),
        cost_estimate=cost(2 * T * D * 4096, 14 << 20),
        name="attention_forward",
    )(x, pack, pack, cosine, signed)


def gate_kernel(small_ref, member_ref, chosen_ref, place_ref, *refs):
    rows, (gates_ref, slot_gate_ref, b_ref) = refs[:PEERS], refs[PEERS:]
    small = small_ref[...]
    for hop in range(PEERS):
        h2 = rows[hop][...]
        member = member_ref[hop] > 0.5
        logits = jnp.where(member, mm(h2, small), -jnp.inf)
        exponent = jnp.exp(logits - jnp.max(logits, axis=-1, keepdims=True))
        gates = exponent / jnp.sum(exponent, axis=-1, keepdims=True)
        gates_ref[hop] = gates
        high = gates.astype(BF16)
        low = (gates - high.astype(F32)).astype(BF16)
        place = place_ref[hop]
        spread = mm(place, high) + mm(place, low)
        picked = jnp.sum(spread * chosen_ref[...], axis=-1, keepdims=True)
        slot_gate_ref[:, hop] = picked.reshape(LOCAL, CAP, 1)
        b_ref[:, hop] = mm(place, h2).astype(BF16).reshape(LOCAL, CAP, D)


def gate_rows(small_pack, member, chosen, place, rows):
    shape = jax.ShapeDtypeStruct
    return pl.pallas_call(
        gate_kernel,
        grid=(1,),
        in_specs=[
            pl.BlockSpec((D, LANES), lambda i: (0, 4096 // LANES)),
            whole((PEERS, T, LANES)),
            whole((SLOTS, LANES)),
            whole((PEERS, SLOTS, T)),
        ]
        + [whole((T, D))] * PEERS,
        out_specs=[
            whole((PEERS, T, LANES)),
            whole((LOCAL, PEERS, CAP, 1)),
            whole((LOCAL, PEERS, CAP, D)),
        ],
        out_shape=[
            shape((PEERS, T, LANES), F32),
            shape((LOCAL, PEERS, CAP, 1), F32),
            shape((LOCAL, PEERS, CAP, D), BF16),
        ],
        compiler_params=params(),
        cost_estimate=cost(2 * PEERS * SLOTS * T * D, 8 << 20),
        name="gate_rows",
    )(small_pack, member, chosen, place, *rows)


def spread_kernel(place_ref, *refs):
    rows, out_ref = refs[:PEERS], refs[PEERS]
    for hop in range(PEERS):
        out_ref[:, hop] = (
            mm(place_ref[hop], rows[hop][:, :D]).astype(BF16).reshape(LOCAL, CAP, D)
        )


def spread_rows(place, rows):
    return pl.pallas_call(
        spread_kernel,
        grid=(1,),
        in_specs=[whole((PEERS, SLOTS, T))] + [whole(rows[0].shape)] * PEERS,
        out_specs=whole((LOCAL, PEERS, CAP, D)),
        out_shape=jax.ShapeDtypeStruct((LOCAL, PEERS, CAP, D), BF16),
        compiler_params=params(),
        cost_estimate=cost(2 * PEERS * SLOTS * T * D, 8 << 20),
        name="spread_rows",
    )(place, *rows)


def expert_kernel(b_ref, dyr_ref, gate_ref, w_ref, grad_ref, gy_ref, db_ref):
    rows = b_ref[0]
    gate = gate_ref[0]
    down = w_ref[0, :, 2 * H : 3 * H]
    pre = mm(rows, w_ref[0, :, 0 : 2 * H])
    gate_pre, up_pre = pre[:, :H], pre[:, H:]
    sigmoid = 1.0 / (1.0 + jnp.exp(-gate_pre))
    silu = gate_pre * sigmoid
    activated = (silu * up_pre).astype(BF16)
    result = mm_nt(activated, down).astype(BF16).astype(F32)
    raw = dyr_ref[0].astype(F32)
    gy_ref[0] = (gate * result).astype(BF16)
    inner = jnp.sum(raw * result, axis=-1, keepdims=True)
    grad_rows = (gate * raw).astype(BF16)
    grad_act = mm(grad_rows, down)
    grad_ref[0, :, 2 * H : 3 * H] = mm_tn(grad_rows, activated).astype(BF16)
    grad_gate = (grad_act * up_pre * sigmoid * (1.0 + gate_pre * (1.0 - sigmoid))).astype(BF16)
    grad_up = (grad_act * silu).astype(BF16)
    both = jnp.concatenate([grad_gate, grad_up], axis=1)
    db_ref[0, :, 0:D] = mm_nt(both, w_ref[0, :, 0 : 2 * H]).astype(BF16)
    grad_ref[0, :, 0 : 2 * H] = mm_tn(rows, both).astype(BF16)
    expert = pl.program_id(0)
    lane = lax.broadcasted_iota(jnp.int32, (PEERS * CAP, LANES), 1)
    high = inner.astype(BF16).astype(F32)
    low = inner - high
    tail = jnp.where(lane == expert, high, jnp.where(lane == expert + LOCAL, low, 0.0))
    db_ref[0, :, D : D + LANES] = tail.astype(BF16)


def experts(b, dyr, slot_gate, pack):
    shape = jax.ShapeDtypeStruct
    rows = PEERS * CAP
    return pl.pallas_call(
        expert_kernel,
        grid=(LOCAL,),
        in_specs=[
            pl.BlockSpec((1, rows, D), lambda e: (e, 0, 0)),
            pl.BlockSpec((1, rows, D), lambda e: (e, 0, 0)),
            pl.BlockSpec((1, rows, 1), lambda e: (e, 0, 0)),
            pl.BlockSpec((1, D, 3 * H), lambda e: (e, 0, 0)),
        ],
        out_specs=[
            pl.BlockSpec((1, D, 3 * H), lambda e: (e, 0, 0)),
            pl.BlockSpec((1, rows, D), lambda e: (e, 0, 0)),
            pl.BlockSpec((1, rows, D + LANES), lambda e: (e, 0, 0)),
        ],
        out_shape=[
            shape((LOCAL, D, 3 * H), BF16),
            shape((LOCAL, rows, D), BF16),
            shape((LOCAL, rows, D + LANES), BF16),
        ],
        compiler_params=params(),
        cost_estimate=cost(18 * LOCAL * rows * D * H, 60 << 20),
        name="experts",
    )(b, dyr, slot_gate, pack)


def collect_kernel(place_ref, value_ref, *out_refs):
    for hop in range(PEERS):
        rows = value_ref[:, hop].reshape(SLOTS, value_ref.shape[-1])
        out_refs[hop][...] = mm_tn(place_ref[hop], rows).astype(BF16)


def collect(place, values, name):
    width = values.shape[-1]
    return pl.pallas_call(
        collect_kernel,
        grid=(1,),
        in_specs=[whole((PEERS, SLOTS, T)), whole((LOCAL, PEERS, CAP, width))],
        out_specs=[whole((T, width))] * PEERS,
        out_shape=[jax.ShapeDtypeStruct((T, width), BF16)] * PEERS,
        compiler_params=params(),
        cost_estimate=cost(2 * PEERS * SLOTS * T * width, 8 << 20),
        name=name,
    )(place, values.reshape(LOCAL, PEERS, CAP, width))


def mixed_kernel(x1_ref, *refs):
    total = x1_ref[...]
    for ref in refs[:PEERS]:
        total = total + ref[...].astype(F32)
    refs[PEERS][...] = total.astype(BF16)


def mix(x1, parts):
    return pl.pallas_call(
        mixed_kernel,
        grid=(1,),
        in_specs=[whole((T, D))] * (1 + PEERS),
        out_specs=whole((T, D)),
        out_shape=jax.ShapeDtypeStruct((T, D), BF16),
        compiler_params=params(),
        cost_estimate=cost(T * D * 8, 5 << 20),
        name="mix",
    )(x1, *parts)


def norm_back(grad, normed, inverse, gain):
    scaled = grad * gain
    return inverse * (scaled - normed * jnp.mean(scaled * normed, axis=-1, keepdims=True))


def attention_backward_kernel(
    x_ref,
    x1_ref,
    h2_ref,
    dy_ref,
    gates_ref,
    place_ref,
    q_ref,
    k_ref,
    v_ref,
    ob_ref,
    w_ref,
    small_ref,
    cos_ref,
    sin_ref,
    *refs,
):
    parts = refs[:PEERS]
    grad_tokens_ref, pack_ref = refs[PEERS : PEERS + 2]
    h1, da, dx1, dob, dqf, dkf, dvf, dqkv, dh1, dh2, dlogits, stage, small_stage, sems = refs[
        PEERS + 2 :
    ]
    step = pl.program_id(0)
    slot = lax.rem(step, 2)

    def block_copy(at, which):
        column = lax.rem(at + 5, 8) * BLOCK
        return pltpu.make_async_copy(
            stage.at[which],
            pack_ref.at[:, pl.ds(pl.multiple_of(column, BLOCK), BLOCK)],
            sems.at[which],
        )

    @pl.when(step == 0)
    def _():
        grad = jnp.zeros((T, D), F32)
        inner = jnp.zeros((T, LANES), F32)
        for hop in range(PEERS):
            grad = grad + parts[hop][:, :D].astype(F32)
            inner = inner + mm(parts[hop][:, D:], place_ref[hop])
        gates = gates_ref[...]
        score = gates * (inner - jnp.sum(gates * inner, axis=-1, keepdims=True))
        dlogits[...] = score.astype(BF16)
        grad = grad + mm_nt(dlogits[...], small_ref[...])
        dh2[...] = grad
        gains = gain_rows(small_ref[...])
        normed_two, inverse_two = norm_of(x1_ref[...])
        through = dy_ref[...].astype(F32) + norm_back(grad, normed_two, inverse_two, gains[1:2, :])
        dx1[...] = through
        da[...] = through.astype(BF16)
        normed_one, _ = norm_of(x_ref[...].astype(F32))
        h1[...] = (normed_one * gains[0:1, :]).astype(BF16)
        dob[...] = jnp.zeros((T, D), F32)
        dh1[...] = jnp.zeros((T, D), F32)

    @pl.when(step >= 2)
    def _():
        block_copy(step - 2, slot).wait()

    @pl.when(step < 3)
    def _():
        columns = pl.ds(pl.multiple_of(step * BLOCK, BLOCK), BLOCK)
        piece = da[:, columns]
        dob[...] += mm_nt(piece, w_ref[...])
        stage[slot] = mm_tn(ob_ref[...], piece).astype(BF16)

    @pl.when(step == 3)
    def _():
        for group in range(KEY_VALUE_HEADS):
            key, value = head(k_ref, group), head(v_ref, group)
            grad_key = jnp.zeros((T, HEAD_DIM), F32)
            grad_value = jnp.zeros((T, HEAD_DIM), F32)
            for index in range(group * GROUP, (group + 1) * GROUP):
                query = head(q_ref, index)
                out_grad = head(dob, index).astype(BF16)
                probability = probabilities(query, key)
                grad_prob = mm_nt(out_grad, value)
                grad_value = grad_value + mm_tn(probability.astype(BF16), out_grad)
                held = jnp.sum(probability * grad_prob, axis=-1, keepdims=True)
                grad_scores = (probability * (grad_prob - held)).astype(BF16)
                dqf[:, index * HEAD_DIM : (index + 1) * HEAD_DIM] = mm(grad_scores, key) * SCALE
                grad_key = grad_key + mm_tn(grad_scores, query)
            dkf[:, group * HEAD_DIM : (group + 1) * HEAD_DIM] = grad_key * SCALE
            dvf[:, group * HEAD_DIM : (group + 1) * HEAD_DIM] = grad_value
        cosine, signed = cos_ref[...], sin_ref[...]
        dqkv[:, 0:D] = rotate_back(dqf[...], cosine, signed).astype(BF16)
        dqkv[:, D : D + BLOCK] = rotate_back(dkf[...], cosine, signed).astype(BF16)
        dqkv[:, D + BLOCK : D + 2 * BLOCK] = dvf[...].astype(BF16)

    @pl.when(step >= 3)
    def _():
        columns = pl.ds(pl.multiple_of((step - 3) * BLOCK, BLOCK), BLOCK)
        piece = dqkv[:, columns]
        dh1[...] += mm_nt(piece, w_ref[...])
        stage[slot] = mm_tn(h1[...], piece).astype(BF16)

    block_copy(step, slot).start()

    @pl.when(step == 7)
    def _():
        gains = gain_rows(small_ref[...])
        normed_one, inverse_one = norm_of(x_ref[...].astype(F32))
        grad = dh1[...]
        grad_tokens_ref[...] = dx1[...] + norm_back(grad, normed_one, inverse_one, gains[0:1, :])
        normed_two, _ = norm_of(x1_ref[...])
        lane = lax.broadcasted_iota(jnp.int32, (T, LANES), 1)
        total = mm_tn(h2_ref[...], dlogits[...])
        total += mm_tn((grad * normed_one).astype(BF16), (lane == E).astype(BF16))
        total += mm_tn((dh2[...] * normed_two).astype(BF16), (lane == E + 1).astype(BF16))
        small_stage[...] = total.astype(BF16)
        last = pltpu.make_async_copy(small_stage, pack_ref.at[:, pl.ds(4096, LANES)], sems.at[2])
        last.start()
        block_copy(step - 1, 1 - slot).wait()
        block_copy(step, slot).wait()
        last.wait()


def attention_backward(x, x1, h2, dy, gates, place, q, k, v, ob, pack, cosine, signed, parts):
    shape = jax.ShapeDtypeStruct
    return pl.pallas_call(
        attention_backward_kernel,
        grid=(8,),
        in_specs=[
            whole((T, D)),
            whole((T, D)),
            whole((T, D)),
            whole((T, D)),
            whole((T, LANES)),
            whole((PEERS, LANES, LANES)),
            whole((T, D)),
            whole((T, BLOCK)),
            whole((T, BLOCK)),
            whole((T, D)),
            pl.BlockSpec((D, BLOCK), lambda i: (0, lax.rem(i + 5, 8))),
            pl.BlockSpec((D, LANES), lambda i: (0, 4096 // LANES)),
            whole((T, LANES)),
            whole((T, LANES)),
        ]
        + [whole((T, D + LANES))] * PEERS,
        out_specs=[whole((T, D)), pl.BlockSpec(memory_space=pl.ANY)],
        out_shape=[shape((T, D), F32), shape((D, PACK), BF16)],
        scratch_shapes=[
            pltpu.VMEM((T, D), BF16),
            pltpu.VMEM((T, D), BF16),
            pltpu.VMEM((T, D), F32),
            pltpu.VMEM((T, D), F32),
            pltpu.VMEM((T, D), F32),
            pltpu.VMEM((T, BLOCK), F32),
            pltpu.VMEM((T, BLOCK), F32),
            pltpu.VMEM((T, D + 2 * BLOCK), BF16),
            pltpu.VMEM((T, D), F32),
            pltpu.VMEM((T, D), F32),
            pltpu.VMEM((T, LANES), BF16),
            pltpu.VMEM((2, D, BLOCK), BF16),
            pltpu.VMEM((D, LANES), BF16),
            pltpu.SemaphoreType.DMA((3,)),
        ],
        compiler_params=params(),
        cost_estimate=cost(4 * T * D * 4096, 30 << 20),
        name="attention_backward",
    )(x, x1, h2, dy, gates, place, q, k, v, ob, pack, pack, cosine, signed, *parts)


def spread_tables(all_routes, me):
    lane = jnp.arange(LANES, dtype=jnp.int32)
    member = jnp.sum((all_routes[..., None] == lane).astype(F32), axis=2)
    mine = me * LOCAL + jnp.arange(LOCAL, dtype=jnp.int32)
    own = jnp.sum((all_routes[..., None] == mine).astype(F32), axis=2)
    earlier = (np.arange(T)[:, None] > np.arange(T)[None, :]).astype(np.float32)
    before = jnp.einsum(
        "ts,rse->rte", jnp.asarray(earlier, BF16), own.astype(BF16), preferred_element_type=F32
    )
    slots = jnp.where(own > 0.5, before.astype(jnp.int32), -1)
    slots = jnp.swapaxes(slots, 1, 2)[:, :, None, :]
    place = slots == jnp.arange(CAP, dtype=jnp.int32)[None, None, :, None]
    return member, place.astype(BF16).reshape(PEERS, SLOTS, T)


def total_over_peers(share, me):
    wide_share = jnp.pad(share, ((0, 0), (0, PEERS * 640 - share.shape[1])))
    total = jnp.zeros((share.shape[0], 640), F32)
    for hop in range(PEERS):
        piece = lax.dynamic_slice_in_dim(wide_share, peer(me, hop) * 640, 640, 1)
        total = total + send(piece, hop).astype(F32)
    low = total.astype(BF16)
    result = jnp.zeros(wide_share.shape, BF16)
    for hop in range(PEERS):
        result = lax.dynamic_update_slice_in_dim(
            result, send(low, hop), peer(me, hop, True) * 640, 1
        )
    return result[:, : share.shape[1]]


def body(
    tokens,
    cotangent,
    routes,
    norm_one,
    w_query,
    key_weight,
    value_weight,
    w_out,
    norm_two,
    w_router,
    w_gate,
    w_up,
    w_down,
):
    me = lax.axis_index("expert")
    cosine, signed = (jnp.asarray(table) for table in rope_tables())
    rows = norm_one.shape[0]
    small = jnp.concatenate(
        [
            w_router,
            norm_one[:, None],
            norm_two[:, None],
            jnp.zeros((rows, LANES - E - 2), BF16),
        ],
        axis=1,
    )
    pack = lax.all_gather(
        jnp.concatenate([w_query, key_weight, value_weight, w_out, small], axis=1),
        "fsdp",
        axis=0,
        tiled=True,
    )
    expert_pack = lax.all_gather(
        jnp.concatenate([w_gate, w_up, jnp.swapaxes(w_down, 1, 2)], axis=2),
        "fsdp",
        axis=1,
        tiled=True,
    )

    early = jnp.concatenate(
        [cotangent, jnp.pad(routes, ((0, 0), (0, LANES - routes.shape[1]))).astype(BF16)], axis=1
    )
    early_rows = [send(early, hop) for hop in range(PEERS)]
    all_routes = jnp.stack(
        [r[:, D : D + routes.shape[1]].astype(jnp.int32) for r in early_rows]
    )
    member, place = spread_tables(all_routes, me)
    row_expert = me * LOCAL + jnp.arange(SLOTS, dtype=jnp.int32) // CAP
    chosen = (row_expert[:, None] == jnp.arange(LANES, dtype=jnp.int32)[None, :]).astype(F32)
    dyr = spread_rows(place, early_rows).reshape(LOCAL, PEERS * CAP, D)

    lane = jnp.arange(LANES, dtype=jnp.int32)
    homes = jnp.stack([peer(me, hop) for hop in range(PEERS)])[:, None] * LOCAL + (lane % LOCAL)
    homes = jnp.where(lane < 2 * LOCAL, homes, -1)
    back_place = (homes[:, :, None] == lane[None, None, :]).astype(BF16)

    q, k, v, ob, x1, h2 = attention_forward(tokens, pack, cosine, signed)
    h2_rows = [send(h2, hop) for hop in range(PEERS)]
    gates, slot_gate, b = gate_rows(pack, member, chosen, place, h2_rows)
    grad_pack, gy, db = experts(
        b.reshape(LOCAL, PEERS * CAP, D),
        dyr,
        slot_gate.reshape(LOCAL, PEERS * CAP, 1),
        expert_pack,
    )
    db_parts = collect(place, db, "collect_grads")
    parts = [send(db_parts[hop], hop, True) for hop in range(PEERS)]
    gy_parts = collect(place, gy, "collect_results")
    mixed_parts = [send(gy_parts[hop], hop, True) for hop in range(PEERS)]
    mixed_out = mix(x1, mixed_parts)

    expert_share = lax.psum_scatter(grad_pack, "fsdp", scatter_dimension=1, tiled=True)
    grad_tokens, attn_pack = attention_backward(
        tokens, x1, h2, cotangent, gates[0], back_place, q, k, v, ob, pack, cosine, signed, parts
    )
    share = lax.psum_scatter(attn_pack, "fsdp", scatter_dimension=0, tiled=True)
    total = total_over_peers(share, me).astype(F32)

    expert_share = expert_share.astype(F32)
    return (
        mixed_out,
        grad_tokens,
        total[:, 4096 + E],
        total[:, 0:D],
        total[:, D : D + BLOCK],
        total[:, D + BLOCK : D + 2 * BLOCK],
        total[:, D + 2 * BLOCK : 4096],
        total[:, 4096 + E + 1],
        total[:, 4096 : 4096 + E],
        expert_share[:, :, 0:H],
        expert_share[:, :, H : 2 * H],
        jnp.swapaxes(expert_share[:, :, 2 * H :], 1, 2),
    )


def solution(mesh):
    return jax.shard_map(
        body,
        mesh=mesh,
        in_specs=(
            P(("expert", "fsdp"), None),
            P(("expert", "fsdp"), None),
            P(("expert", "fsdp"), None),
            P("fsdp"),
            P("fsdp", None),
            P("fsdp", None),
            P("fsdp", None),
            P("fsdp", None),
            P("fsdp"),
            P("fsdp", None),
            P("expert", "fsdp", None),
            P("expert", "fsdp", None),
            P("expert", None, "fsdp"),
        ),
        out_specs=(
            P(("expert", "fsdp"), None),
            P(("expert", "fsdp"), None),
            P("fsdp"),
            P("fsdp", None),
            P("fsdp", None),
            P("fsdp", None),
            P("fsdp", None),
            P("fsdp"),
            P("fsdp", None),
            P("expert", "fsdp", None),
            P("expert", "fsdp", None),
            P("expert", None, "fsdp"),
        ),
        check_vma=False,
    )
```

time: 1260 us -> 685 us (0.54)
  waiting for transfers between devices: 848 us -> 425 us
  blocking collectives: 117 us -> 0 us
  matrix products: 101 us -> 0.13 us
  Pallas kernels: 0 us -> 100 us
  starting transfers between devices: 37.1 us -> 101 us
  local copies, waits for them, and re-layouts: 84.2 us -> 25.8 us
  other arithmetic: 42.2 us -> 9.52 us
    reduce_scatter x7 -> x2, waiting for transfers between devices: 460 us -> 158 us  [the longest x1 81.5 us: body(): lax.psum_scatter(grad_pack, 'fsdp', scatter_dimension=1, tiled=True)]
    all_to_all x4 -> x0, waiting for transfers between devices: 255 us -> none  [the longest x1 71.9 us: body(): lax.all_to_all(send_rows, 'expert', split_axis=0, concat_axis=1, tiled=True)]
    ppermute x0 -> x42, waiting for transfers between devices: none -> 185 us  [send(): lax.ppermute(value, 'expert', [(i, peer(i, hop, back)) for i in range(PEE...]
    ppermute x0 -> x42, starting transfers between devices: none -> 101 us  [send(): lax.ppermute(value, 'expert', [(i, peer(i, hop, back)) for i in range(PEE...]
    dot_general x30 -> x1, matrix products: 101 us -> 0.13 us  [spread_tables(): jnp.einsum('ts,rse->rte', jnp.asarray(earlier, BF16), own.astype(BF16), p...]
    pallas_call x0 -> x8, Pallas kernels: none -> 100 us  [the longest x1 28.3 us: attention_backward(): pl.pallas_call(attention_backward_kernel, grid=(8,), in_specs=[whole((T,...]
    unnamed x2 -> x0, blocking collectives: 59.2 us -> none
    psum x1 -> x0, waiting for transfers between devices: 44.3 us -> none  [body(): lax.psum(shares[1].astype(jnp.bfloat16), 'expert').astype(jnp.float32)]
  transfers between devices with their start and end apart: 20 -> 46, of which waited for: 16 -> 21; matrix products, arithmetic and copies ran while one was open for 13% -> 3% of each run, Pallas kernels for 0% -> 6%
where the time goes in v1:
time: 685 us; the launch traced here: 677 us
  waiting for transfers between devices  425 us (62%)
  starting transfers between devices  101 us (15%)
  Pallas kernels  100 us (15%)
  local copies, waits for them, and re-layouts  25.8 us (4%)
  between operations  14.8 us (2%)
  other arithmetic  9.52 us (1%)
    ppermute x42, waiting for transfers between devices, send(): lax.ppermute(value, 'expert', [(i, peer(i, hop, back)) for i in range(PEE...  185 us
    ppermute x42, starting transfers between devices, send(): lax.ppermute(value, 'expert', [(i, peer(i, hop, back)) for i in range(PEE...  101 us
    reduce_scatter x1, waiting for transfers between devices, body(): lax.psum_scatter(grad_pack, 'fsdp', scatter_dimension=1, tiled=True)  81.5 us
    reduce_scatter x1, waiting for transfers between devices, body(): share = lax.psum_scatter(attn_pack, 'fsdp', scatter_dimension=0, tiled=True)  76.5 us
    all_gather x1, waiting for transfers between devices, body(): lax.all_gather(jnp.concatenate([w_gate, w_up, jnp.swapaxes(w_down, 1, 2)]...  55.3 us
    pallas_call x1, Pallas kernels, attention_backward(): pl.pallas_call(attention_backward_kernel, grid=(8,), in_specs=[whole((T,...  28.3 us
    pallas_call x1, Pallas kernels, experts(): pl.pallas_call(expert_kernel, grid=(LOCAL,), in_specs=[pl.BlockSpec((1, r...  27.6 us
    all_gather x1, waiting for transfers between devices, body(): lax.all_gather(jnp.concatenate([w_query, key_weight, value_weight, w_out,...  26.1 us
  transfers between devices with their start and end apart: 46, of which 21 were waited for; matrix products, arithmetic and copies ran while one was open for 3% of the time, Pallas kernels for 6%

profile of v1, /device:TPU:0, one launch (start us, length us, event | category | flops | bytes accessed | tf_op | source)
XLA Modules:
  0.0 676.7 jit_solution(16614004459898159571)
XLA Ops:
  16.3 3.6 collective-permute-start.1
  20.9 3.0 collective-permute-start.3
  25.9 2.3 collective-permute-done.refs_1_
  28.2 13.2 %collective-permute-start.5 = (bf16[128,1664]{1,0:T(8,128)(2,1)S(1)}, bf16[128,1664]{1,0:T(8,128)(2,1)S(1)}, u32[]{:S(2)}, u32[]{:S(2)}) collective-permute-start(bf16[128,1664]{1,0:T(8,128)(2,1)S(1)} %fusion.4.refs_0_), channel_id=1, source_target_pairs={{0,96},{16,112},{32,64},{48,80},{64,32},{80,48},{96,0},{112,16},{1... | collective-permute-start | bytes 1277960 | tf_op jit(solution)/shard_map/ppermute | solution.py:46
  43.4 17.9 %collective-permute-done.4.refs_5_ = bf16[128,1664]{1,0:T(8,128)(2,1)S(1)} collective-permute-done((bf16[128,1664]{1,0:T(8,128)(2,1)S(1)}, bf16[128,1664]{1,0:T(8,128)(2,1)S(1)}, u32[]{:S(2)}, u32[]{:S(2)}) %collective-permute-start.4) | collective-permute-done | bytes 426016 | tf_op jit(solution)/shard_map/ppermute | solution.py:46
  61.4 18.1 %collective-permute-done.5.refs_6_ = bf16[128,1664]{1,0:T(8,128)(2,1)S(1)} collective-permute-done((bf16[128,1664]{1,0:T(8,128)(2,1)S(1)}, bf16[128,1664]{1,0:T(8,128)(2,1)S(1)}, u32[]{:S(2)}, u32[]{:S(2)}) %collective-permute-start.5) | collective-permute-done | bytes 426016 | tf_op jit(solution)/shard_map/ppermute | solution.py:46
  79.5 17.4 %collective-permute-done.6.refs_7_ = bf16[128,1664]{1,0:T(8,128)(2,1)S(1)} collective-permute-done((bf16[128,1664]{1,0:T(8,128)(2,1)S(1)}, bf16[128,1664]{1,0:T(8,128)(2,1)S(1)}, u32[]{:S(2)}, u32[]{:S(2)}) %collective-permute-start.6) | collective-permute-done | bytes 426016 | tf_op jit(solution)/shard_map/ppermute | solution.py:46
  97.0 26.1 %all-gather.3.cloned.1.call-done.w_ref.small_ref = bf16[1536,4224]{1,0:T(8,128)(2,1)} async-done(((bf16[96,4224]{1,0:T(8,128)(2,1)}), bf16[1536,4224]{1,0:T(8,128)(2,1)}) %all-gather.3.cloned.1.call-update) | async-done | bytes 12976144 | tf_op jit(solution)/shard_map/all_gather | solution.py:597
  123.1 18.0 %attention_forward.1 = (bf16[128,1536]{1,0:T(8,128)(2,1)}, bf16[128,512]{1,0:T(8,128)(2,1)}, bf16[128,512]{1,0:T(8,128)(2,1)}, bf16[128,1536]{1,0:T(8,128)(2,1)}...) custom-call(bf16[128,1536]{1,0:T(8,128)(2,1)} %x_ref.3, ...), custom_call_target="tpu_custom_call" | custom-call | flops 1610612736 | bytes 14680064 | tf_op jit(solution)/shard_map/attention_forward/pallas_call | solution.py:174
  147.8 2.6 collective-permute-start.13
  150.8 12.5 %collective-permute-done.10.refs_4_ = bf16[128,1536]{1,0:T(8,128)(2,1)S(1)} collective-permute-done((bf16[128,1536]{1,0:T(8,128)(2,1)}, bf16[128,1536]{1,0:T(8,128)(2,1)S(1)}, u32[]{:S(2)}, u32[]{:S(2)}) %collective-permute-start.10) | collective-permute-done | bytes 393248 | tf_op jit(solution)/shard_map/ppermute | solution.py:46
  164.1 15.8 %collective-permute-done.11.refs_5_ = bf16[128,1536]{1,0:T(8,128)(2,1)S(1)} collective-permute-done((bf16[128,1536]{1,0:T(8,128)(2,1)}, bf16[128,1536]{1,0:T(8,128)(2,1)S(1)}, u32[]{:S(2)}, u32[]{:S(2)}) %collective-permute-start.11) | collective-permute-done | bytes 393248 | tf_op jit(solution)/shard_map/ppermute | solution.py:46
  182.4 5.2 spread_rows.1
  187.5 2.4 convert_reduce_fusion.member_ref
  189.9 7.4 %collective-permute-done.12.refs_6_ = bf16[128,1536]{1,0:T(8,128)(2,1)S(1)} collective-permute-done((bf16[128,1536]{1,0:T(8,128)(2,1)}, bf16[128,1536]{1,0:T(8,128)(2,1)S(1)}, u32[]{:S(2)}, u32[]{:S(2)}) %collective-permute-start.12) | collective-permute-done | bytes 393248 | tf_op jit(solution)/shard_map/ppermute | solution.py:46
  197.3 16.8 %collective-permute-done.13.refs_7_ = bf16[128,1536]{1,0:T(8,128)(2,1)S(1)} collective-permute-done((bf16[128,1536]{1,0:T(8,128)(2,1)}, bf16[128,1536]{1,0:T(8,128)(2,1)S(1)}, u32[]{:S(2)}, u32[]{:S(2)}) %collective-permute-start.13) | collective-permute-done | bytes 393248 | tf_op jit(solution)/shard_map/ppermute | solution.py:46
  215.8 9.2 %gate_rows.1 = (f32[8,128,128]{2,1,0:T(8,128)}, f32[5,8,32,1]{3,2,1,0:T(8,128)}, bf16[5,8,32,1536]{3,2,1,0:T(8,128)(2,1)}) custom-call(bf16[1536,4224]{1,0:T(8,128)(2,1)} %all-gather.3.cloned.1.call-done.w_ref.small_ref, f32[8,128,128]{2,1,0:T(8,128)} %convert_reduce_fusion.member_ref, f32[160,128]{1,0:T(8,128)} %fusion.5.chosen_ref, ...), custom_call_target="tpu_custom_call" | custom-call | flops 503316480 | bytes 8388608 | tf_op jit(solution)/shard_map/gate_rows/pallas_call | solution.py:228
  225.0 55.3 %all-gather.5.cloned.1.call-done.w_ref = bf16[5,1536,1536]{2,1,0:T(8,128)(2,1)} async-done(((bf16[5,96,1536]{2,1,0:T(8,128)(2,1)}), bf16[5,1536,1536]{2,1,0:T(8,128)(2,1)}) %all-gather.5.cloned.1.call-update) | async-done | bytes 23592976 | tf_op jit(solution)/shard_map/all_gather | solution.py:603
  280.3 27.6 %experts.1 = (bf16[5,1536,1536]{2,1,0:T(8,128)(2,1)}, bf16[5,256,1536]{2,1,0:T(8,128)(2,1)}, bf16[5,256,1664]{2,1,0:T(8,128)(2,1)}) custom-call(bf16[5,256,1536]{2,1,0:T(8,128)(2,1)} %bitcast.54, bf16[5,256,1536]{2,1,0:T(8,128)(2,1)} %bitcast.50, f32[5,256,1]{2,1,0:T(8,128)} %bitcast.55, bf16[5,1536,1536]{2,1,0:T(8,128)(2,1)} %all-gather.5.cloned.1.call-done.w_ref), custom_call_target="tpu_custom_call" | custom-call | flops 18119393280 | bytes 62914560 | tf_op jit(solution)/shard_map/experts/pallas_call | solution.py:307
  308.0 4.4 collect_grads.1
  312.4 2.8 collective-permute-start.21
  317.0 2.7 collective-permute-start.24
  319.7 2.5 collective-permute-start.25
  322.2 21.1 %collective-permute-done.21.refs_1_ = bf16[128,1664]{1,0:T(8,128)(2,1)S(1)} collective-permute-done((bf16[128,1664]{1,0:T(8,128)(2,1)}, bf16[128,1664]{1,0:T(8,128)(2,1)S(1)}, u32[]{:S(2)}, u32[]{:S(2)}) %collective-permute-start.21) | collective-permute-done | bytes 426016 | tf_op jit(solution)/shard_map/ppermute | solution.py:46
  343.6 6.8 %collective-permute-start.27 = (bf16[128,1664]{1,0:T(8,128)(2,1)}, bf16[128,1664]{1,0:T(8,128)(2,1)S(1)}, u32[]{:S(2)}, u32[]{:S(2)}) collective-permute-start(bf16[128,1664]{1,0:T(8,128)(2,1)} %get-tuple-element.68), channel_id=1, source_target_pairs={{0,80},{16,96},{32,112},{48,64},{64,16},{80,32},{96,48},{112,0},{1... | collective-permute-start | bytes 1277960 | tf_op jit(solution)/shard_map/ppermute | solution.py:46
  352.8 7.7 %collective-permute-done.26.refs_6_ = bf16[128,1664]{1,0:T(8,128)(2,1)S(1)} collective-permute-done((bf16[128,1664]{1,0:T(8,128)(2,1)}, bf16[128,1664]{1,0:T(8,128)(2,1)S(1)}, u32[]{:S(2)}, u32[]{:S(2)}) %collective-permute-start.26) | collective-permute-done | bytes 426016 | tf_op jit(solution)/shard_map/ppermute | solution.py:46
  360.5 7.6 %collective-permute-done.27.refs_7_ = bf16[128,1664]{1,0:T(8,128)(2,1)S(1)} collective-permute-done((bf16[128,1664]{1,0:T(8,128)(2,1)}, bf16[128,1664]{1,0:T(8,128)(2,1)S(1)}, u32[]{:S(2)}, u32[]{:S(2)}) %collective-permute-start.27) | collective-permute-done | bytes 426016 | tf_op jit(solution)/shard_map/ppermute | solution.py:46
  368.9 28.3 %attention_backward.1 = (f32[128,1536]{1,0:T(8,128)}, bf16[1536,4224]{1,0:T(8,128)(2,1)}) custom-call(bf16[128,1536]{1,0:T(8,128)(2,1)} %x_ref.3, f32[128,1536]{1,0:T(8,128)} %get-tuple-element.42.x1_ref, bf16[128,1536]{1,0:T(8,128)(2,1)} %get-tuple-element.43.refs_0_.h2_ref, bf16[128,1536]{1,0:T(8,128)(2,1)} %dy_ref.1, ...), custom_call_target="tpu_custom_call" | custom-call | flops 3221225472 | bytes 31457280 | tf_op jit(solution)/shard_map/attention_backward/pallas_call | solution.py:496
  397.8 4.2 collect_results.1
  402.2 2.6 collective-permute-start.15
  404.8 76.5 %reduce-scatter.3.cloned.1.call-done = bf16[96,4224]{1,0:T(8,128)(2,1)} async-done(((bf16[1536,4224]{1,0:T(8,128)(2,1)}), bf16[96,4224]{1,0:T(8,128)(2,1)}) %reduce-scatter.3.cloned.1.call-update) | async-done | bytes 811024 | tf_op jit(solution)/shard_map/reduce_scatter | solution.py:646
  484.5 2.8 collective-permute-start.29
  488.8 2.6 collective-permute-start.31
  492.6 2.9 collective-permute-start.33
  495.5 2.8 collective-permute-start.34
  498.3 2.4 collective-permute-start.17
  502.2 2.3 collective-permute-start.18
  504.5 5.7 collective-permute-start.19
  514.0 8.1 %collective-permute-done.17.refs_4_ = bf16[128,1536]{1,0:T(8,128)(2,1)S(1)} collective-permute-done((bf16[128,1536]{1,0:T(8,128)(2,1)}, bf16[128,1536]{1,0:T(8,128)(2,1)S(1)}, u32[]{:S(2)}, u32[]{:S(2)}) %collective-permute-start.17) | collective-permute-done | bytes 393248 | tf_op jit(solution)/shard_map/ppermute | solution.py:46
  522.1 11.7 %collective-permute-done.18.refs_5_ = bf16[128,1536]{1,0:T(8,128)(2,1)S(1)} collective-permute-done((bf16[128,1536]{1,0:T(8,128)(2,1)}, bf16[128,1536]{1,0:T(8,128)(2,1)S(1)}, u32[]{:S(2)}, u32[]{:S(2)}) %collective-permute-start.18) | collective-permute-done | bytes 393248 | tf_op jit(solution)/shard_map/ppermute | solution.py:46
  533.8 3.6 collective-permute-start.37
  537.4 8.6 %collective-permute-done.19.refs_6_ = bf16[128,1536]{1,0:T(8,128)(2,1)} collective-permute-done((bf16[128,1536]{1,0:T(8,128)(2,1)}, bf16[128,1536]{1,0:T(8,128)(2,1)}, u32[]{:S(2)}, u32[]{:S(2)}) %collective-permute-start.19) | collective-permute-done | bytes 393248 | tf_op jit(solution)/shard_map/ppermute | solution.py:46
  546.0 3.5 collective-permute-start.38
  549.5 9.9 %collective-permute-done.20.refs_7_ = bf16[128,1536]{1,0:T(8,128)(2,1)} collective-permute-done((bf16[128,1536]{1,0:T(8,128)(2,1)}, bf16[128,1536]{1,0:T(8,128)(2,1)}, u32[]{:S(2)}, u32[]{:S(2)}) %collective-permute-start.20) | collective-permute-done | bytes 393248 | tf_op jit(solution)/shard_map/ppermute | solution.py:46
  559.4 3.2 collective-permute-start.39
  564.6 5.0 collective-permute-start.41
  569.6 3.2 mix.1
  584.6 81.5 %reduce-scatter.5.cloned.1.call-done = bf16[5,96,1536]{2,1,0:T(8,128)(2,1)} async-done(((bf16[5,1536,1536]{2,1,0:T(8,128)(2,1)}), bf16[5,96,1536]{2,1,0:T(8,128)(2,1)}) %reduce-scatter.5.cloned.1.call-update) | async-done | bytes 1474576 | tf_op jit(solution)/shard_map/reduce_scatter | solution.py:642
  (212 shorter events, 60.3 us)
Async XLA Ops:
  7.2 115.9 %all-gather.3.cloned.1.call-start = ((), (), s32[]{:S(2)}) async-start(), calls=%async_computation.2 | async-start | bytes 13787136 | tf_op jit(solution)/shard_map/all_gather | solution.py:597
  11.8 268.5 %all-gather.5.cloned.1.call-start = ((), (), s32[]{:S(2)}) async-start(), calls=%async_computation.3 | async-start | bytes 25067520 | tf_op jit(solution)/shard_map/all_gather | solution.py:603
  13.2 468.0 %reduce-scatter.3.cloned.1.call-start = ((), (), s32[]{:S(2)}) async-start(), calls=%async_computation.4 | async-start | bytes 13787136 | tf_op jit(solution)/shard_map/reduce_scatter | solution.py:646
  14.2 126.8 %copy-start.2 = (bf16[128,1664]{1,0:T(8,128)(2,1)}, bf16[128,1664]{1,0:T(8,128)(2,1)S(1)}, u32[]{:S(2)}) copy-start(bf16[128,1664]{1,0:T(8,128)(2,1)S(1)} %fusion.4.refs_0_) | copy-start | bytes 1277956
  14.2 14.0 %collective-permute-start = (bf16[128,1664]{1,0:T(8,128)(2,1)S(1)}, bf16[128,1664]{1,0:T(8,128)(2,1)S(1)}, u32[]{:S(2)}, u32[]{:S(2)}) collective-permute-start(bf16[128,1664]{1,0:T(8,128)(2,1)S(1)} %fusion.4.refs_0_), channel_id=1, source_target_pairs={{0,16},{16,32},{32,48},{48,0},{64,80},{80,96},{96,112},{112,64},{1... | collective-permute-start | bytes 1277960 | tf_op jit(solution)/shard_map/ppermute | solution.py:46
  16.3 25.2 %collective-permute-start.1 = (bf16[128,1664]{1,0:T(8,128)(2,1)S(1)}, bf16[128,1664]{1,0:T(8,128)(2,1)S(1)}, u32[]{:S(2)}, u32[]{:S(2)}) collective-permute-start(bf16[128,1664]{1,0:T(8,128)(2,1)S(1)} %fusion.4.refs_0_), channel_id=1, source_target_pairs={{0,32},{16,48},{32,0},{48,16},{64,96},{80,112},{96,64},{112,80},{1... | collective-permute-start | bytes 1277960 | tf_op jit(solution)/shard_map/ppermute | solution.py:46
  19.9 22.4 %collective-permute-start.2 = (bf16[128,1664]{1,0:T(8,128)(2,1)S(1)}, bf16[128,1664]{1,0:T(8,128)(2,1)S(1)}, u32[]{:S(2)}, u32[]{:S(2)}) collective-permute-start(bf16[128,1664]{1,0:T(8,128)(2,1)S(1)} %fusion.4.refs_0_), channel_id=1, source_target_pairs={{0,48},{16,0},{32,16},{48,32},{64,112},{80,64},{96,80},{112,96},{1... | collective-permute-start | bytes 1277960 | tf_op jit(solution)/shard_map/ppermute | solution.py:46
  20.9 22.4 %collective-permute-start.3 = (bf16[128,1664]{1,0:T(8,128)(2,1)S(1)}, bf16[128,1664]{1,0:T(8,128)(2,1)S(1)}, u32[]{:S(2)}, u32[]{:S(2)}) collective-permute-start(bf16[128,1664]{1,0:T(8,128)(2,1)S(1)} %fusion.4.refs_0_), channel_id=1, source_target_pairs={{0,64},{16,80},{32,96},{48,112},{64,0},{80,16},{96,32},{112,48},{1... | collective-permute-start | bytes 1277960 | tf_op jit(solution)/shard_map/ppermute | solution.py:46
  23.9 37.4 %collective-permute-start.4 = (bf16[128,1664]{1,0:T(8,128)(2,1)S(1)}, bf16[128,1664]{1,0:T(8,128)(2,1)S(1)}, u32[]{:S(2)}, u32[]{:S(2)}) collective-permute-start(bf16[128,1664]{1,0:T(8,128)(2,1)S(1)} %fusion.4.refs_0_), channel_id=1, source_target_pairs={{0,80},{16,96},{32,112},{48,64},{64,16},{80,32},{96,48},{112,0},{1... | collective-permute-start | bytes 1277960 | tf_op jit(solution)/shard_map/ppermute | solution.py:46
  28.2 112.8 %copy-start.4 = (bf16[128,1664]{1,0:T(8,128)(2,1)}, bf16[128,1664]{1,0:T(8,128)(2,1)S(1)}, u32[]{:S(2)}) copy-start(bf16[128,1664]{1,0:T(8,128)(2,1)S(1)} %collective-permute-done.refs_1_) | copy-start | bytes 1277956
  28.2 51.3 %collective-permute-start.5 = (bf16[128,1664]{1,0:T(8,128)(2,1)S(1)}, bf16[128,1664]{1,0:T(8,128)(2,1)S(1)}, u32[]{:S(2)}, u32[]{:S(2)}) collective-permute-start(bf16[128,1664]{1,0:T(8,128)(2,1)S(1)} %fusion.4.refs_0_), channel_id=1, source_target_pairs={{0,96},{16,112},{32,64},{48,80},{64,32},{80,48},{96,0},{112,16},{1... | collective-permute-start | bytes 1277960 | tf_op jit(solution)/shard_map/ppermute | solution.py:46
  41.5 55.5 %collective-permute-start.6 = (bf16[128,1664]{1,0:T(8,128)(2,1)S(1)}, bf16[128,1664]{1,0:T(8,128)(2,1)S(1)}, u32[]{:S(2)}, u32[]{:S(2)}) collective-permute-start(bf16[128,1664]{1,0:T(8,128)(2,1)S(1)} %fusion.4.refs_0_), channel_id=1, source_target_pairs={{0,112},{16,64},{32,80},{48,96},{64,48},{80,0},{96,16},{112,32},{1... | collective-permute-start | bytes 1277960 | tf_op jit(solution)/shard_map/ppermute | solution.py:46
  141.1 22.2 %collective-permute-start.10 = (bf16[128,1536]{1,0:T(8,128)(2,1)}, bf16[128,1536]{1,0:T(8,128)(2,1)S(1)}, u32[]{:S(2)}, u32[]{:S(2)}) collective-permute-start(bf16[128,1536]{1,0:T(8,128)(2,1)} %get-tuple-element.43.refs_0_.h2_ref), channel_id=1, source_target_pairs={{0,64},{16,80},{32,96},{48,112},{64,0},{80,16},{96,32},{112,48},{1... | collective-permute-start | bytes 1179656 | tf_op jit(solution)/shard_map/ppermute | solution.py:46
  143.2 36.7 %collective-permute-start.11 = (bf16[128,1536]{1,0:T(8,128)(2,1)}, bf16[128,1536]{1,0:T(8,128)(2,1)S(1)}, u32[]{:S(2)}, u32[]{:S(2)}) collective-permute-start(bf16[128,1536]{1,0:T(8,128)(2,1)} %get-tuple-element.43.refs_0_.h2_ref), channel_id=1, source_target_pairs={{0,80},{16,96},{32,112},{48,64},{64,16},{80,32},{96,48},{112,0},{1... | collective-permute-start | bytes 1179656 | tf_op jit(solution)/shard_map/ppermute | solution.py:46
  145.5 51.7 %collective-permute-start.12 = (bf16[128,1536]{1,0:T(8,128)(2,1)}, bf16[128,1536]{1,0:T(8,128)(2,1)S(1)}, u32[]{:S(2)}, u32[]{:S(2)}) collective-permute-start(bf16[128,1536]{1,0:T(8,128)(2,1)} %get-tuple-element.43.refs_0_.h2_ref), channel_id=1, source_target_pairs={{0,96},{16,112},{32,64},{48,80},{64,32},{80,48},{96,0},{112,16},{1... | collective-permute-start | bytes 1179656 | tf_op jit(solution)/shard_map/ppermute | solution.py:46
  147.8 66.3 %collective-permute-start.13 = (bf16[128,1536]{1,0:T(8,128)(2,1)}, bf16[128,1536]{1,0:T(8,128)(2,1)S(1)}, u32[]{:S(2)}, u32[]{:S(2)}) collective-permute-start(bf16[128,1536]{1,0:T(8,128)(2,1)} %get-tuple-element.43.refs_0_.h2_ref), channel_id=1, source_target_pairs={{0,112},{16,64},{32,80},{48,96},{64,48},{80,0},{96,16},{112,32},{1... | collective-permute-start | bytes 1179656 | tf_op jit(solution)/shard_map/ppermute | solution.py:46
  150.4 63.6 %collective-permute-start.7 = (bf16[128,1536]{1,0:T(8,128)(2,1)}, bf16[128,1536]{1,0:T(8,128)(2,1)S(1)}, u32[]{:S(2)}, u32[]{:S(2)}) collective-permute-start(bf16[128,1536]{1,0:T(8,128)(2,1)} %get-tuple-element.43.refs_0_.h2_ref), channel_id=1, source_target_pairs={{0,16},{16,32},{32,48},{48,0},{64,80},{80,96},{96,112},{112,64},{1... | collective-permute-start | bytes 1179656 | tf_op jit(solution)/shard_map/ppermute | solution.py:46
  163.3 50.8 %collective-permute-start.8 = (bf16[128,1536]{1,0:T(8,128)(2,1)}, bf16[128,1536]{1,0:T(8,128)(2,1)S(1)}, u32[]{:S(2)}, u32[]{:S(2)}) collective-permute-start(bf16[128,1536]{1,0:T(8,128)(2,1)} %get-tuple-element.43.refs_0_.h2_ref), channel_id=1, source_target_pairs={{0,32},{16,48},{32,0},{48,16},{64,96},{80,112},{96,64},{112,80},{1... | collective-permute-start | bytes 1179656 | tf_op jit(solution)/shard_map/ppermute | solution.py:46
  179.9 34.2 %collective-permute-start.9 = (bf16[128,1536]{1,0:T(8,128)(2,1)}, bf16[128,1536]{1,0:T(8,128)(2,1)S(1)}, u32[]{:S(2)}, u32[]{:S(2)}) collective-permute-start(bf16[128,1536]{1,0:T(8,128)(2,1)} %get-tuple-element.43.refs_0_.h2_ref), channel_id=1, source_target_pairs={{0,48},{16,0},{32,16},{48,32},{64,112},{80,64},{96,80},{112,96},{1... | collective-permute-start | bytes 1179656 | tf_op jit(solution)/shard_map/ppermute | solution.py:46
  312.4 31.0 %collective-permute-start.21 = (bf16[128,1664]{1,0:T(8,128)(2,1)}, bf16[128,1664]{1,0:T(8,128)(2,1)S(1)}, u32[]{:S(2)}, u32[]{:S(2)}) collective-permute-start(bf16[128,1664]{1,0:T(8,128)(2,1)} %get-tuple-element.62), channel_id=1, source_target_pairs={{0,48},{16,0},{32,16},{48,32},{64,112},{80,64},{96,80},{112,96},{1... | collective-permute-start | bytes 1277960 | tf_op jit(solution)/shard_map/ppermute | solution.py:46
  315.2 28.3 %collective-permute-start.22 = (bf16[128,1664]{1,0:T(8,128)(2,1)}, bf16[128,1664]{1,0:T(8,128)(2,1)S(1)}, u32[]{:S(2)}, u32[]{:S(2)}) collective-permute-start(bf16[128,1664]{1,0:T(8,128)(2,1)} %get-tuple-element.63), channel_id=1, source_target_pairs={{0,32},{16,48},{32,0},{48,16},{64,96},{80,112},{96,64},{112,80},{1... | collective-permute-start | bytes 1277960 | tf_op jit(solution)/shard_map/ppermute | solution.py:46
  316.0 36.8 %collective-permute-start.23 = (bf16[128,1664]{1,0:T(8,128)(2,1)}, bf16[128,1664]{1,0:T(8,128)(2,1)S(1)}, u32[]{:S(2)}, u32[]{:S(2)}) collective-permute-start(bf16[128,1664]{1,0:T(8,128)(2,1)} %get-tuple-element.64), channel_id=1, source_target_pairs={{0,16},{16,32},{32,48},{48,0},{64,80},{80,96},{96,112},{112,64},{1... | collective-permute-start | bytes 1277960 | tf_op jit(solution)/shard_map/ppermute | solution.py:46
  317.0 35.8 %collective-permute-start.24 = (bf16[128,1664]{1,0:T(8,128)(2,1)}, bf16[128,1664]{1,0:T(8,128)(2,1)S(1)}, u32[]{:S(2)}, u32[]{:S(2)}) collective-permute-start(bf16[128,1664]{1,0:T(8,128)(2,1)} %get-tuple-element.65), channel_id=1, source_target_pairs={{0,64},{16,80},{32,96},{48,112},{64,0},{80,16},{96,32},{112,48},{1... | collective-permute-start | bytes 1277960 | tf_op jit(solution)/shard_map/ppermute | solution.py:46
  319.7 33.1 %collective-permute-start.25 = (bf16[128,1664]{1,0:T(8,128)(2,1)}, bf16[128,1664]{1,0:T(8,128)(2,1)S(1)}, u32[]{:S(2)}, u32[]{:S(2)}) collective-permute-start(bf16[128,1664]{1,0:T(8,128)(2,1)} %get-tuple-element.66), channel_id=1, source_target_pairs={{0,112},{16,64},{32,80},{48,96},{64,48},{80,0},{96,16},{112,32},{1... | collective-permute-start | bytes 1277960 | tf_op jit(solution)/shard_map/ppermute | solution.py:46
  343.4 17.2 %collective-permute-start.26 = (bf16[128,1664]{1,0:T(8,128)(2,1)}, bf16[128,1664]{1,0:T(8,128)(2,1)S(1)}, u32[]{:S(2)}, u32[]{:S(2)}) collective-permute-start(bf16[128,1664]{1,0:T(8,128)(2,1)} %get-tuple-element.67), channel_id=1, source_target_pairs={{0,96},{16,112},{32,64},{48,80},{64,32},{80,48},{96,0},{112,16},{1... | collective-permute-start | bytes 1277960 | tf_op jit(solution)/shard_map/ppermute | solution.py:46
  343.6 24.6 %collective-permute-start.27 = (bf16[128,1664]{1,0:T(8,128)(2,1)}, bf16[128,1664]{1,0:T(8,128)(2,1)S(1)}, u32[]{:S(2)}, u32[]{:S(2)}) collective-permute-start(bf16[128,1664]{1,0:T(8,128)(2,1)} %get-tuple-element.68), channel_id=1, source_target_pairs={{0,80},{16,96},{32,112},{48,64},{64,16},{80,32},{96,48},{112,0},{1... | collective-permute-start | bytes 1277960 | tf_op jit(solution)/shard_map/ppermute | solution.py:46
  397.2 268.9 %reduce-scatter.5.cloned.1.call-start = ((), (), s32[]{:S(2)}) async-start(), calls=%async_computation.5 | async-start | bytes 25067520 | tf_op jit(solution)/shard_map/reduce_scatter | solution.py:642
  401.9 86.8 %collective-permute-start.14 = (bf16[128,1536]{1,0:T(8,128)(2,1)}, bf16[128,1536]{1,0:T(8,128)(2,1)S(1)}, u32[]{:S(2)}, u32[]{:S(2)}) collective-permute-start(bf16[128,1536]{1,0:T(8,128)(2,1)} %get-tuple-element.48), channel_id=1, source_target_pairs={{0,48},{16,0},{32,16},{48,32},{64,112},{80,64},{96,80},{112,96},{1... | collective-permute-start | bytes 1179656 | tf_op jit(solution)/shard_map/ppermute | solution.py:46
  402.2 89.2 %collective-permute-start.15 = (bf16[128,1536]{1,0:T(8,128)(2,1)}, bf16[128,1536]{1,0:T(8,128)(2,1)S(1)}, u32[]{:S(2)}, u32[]{:S(2)}) collective-permute-start(bf16[128,1536]{1,0:T(8,128)(2,1)} %get-tuple-element.49), channel_id=1, source_target_pairs={{0,32},{16,48},{32,0},{48,16},{64,96},{80,112},{96,64},{112,80},{1... | collective-permute-start | bytes 1179656 | tf_op jit(solution)/shard_map/ppermute | solution.py:46
  482.7 10.0 %collective-permute-start.28 = (bf16[96,640]{1,0:T(8,128)(2,1)S(1)}, bf16[96,640]{1,0:T(8,128)(2,1)S(1)}, u32[]{:S(2)}, u32[]{:S(2)}) collective-permute-start(bf16[96,640]{1,0:T(8,128)(2,1)S(1)} %get-tuple-element.128), channel_id=1, source_target_pairs={{0,16},{16,32},{32,48},{48,0},{64,80},{80,96},{96,112},{112,64},{1... | collective-permute-start | bytes 368648 | tf_op jit(solution)/shard_map/ppermute | solution.py:46
  484.5 11.0 %collective-permute-start.29 = (bf16[96,640]{1,0:T(8,128)(2,1)S(1)}, bf16[96,640]{1,0:T(8,128)(2,1)S(1)}, u32[]{:S(2)}, u32[]{:S(2)}) collective-permute-start(bf16[96,640]{1,0:T(8,128)(2,1)S(1)} %get-tuple-element.129), channel_id=1, source_target_pairs={{0,32},{16,48},{32,0},{48,16},{64,96},{80,112},{96,64},{112,80},{1... | collective-permute-start | bytes 368648 | tf_op jit(solution)/shard_map/ppermute | solution.py:46
  487.4 10.9 %collective-permute-start.30 = (bf16[96,640]{1,0:T(8,128)(2,1)S(1)}, bf16[96,640]{1,0:T(8,128)(2,1)S(1)}, u32[]{:S(2)}, u32[]{:S(2)}) collective-permute-start(bf16[96,640]{1,0:T(8,128)(2,1)S(1)} %get-tuple-element.130), channel_id=1, source_target_pairs={{0,48},{16,0},{32,16},{48,32},{64,112},{80,64},{96,80},{112,96},{1... | collective-permute-start | bytes 368648 | tf_op jit(solution)/shard_map/ppermute | solution.py:46
  488.8 9.5 %collective-permute-start.31 = (bf16[96,640]{1,0:T(8,128)(2,1)S(1)}, bf16[96,640]{1,0:T(8,128)(2,1)S(1)}, u32[]{:S(2)}, u32[]{:S(2)}) collective-permute-start(bf16[96,640]{1,0:T(8,128)(2,1)S(1)} %get-tuple-element.131), channel_id=1, source_target_pairs={{0,64},{16,80},{32,96},{48,112},{64,0},{80,16},{96,32},{112,48},{1... | collective-permute-start | bytes 368648 | tf_op jit(solution)/shard_map/ppermute | solution.py:46
  491.3 10.8 %collective-permute-start.32 = (bf16[96,640]{1,0:T(8,128)(2,1)S(1)}, bf16[96,640]{1,0:T(8,128)(2,1)S(1)}, u32[]{:S(2)}, u32[]{:S(2)}) collective-permute-start(bf16[96,640]{1,0:T(8,128)(2,1)S(1)} %get-tuple-element.132), channel_id=1, source_target_pairs={{0,80},{16,96},{32,112},{48,64},{64,16},{80,32},{96,48},{112,0},{1... | collective-permute-start | bytes 368648 | tf_op jit(solution)/shard_map/ppermute | solution.py:46
  492.6 11.9 %collective-permute-start.33 = (bf16[96,640]{1,0:T(8,128)(2,1)S(1)}, bf16[96,640]{1,0:T(8,128)(2,1)S(1)}, u32[]{:S(2)}, u32[]{:S(2)}) collective-permute-start(bf16[96,640]{1,0:T(8,128)(2,1)S(1)} %get-tuple-element.133), channel_id=1, source_target_pairs={{0,96},{16,112},{32,64},{48,80},{64,32},{80,48},{96,0},{112,16},{1... | collective-permute-start | bytes 368648 | tf_op jit(solution)/shard_map/ppermute | solution.py:46
  495.5 14.7 %collective-permute-start.34 = (bf16[96,640]{1,0:T(8,128)(2,1)S(1)}, bf16[96,640]{1,0:T(8,128)(2,1)S(1)}, u32[]{:S(2)}, u32[]{:S(2)}) collective-permute-start(bf16[96,640]{1,0:T(8,128)(2,1)S(1)} %get-tuple-element.134), channel_id=1, source_target_pairs={{0,112},{16,64},{32,80},{48,96},{64,48},{80,0},{96,16},{112,32},{1... | collective-permute-start | bytes 368648 | tf_op jit(solution)/shard_map/ppermute | solution.py:46
  498.3 14.4 %collective-permute-start.16 = (bf16[128,1536]{1,0:T(8,128)(2,1)}, bf16[128,1536]{1,0:T(8,128)(2,1)S(1)}, u32[]{:S(2)}, u32[]{:S(2)}) collective-permute-start(bf16[128,1536]{1,0:T(8,128)(2,1)} %get-tuple-element.50), channel_id=1, source_target_pairs={{0,16},{16,32},{32,48},{48,0},{64,80},{80,96},{96,112},{112,64},{1... | collective-permute-start | bytes 1179656 | tf_op jit(solution)/shard_map/ppermute | solution.py:46
  498.3 23.8 %collective-permute-start.17 = (bf16[128,1536]{1,0:T(8,128)(2,1)}, bf16[128,1536]{1,0:T(8,128)(2,1)S(1)}, u32[]{:S(2)}, u32[]{:S(2)}) collective-permute-start(bf16[128,1536]{1,0:T(8,128)(2,1)} %get-tuple-element.51), channel_id=1, source_target_pairs={{0,64},{16,80},{32,96},{48,112},{64,0},{80,16},{96,32},{112,48},{1... | collective-permute-start | bytes 1179656 | tf_op jit(solution)/shard_map/ppermute | solution.py:46
  502.2 31.6 %collective-permute-start.18 = (bf16[128,1536]{1,0:T(8,128)(2,1)}, bf16[128,1536]{1,0:T(8,128)(2,1)S(1)}, u32[]{:S(2)}, u32[]{:S(2)}) collective-permute-start(bf16[128,1536]{1,0:T(8,128)(2,1)} %get-tuple-element.52), channel_id=1, source_target_pairs={{0,112},{16,64},{32,80},{48,96},{64,48},{80,0},{96,16},{112,32},{1... | collective-permute-start | bytes 1179656 | tf_op jit(solution)/shard_map/ppermute | solution.py:46
  504.5 41.5 %collective-permute-start.19 = (bf16[128,1536]{1,0:T(8,128)(2,1)}, bf16[128,1536]{1,0:T(8,128)(2,1)}, u32[]{:S(2)}, u32[]{:S(2)}) collective-permute-start(bf16[128,1536]{1,0:T(8,128)(2,1)} %get-tuple-element.53), channel_id=1, source_target_pairs={{0,96},{16,112},{32,64},{48,80},{64,32},{80,48},{96,0},{112,16},{1... | collective-permute-start | bytes 1179656 | tf_op jit(solution)/shard_map/ppermute | solution.py:46
  510.9 48.6 %collective-permute-start.20 = (bf16[128,1536]{1,0:T(8,128)(2,1)}, bf16[128,1536]{1,0:T(8,128)(2,1)}, u32[]{:S(2)}, u32[]{:S(2)}) collective-permute-start(bf16[128,1536]{1,0:T(8,128)(2,1)} %get-tuple-element.54), channel_id=1, source_target_pairs={{0,80},{16,96},{32,112},{48,64},{64,16},{80,32},{96,48},{112,0},{1... | collective-permute-start | bytes 1179656 | tf_op jit(solution)/shard_map/ppermute | solution.py:46
  512.7 50.0 %collective-permute-start.35 = (bf16[96,640]{1,0:T(8,128)(2,1)S(1)}, bf16[96,640]{1,0:T(8,128)(2,1)S(1)}, u32[]{:S(2)}, u32[]{:S(2)}) collective-permute-start(bf16[96,640]{1,0:T(8,128)(2,1)S(1)} %add_convert_fusion), channel_id=1, source_target_pairs={{0,16},{16,32},{32,48},{48,0},{64,80},{80,96},{96,112},{112,64},{1... | collective-permute-start | bytes 368648 | tf_op jit(solution)/shard_map/ppermute | solution.py:46
  522.1 42.5 %collective-permute-start.36 = (bf16[96,640]{1,0:T(8,128)(2,1)S(1)}, bf16[96,640]{1,0:T(8,128)(2,1)S(1)}, u32[]{:S(2)}, u32[]{:S(2)}) collective-permute-start(bf16[96,640]{1,0:T(8,128)(2,1)S(1)} %add_convert_fusion), channel_id=1, source_target_pairs={{0,32},{16,48},{32,0},{48,16},{64,96},{80,112},{96,64},{112,80},{1... | collective-permute-start | bytes 368648 | tf_op jit(solution)/shard_map/ppermute | solution.py:46
  533.8 39.8 %collective-permute-start.37 = (bf16[96,640]{1,0:T(8,128)(2,1)S(1)}, bf16[96,640]{1,0:T(8,128)(2,1)S(1)}, u32[]{:S(2)}, u32[]{:S(2)}) collective-permute-start(bf16[96,640]{1,0:T(8,128)(2,1)S(1)} %add_convert_fusion), channel_id=1, source_target_pairs={{0,48},{16,0},{32,16},{48,32},{64,112},{80,64},{96,80},{112,96},{1... | collective-permute-start | bytes 368648 | tf_op jit(solution)/shard_map/ppermute | solution.py:46
  546.0 27.8 %collective-permute-start.38 = (bf16[96,640]{1,0:T(8,128)(2,1)S(1)}, bf16[96,640]{1,0:T(8,128)(2,1)S(1)}, u32[]{:S(2)}, u32[]{:S(2)}) collective-permute-start(bf16[96,640]{1,0:T(8,128)(2,1)S(1)} %add_convert_fusion), channel_id=1, source_target_pairs={{0,64},{16,80},{32,96},{48,112},{64,0},{80,16},{96,32},{112,48},{1... | collective-permute-start | bytes 368648 | tf_op jit(solution)/shard_map/ppermute | solution.py:46
  559.4 14.5 %collective-permute-start.39 = (bf16[96,640]{1,0:T(8,128)(2,1)S(1)}, bf16[96,640]{1,0:T(8,128)(2,1)}, u32[]{:S(2)}, u32[]{:S(2)}) collective-permute-start(bf16[96,640]{1,0:T(8,128)(2,1)S(1)} %add_convert_fusion), channel_id=1, source_target_pairs={{0,80},{16,96},{32,112},{48,64},{64,16},{80,32},{96,48},{112,0},{1... | collective-permute-start | bytes 368648 | tf_op jit(solution)/shard_map/ppermute | solution.py:46
  562.6 12.4 %collective-permute-start.40 = (bf16[96,640]{1,0:T(8,128)(2,1)S(1)}, bf16[96,640]{1,0:T(8,128)(2,1)}, u32[]{:S(2)}, u32[]{:S(2)}) collective-permute-start(bf16[96,640]{1,0:T(8,128)(2,1)S(1)} %add_convert_fusion), channel_id=1, source_target_pairs={{0,96},{16,112},{32,64},{48,80},{64,32},{80,48},{96,0},{112,16},{1... | collective-permute-start | bytes 368648 | tf_op jit(solution)/shard_map/ppermute | solution.py:46
  564.6 11.5 %collective-permute-start.41 = (bf16[96,640]{1,0:T(8,128)(2,1)S(1)}, bf16[96,640]{1,0:T(8,128)(2,1)}, u32[]{:S(2)}, u32[]{:S(2)}) collective-permute-start(bf16[96,640]{1,0:T(8,128)(2,1)S(1)} %add_convert_fusion), channel_id=1, source_target_pairs={{0,112},{16,64},{32,80},{48,96},{64,48},{80,0},{96,16},{112,32},{1... | collective-permute-start | bytes 368648 | tf_op jit(solution)/shard_map/ppermute | solution.py:46
  (35 other events, 1075.5 us)
Sparse Core Ops, SparseCore 0:
  11.9 111.1 all-gather.2
  124.8 155.5 all-gather.4
  397.3 83.8 reduce-scatter.2
  483.5 182.5 reduce-scatter.4

commit v2 on v1

v2 whole, which is shorter than its diff:
```python
import jax
import jax.numpy as jnp
import numpy as np
from jax import lax
from jax.experimental import pallas as pl
from jax.experimental.pallas import tpu as pltpu
from jax.sharding import PartitionSpec as P

QUERY_HEADS = 24
KEY_VALUE_HEADS = 8
GROUP = QUERY_HEADS // KEY_VALUE_HEADS
HEAD_DIM = 64
HALF = HEAD_DIM // 2
E = 40
H = 512
D = 1536
T = 128
CAP = 32
NORM_EPSILON = 1e-05
SCALE = HEAD_DIM ** (-0.5)

Z = 4
PEERS = 8
LOCAL = E // PEERS
SLOTS = LOCAL * CAP
LANES = 128
CHIPS = 8
LINE = 4
TOPK = 8
SHARDS = 2 * CHIPS
ROWS = D // SHARDS
QH = QUERY_HEADS // Z
KH = KEY_VALUE_HEADS // Z
QW = QH * HEAD_DIM
KW = KH * HEAD_DIM
QKV = QW + 2 * KW
MAIN = QW + QKV
SLICE = MAIN + LANES
VMEM_LIMIT = 60 * 1024 * 1024

F32 = jnp.float32
BF16 = jnp.bfloat16


def peer(index, hop, back=False):
    shift = hop % Z
    turned = (index % Z + (Z - shift if back else shift)) % Z
    return (index // Z + hop // Z) % 2 * Z + turned


def send(value, hop, back=False):
    if hop == 0:
        return value
    return lax.ppermute(value, "expert", [(i, peer(i, hop, back)) for i in range(PEERS)])


def chip_at(index, hop, back=False):
    shift = hop % 4
    turned = (index // 2 % 4 + (4 - shift if back else shift)) % 4
    return (index // 8 + hop // 4) % 2 * 4 + turned


def send_chip(value, hop):
    if hop == 0:
        return value
    pairs = [(i, 2 * chip_at(i, hop) + i % 2) for i in range(SHARDS)]
    return lax.ppermute(value, "fsdp", pairs)


def after(value, *others):
    return lax.optimization_barrier((value, others))[0]


def send_across(pair):
    def flip(value, half, low):
        pairs = []
        for index in range(PEERS * SHARDS):
            group, place = index // SHARDS, index % SHARDS
            pairs.append((index, (group ^ (half * Z)) * SHARDS + (place ^ (low * CHIPS))))
        return lax.ppermute(value, ("expert", "fsdp"), pairs)

    return flip(pair[1], 0, 1), flip(pair[0], 1, 0), flip(pair[1], 1, 1)


def swap_core(value):
    return lax.ppermute(value, "fsdp", [(i, i ^ 1) for i in range(SHARDS)])


def mm(left, right):
    return jnp.dot(left, right, preferred_element_type=F32)


def mm_nt(left, right):
    return lax.dot_general(left, right, (((1,), (1,)), ((), ())), preferred_element_type=F32)


def mm_tn(left, right):
    return lax.dot_general(left, right, (((0,), (0,)), ((), ())), preferred_element_type=F32)


def rope_tables():
    frequency = np.exp(-np.log(10000.0) * np.arange(HALF, dtype=np.float64) * 2.0 / HEAD_DIM)
    angles = np.arange(T, dtype=np.float64)[:, None] * frequency[None, :]
    cosine = np.tile(np.cos(angles), (1, 4)).astype(np.float32)
    sine = np.sin(angles)
    signed = np.tile(np.concatenate([-sine, sine], axis=1), (1, 2)).astype(np.float32)
    return cosine, signed


def swap_halves(values):
    width = values.shape[1]
    lane = lax.broadcasted_iota(jnp.int32, values.shape, 1)
    up = pltpu.roll(values, width - HALF, 1)
    down = pltpu.roll(values, HALF, 1)
    return jnp.where(lane % HEAD_DIM < HALF, up, down)


def wide(table, width):
    return jnp.concatenate([table] * (width // LANES), axis=1)


def rotate(values, cosine, signed):
    width = values.shape[1]
    return values * wide(cosine, width) + swap_halves(values) * wide(signed, width)


def rotate_back(values, cosine, signed):
    width = values.shape[1]
    return values * wide(cosine, width) + swap_halves(values * wide(signed, width))


def gain_rows(small):
    pick = lax.broadcasted_iota(jnp.int32, (16, LANES), 1) == (
        lax.broadcasted_iota(jnp.int32, (16, LANES), 0) + E
    )
    return mm_nt(pick.astype(BF16), small)


def norm_of(values):
    inverse = lax.rsqrt(jnp.mean(values * values, axis=-1, keepdims=True) + NORM_EPSILON)
    return values * inverse, inverse


def head(ref, rows, index):
    return ref[rows, index * HEAD_DIM : (index + 1) * HEAD_DIM]


def stack_heads(ref, rows, first):
    return jnp.concatenate([head(ref, rows, first + index) for index in range(GROUP)], axis=0)


def probabilities(query, key):
    scores = mm_nt(query, key) * SCALE
    rows = lax.broadcasted_iota(jnp.int32, scores.shape, 0) % T
    cols = lax.broadcasted_iota(jnp.int32, scores.shape, 1)
    scores = jnp.where(rows >= cols, scores, -jnp.inf)
    exponent = jnp.exp(scores - jnp.max(scores, axis=-1, keepdims=True))
    return exponent / jnp.sum(exponent, axis=-1, keepdims=True)


def whole(shape):
    return pl.BlockSpec(shape, lambda *_: (0,) * len(shape))


SCALARS = pl.BlockSpec(memory_space=pltpu.SMEM)


def params(**more):
    return pltpu.CompilerParams(vmem_limit_bytes=VMEM_LIMIT, **more)


WEIGHT = 60


def cost(flops, moved):
    return pl.CostEstimate(flops=flops * WEIGHT, bytes_accessed=moved * WEIGHT, transcendentals=0)


def shape(dims, kind):
    return jax.ShapeDtypeStruct(dims, kind)


def call(kernel, name, inputs, in_specs, outputs, out_specs=None, scratch=(), flops=0, moved=0):
    in_specs = [whole(v.shape) if spec is None else spec for v, spec in zip(inputs, in_specs)]
    if out_specs is None:
        out_specs = [whole(o.shape) for o in outputs]
    return pl.pallas_call(
        kernel,
        grid=(1,),
        in_specs=in_specs,
        out_specs=out_specs,
        out_shape=outputs,
        scratch_shapes=list(scratch),
        compiler_params=params(),
        cost_estimate=cost(flops, moved),
        name=name,
    )(*inputs)


SMALL_SPEC = pl.BlockSpec((SHARDS, ROWS, LANES), lambda *_: (0, 0, MAIN // LANES))
X_SPEC = pl.BlockSpec((T, D), lambda *_: (0, 0))
DY_SPEC = pl.BlockSpec((T, D), lambda *_: (0, 1))
OUT_SPEC = pl.BlockSpec((SHARDS, ROWS, QW), lambda *_: (0, 0, 0))


def small_of(ref):
    return ref[...].reshape(D, LANES)


def columns_of(index):
    return pl.ds(pl.multiple_of(index * QW, QW), QW)


def pack_kernel(z_ref, out_ref, query_ref, key_ref, value_ref, router_ref, one_ref, two_ref, own_ref):
    own_ref[:, 0:QW] = out_ref[...]
    own_ref[:, QW : 2 * QW] = query_ref[...]
    own_ref[:, 2 * QW : 2 * QW + KW] = key_ref[...]
    own_ref[:, 2 * QW + KW : MAIN] = value_ref[...]
    narrow = [router_ref[...], one_ref[...], two_ref[...], jnp.zeros((LANES - E - 2, ROWS), BF16)]
    own_ref[:, MAIN:] = jnp.concatenate([v.astype(F32) for v in narrow], axis=0).T.astype(BF16)


def pack(z, w_out, w_query, key_weight, value_weight, router, one, two):
    def slice_of(width):
        return pl.BlockSpec((ROWS, width), lambda i, z: (0, z[0]))

    return pl.pallas_call(
        pack_kernel,
        grid_spec=pltpu.PrefetchScalarGridSpec(
            num_scalar_prefetch=1,
            grid=(1,),
            in_specs=[
                slice_of(QW),
                slice_of(QW),
                slice_of(KW),
                slice_of(KW),
                whole((E, ROWS)),
                whole((1, ROWS)),
                whole((1, ROWS)),
            ],
            out_specs=whole((ROWS, SLICE)),
        ),
        out_shape=shape((ROWS, SLICE), BF16),
        compiler_params=params(),
        cost_estimate=cost(ROWS * SLICE, 1 << 20),
        name="pack",
    )(z, w_out, w_query, key_weight, value_weight, router, one, two)


def project_kernel(order_ref, cos_ref, sin_ref, *refs):
    own, other, xs = refs[:LINE], refs[LINE : 2 * LINE], refs[2 * LINE : 2 * LINE + Z]
    w_ref, gains_ref, h1_ref, qkv_ref, ob_ref = refs[2 * LINE + Z :]
    for chip in range(CHIPS):
        w_ref[order_ref[chip]] = own[chip % LINE][chip // LINE]
        w_ref[order_ref[CHIPS + chip]] = other[chip % LINE][chip // LINE]
    gains = gain_rows(w_ref[:, :, MAIN:].reshape(D, LANES))
    gains_ref[...] = gains
    for hop in range(Z):
        normed, _ = norm_of(xs[hop][...].astype(F32))
        h1_ref[hop * T : (hop + 1) * T] = (normed * gains[0:1, :]).astype(BF16)
    pre = mm(h1_ref[...], w_ref[:, :, QW:MAIN].reshape(D, QKV))
    cosine = jnp.concatenate([cos_ref[...]] * Z, axis=0)
    signed = jnp.concatenate([sin_ref[...]] * Z, axis=0)
    qkv_ref[:, 0:QW] = rotate(pre[:, 0:QW], cosine, signed).astype(BF16)
    qkv_ref[:, QW : QW + KW] = rotate(pre[:, QW : QW + KW], cosine, signed).astype(BF16)
    qkv_ref[:, QW + KW :] = pre[:, QW + KW :].astype(BF16)
    for hop in range(Z):
        rows = slice(hop * T, (hop + 1) * T)
        for group in range(KH):
            key, value = head(qkv_ref, rows, QH + group), head(qkv_ref, rows, QH + KH + group)
            query = stack_heads(qkv_ref, rows, group * GROUP)
            result = mm(probabilities(query, key).astype(BF16), value).astype(BF16)
            for index in range(GROUP):
                at = (group * GROUP + index) * HEAD_DIM
                ob_ref[rows, at : at + HEAD_DIM] = result[index * T : (index + 1) * T]


def project(order, cosine, signed, own, other, xs):
    return call(
        project_kernel,
        "project",
        [order, cosine, signed, *own, *other, *xs],
        [SCALARS] + [None] * (2 + 2 * LINE) + [X_SPEC] * Z,
        [
            shape((SHARDS, ROWS, SLICE), BF16),
            shape((16, D), F32),
            shape((Z * T, D), BF16),
            shape((Z * T, QKV), BF16),
            shape((Z * T, QW), BF16),
        ],
        flops=2 * Z * T * D * QKV,
        moved=12 << 20,
    )


def out_project_kernel(peers_ref, w_ref, *refs):
    obs, full_ref, outs = refs[:Z], refs[Z], refs[Z + 1 :]
    total = jnp.zeros((Z * T, QW), F32)
    for hop in range(Z):
        peer_index = peers_ref[hop]
        blocks = [(row - hop) % Z for row in range(Z)]
        rows = jnp.concatenate([obs[hop][b * T : (b + 1) * T, :] for b in blocks], axis=0)
        full_ref[:, columns_of(peer_index)] = rows
        weight = w_ref[pl.ds(peer_index * Z, Z)].reshape(QW, QW)
        total = total + mm(rows, weight)
    for hop in range(Z):
        outs[hop][...] = total[hop * T : (hop + 1) * T].astype(BF16)


def out_project(peers, w, obs):
    return call(
        out_project_kernel,
        "out_project",
        [peers, w, *obs],
        [SCALARS, OUT_SPEC] + [None] * Z,
        [shape((Z * T, D), BF16)] + [shape((T, QW), BF16)] * Z,
        flops=2 * Z * T * D * QW,
        moved=6 << 20,
    )


def cut_out_kernel(peers_ref, w_ref, *outs):
    for hop in range(Z):
        outs[hop][...] = w_ref[pl.ds(peers_ref[hop] * Z, Z)].reshape(QW, QW)


def cut_out(peers, w):
    return call(
        cut_out_kernel,
        "cut_out",
        [peers, w],
        [SCALARS, OUT_SPEC],
        [shape((QW, QW), BF16)] * Z,
        flops=D * QW,
        moved=2 << 20,
    )


def residual_kernel(peers_ref, x_ref, gains_ref, *refs):
    pieces, (x1_ref, h2_ref) = refs[:Z], refs[Z:]
    x1_ref[...] = x_ref[...].astype(F32)
    for hop in range(Z):
        x1_ref[:, columns_of(peers_ref[hop])] += pieces[hop][...].astype(F32)
    normed, _ = norm_of(x1_ref[...])
    h2_ref[...] = (normed * gains_ref[1:2, :]).astype(BF16)


def residual(peers, x, gains, pieces):
    return call(
        residual_kernel,
        "residual",
        [peers, x, gains, *pieces],
        [SCALARS] + [None] * (2 + Z),
        [shape((T, D), F32), shape((T, D), BF16)],
        flops=T * D * 8,
        moved=2 << 20,
    )


def gate_kernel(small_ref, member_ref, chosen_ref, place_ref, *refs):
    rows, (gates_ref, slot_gate_ref, b_ref) = refs[:Z], refs[Z:]
    small = small_of(small_ref)
    for hop in range(Z):
        h2 = rows[hop][...]
        member = member_ref[hop] > 0.5
        logits = jnp.where(member, mm(h2, small), -jnp.inf)
        exponent = jnp.exp(logits - jnp.max(logits, axis=-1, keepdims=True))
        gates = exponent / jnp.sum(exponent, axis=-1, keepdims=True)
        gates_ref[hop] = gates
        high = gates.astype(BF16)
        low = (gates - high.astype(F32)).astype(BF16)
        place = place_ref[hop]
        spread = mm(place, high) + mm(place, low)
        picked = jnp.sum(spread * chosen_ref[...], axis=-1, keepdims=True)
        slot_gate_ref[:, hop] = picked.reshape(LOCAL, CAP, 1)
        b_ref[:, hop] = mm(place, h2).astype(BF16).reshape(LOCAL, CAP, D)


def gate_rows(half, w, member, chosen, place, rows):
    gates, slot_gate, b = call(
        gate_kernel,
        "gate_rows",
        [w, member, chosen, place, *rows],
        [
            SMALL_SPEC,
            pl.BlockSpec((Z, T, LANES), lambda *_: (half, 0, 0)),
            None,
            pl.BlockSpec((Z, SLOTS, T), lambda *_: (half, 0, 0)),
        ]
        + [None] * Z,
        [
            shape((Z, T, LANES), F32),
            shape((LOCAL, Z, CAP, 1), F32),
            shape((LOCAL, Z, CAP, D), BF16),
        ],
        flops=2 * Z * SLOTS * T * D,
        moved=5 << 20,
    )
    return gates, slot_gate.reshape(LOCAL, Z * CAP, 1), b.reshape(LOCAL, Z * CAP, D)


def spread_kernel(place_ref, *refs):
    rows, out_ref = refs[:PEERS], refs[PEERS]
    for hop in range(PEERS):
        out_ref[:, hop] = mm(place_ref[hop], rows[hop][...]).astype(BF16).reshape(LOCAL, CAP, D)


def spread_rows(place, line, other):
    return call(
        spread_kernel,
        "spread_rows",
        [place, *line, *other],
        [None] + [DY_SPEC] * Z + [X_SPEC] * Z,
        [shape((LOCAL, PEERS, CAP, D), BF16)],
        flops=2 * PEERS * SLOTS * T * D,
        moved=8 << 20,
    )[0].reshape(LOCAL, PEERS * CAP, D)


def expert_kernel(
    me_ref, b0_ref, b1_ref, dyr_ref, gate0_ref, gate1_ref, w_ref, gy_ref, db_ref, grad_ref
):
    rows = jnp.concatenate([b0_ref[0], b1_ref[0]], axis=0)
    gate = jnp.concatenate([gate0_ref[0], gate1_ref[0]], axis=0)
    down = w_ref[0, :, 2 * H : 3 * H]
    pre = mm(rows, w_ref[0, :, 0 : 2 * H])
    gate_pre, up_pre = pre[:, :H], pre[:, H:]
    sigmoid = 1.0 / (1.0 + jnp.exp(-gate_pre))
    silu = gate_pre * sigmoid
    activated = (silu * up_pre).astype(BF16)
    result = mm_nt(activated, down).astype(BF16).astype(F32)
    raw = dyr_ref[0].astype(F32)
    gy_ref[0] = (gate * result).astype(BF16)
    inner = jnp.sum(raw * result, axis=-1, keepdims=True)
    grad_rows = (gate * raw).astype(BF16)
    grad_act = mm(grad_rows, down)
    grad_ref[0, :, 2 * H : 3 * H] = mm_tn(grad_rows, activated).astype(BF16)
    grad_gate = (grad_act * up_pre * sigmoid * (1.0 + gate_pre * (1.0 - sigmoid))).astype(BF16)
    grad_up = (grad_act * silu).astype(BF16)
    both = jnp.concatenate([grad_gate, grad_up], axis=1)
    db_ref[0, :, 0:D] = mm_nt(both, w_ref[0, :, 0 : 2 * H]).astype(BF16)
    grad_ref[0, :, 0 : 2 * H] = mm_tn(rows, both).astype(BF16)
    expert = me_ref[0] * LOCAL + pl.program_id(0)
    lane = lax.broadcasted_iota(jnp.int32, (PEERS * CAP, LANES), 1)
    high = inner.astype(BF16).astype(F32)
    low = inner - high
    tail = jnp.where(lane == expert, high, jnp.where(lane == expert + E, low, 0.0))
    db_ref[0, :, D : D + LANES] = tail.astype(BF16)


def per_expert(*dims):
    return pl.BlockSpec((1,) + dims, lambda e: (e, 0, 0))


def experts(me, b, dyr, slot_gate, pack):
    rows = PEERS * CAP
    return pl.pallas_call(
        expert_kernel,
        grid=(LOCAL,),
        in_specs=[
            SCALARS,
            per_expert(rows // 2, D),
            per_expert(rows // 2, D),
            per_expert(rows, D),
            per_expert(rows // 2, 1),
            per_expert(rows // 2, 1),
            per_expert(D, 3 * H),
        ],
        out_specs=[
            per_expert(rows, D),
            per_expert(rows, D + LANES),
            per_expert(D, 3 * H),
        ],
        out_shape=[
            shape((LOCAL, rows, D), BF16),
            shape((LOCAL, rows, D + LANES), BF16),
            shape((LOCAL, D, 3 * H), BF16),
        ],
        compiler_params=params(),
        cost_estimate=cost(18 * LOCAL * rows * D * H, 60 << 20),
        name="experts",
    )(me, *b, dyr, *slot_gate, pack)


def collect_kernel(place_ref, value_ref, *out_refs):
    for hop in range(PEERS):
        rows = value_ref[:, hop].reshape(SLOTS, value_ref.shape[-1])
        out_refs[hop][...] = mm_tn(place_ref[hop], rows).astype(BF16)


def collect(place, values, name):
    width = values.shape[-1]
    return call(
        collect_kernel,
        name,
        [place, values.reshape(LOCAL, PEERS, CAP, width)],
        [None, None],
        [shape((T, width), BF16)] * PEERS,
        flops=2 * PEERS * SLOTS * T * width,
        moved=8 << 20,
    )


def mix(x1, returns, other):
    return call(
        add_kernel,
        "mix",
        [x1, *returns, other],
        [None] + [DY_SPEC] * Z + [None],
        [shape((T, D), BF16)],
        flops=T * D * Z,
        moved=4 << 20,
    )[0]


def norm_back(grad, normed, inverse, gain):
    scaled = grad * gain
    return inverse * (scaled - normed * jnp.mean(scaled * normed, axis=-1, keepdims=True))


def token_back_kernel(
    x1_ref, dy_ref, gates_ref, small_ref, gains_ref, *refs
):
    parts, (dx1_ref, dlogits_ref, scaled_ref, da_ref) = refs[: Z + 1], refs[Z + 1 :]
    total = parts[0][...].astype(F32)
    for ref in parts[1:]:
        total = total + ref[...].astype(F32)
    grad, tail = total[:, :D], total[:, D:]
    lane = lax.broadcasted_iota(jnp.int32, (T, LANES), 1)
    inner = jnp.where(lane < E, tail + pltpu.roll(tail, LANES - E, 1), 0.0)
    gates = gates_ref[0]
    score = gates * (inner - jnp.sum(gates * inner, axis=-1, keepdims=True))
    dlogits_ref[...] = score.astype(BF16)
    grad = grad + mm_nt(dlogits_ref[...], small_of(small_ref))
    normed, inverse = norm_of(x1_ref[...])
    scaled_ref[...] = (grad * normed).astype(BF16)
    through = dy_ref[...].astype(F32) + norm_back(grad, normed, inverse, gains_ref[1:2, :])
    dx1_ref[...] = through
    da_ref[...] = through.astype(BF16)


def token_back(x1, dy, gates, w, gains, parts):
    return call(
        token_back_kernel,
        "token_back",
        [x1, dy, gates, w, gains, *parts],
        [None, None, pl.BlockSpec((1, T, LANES), lambda *_: (0, 0, 0)), SMALL_SPEC]
        + [None] * (1 + len(parts)),
        [
            shape((T, D), F32),
            shape((T, LANES), BF16),
            shape((T, D), BF16),
            shape((T, D), BF16),
        ],
        flops=T * D * 64,
        moved=6 << 20,
    )


def shadow_kernel(qkv_ref, h2_ref, dlogits_ref, scaled_ref, *refs):
    xs, (small_ref, inverse_ref, prob_ref) = refs[:Z], refs[Z:]
    lane = lax.broadcasted_iota(jnp.int32, (T, LANES), 1)
    small = mm_tn(h2_ref[...], dlogits_ref[...])
    small_ref[...] = small + mm_tn(scaled_ref[...], (lane == E + 1).astype(BF16))
    for hop in range(Z):
        rows = slice(hop * T, (hop + 1) * T)
        _, inverse = norm_of(xs[hop][...].astype(F32))
        inverse_ref[rows] = inverse
        for group in range(KH):
            query = stack_heads(qkv_ref, rows, group * GROUP)
            prob_ref[hop * KH + group] = probabilities(query, head(qkv_ref, rows, QH + group))


def shadow(qkv, h2, dlogits, scaled, xs):
    return call(
        shadow_kernel,
        "shadow",
        [qkv, h2, dlogits, scaled, *xs],
        [None] * 4 + [X_SPEC] * Z,
        [
            shape((D, LANES), F32),
            shape((Z * T, 1), F32),
            shape((Z * KH, GROUP * T, T), F32),
        ],
        flops=Z * T * D * QW,
        moved=6 << 20,
    )


def head_back_kernel(
    behind_ref,
    parity_ref,
    qkv_ref,
    h1_ref,
    w_ref,
    full_ref,
    partial_ref,
    inverse_ref,
    prob_ref,
    cos_ref,
    sin_ref,
    *refs,
):
    xs, das, weights, results, outs = (refs[at * Z : at * Z + Z] for at in range(5))
    keep_ref, give_ref, dob, dqk, dqkv = refs[5 * Z :]
    total = jnp.zeros((Z * T, QW), F32)
    for hop in range(Z):
        columns = columns_of(behind_ref[hop])
        rows = jnp.concatenate([ref[:, columns] for ref in das], axis=0)
        total = total + mm_nt(rows, weights[hop][...])
        if hop == 0:
            own_columns = rows
    dob[...] = total.astype(BF16)
    for hop in range(Z):
        rows = slice(hop * T, (hop + 1) * T)
        for group in range(KH):
            key, value = head(qkv_ref, rows, QH + group), head(qkv_ref, rows, QH + KH + group)
            query = stack_heads(qkv_ref, rows, group * GROUP)
            out_grad = stack_heads(dob, rows, group * GROUP)
            probability = prob_ref[hop * KH + group]
            grad_prob = mm_nt(out_grad, value)
            held = jnp.sum(probability * grad_prob, axis=-1, keepdims=True)
            grad_scores = (probability * (grad_prob - held)).astype(BF16)
            grad_query = mm(grad_scores, key) * SCALE
            for index in range(GROUP):
                at = (group * GROUP + index) * HEAD_DIM
                dqk[rows, at : at + HEAD_DIM] = grad_query[index * T : (index + 1) * T]
            at = QW + group * HEAD_DIM
            dqk[rows, at : at + HEAD_DIM] = mm_tn(grad_scores, query) * SCALE
            dqkv[rows, at + KW : at + KW + HEAD_DIM] = mm_tn(
                probability.astype(BF16), out_grad
            ).astype(BF16)
    cosine = jnp.concatenate([cos_ref[...]] * Z, axis=0)
    signed = jnp.concatenate([sin_ref[...]] * Z, axis=0)
    dqkv[:, 0 : QW + KW] = rotate_back(dqk[...], cosine, signed).astype(BF16)
    even = parity_ref[0] == 0

    def store(grads, columns):
        pair = grads.astype(BF16).reshape(CHIPS, 2, ROWS, grads.shape[1])
        keep_ref[:, :, columns] = jnp.where(even, pair[:, 0], pair[:, 1])
        give_ref[:, :, columns] = jnp.where(even, pair[:, 1], pair[:, 0])

    store(mm_tn(full_ref[...], own_columns), slice(0, QW))
    store(mm_tn(h1_ref[...], dqkv[...]), slice(QW, MAIN))
    dh1 = mm_nt(dqkv[...], w_ref[:, :, QW:MAIN].reshape(D, QKV))
    lane = lax.broadcasted_iota(jnp.int32, (T, LANES), 1)
    first = (lane == E).astype(BF16)
    small = partial_ref[...]
    for hop in range(Z):
        rows = slice(hop * T, (hop + 1) * T)
        piece = dh1[rows]
        normed = xs[hop][...].astype(F32) * inverse_ref[rows]
        small += mm_tn((piece * normed).astype(BF16), first)
        outs[hop][:, 0:D] = piece.astype(BF16)
        outs[hop][:, D:] = results[hop][...]
    store(small, slice(MAIN, SLICE))


def head_back(behind, parity, qkv, h1, w, full, shadows, cosine, signed, xs, das, weights, results):
    return call(
        head_back_kernel,
        "head_back",
        [behind, parity, qkv, h1, w, full, *shadows, cosine, signed, *xs, *das, *weights, *results],
        [SCALARS] * 2 + [None] * 9 + [X_SPEC] * Z + [None] * (3 * Z),
        [shape((T, 2 * D), BF16)] * Z + [shape((CHIPS, ROWS, SLICE), BF16)] * 2,
        scratch=[
            pltpu.VMEM((Z * T, QW), BF16),
            pltpu.VMEM((Z * T, QW + KW), F32),
            pltpu.VMEM((Z * T, QKV), BF16),
        ],
        flops=4 * Z * T * D * QKV,
        moved=16 << 20,
    )


def token_grad_kernel(x_ref, gains_ref, dx1_ref, *refs):
    grad = refs[0][...].astype(F32)
    for hop in range(1, Z):
        grad = grad + refs[hop][...].astype(F32)
    normed, inverse = norm_of(x_ref[...].astype(F32))
    refs[Z][...] = dx1_ref[...] + norm_back(grad, normed, inverse, gains_ref[0:1, :])


def token_grad(x, gains, dx1, pieces):
    return call(
        token_grad_kernel,
        "token_grad",
        [x, gains, dx1, *pieces],
        [None] * 3 + [X_SPEC] * Z,
        [shape((T, D), F32)],
        flops=T * D * 16,
        moved=4 << 20,
    )[0]


def split_kernel(order_ref, keep_ref, got_ref, *outs):
    for chip in range(CHIPS):
        at = order_ref[chip]
        total = (keep_ref[at].astype(F32) + got_ref[at].astype(F32)).astype(BF16)
        outs[chip % 4][chip // 4] = total


def split(order, keep, got):
    return call(
        split_kernel,
        "split",
        [order, keep, got],
        [SCALARS, None, None],
        [shape((2, ROWS, SLICE), BF16)] * 4,
        flops=CHIPS * ROWS * SLICE,
        moved=6 << 20,
    )


def add_kernel(*refs):
    total = refs[0][...].astype(F32)
    for ref in refs[1:-1]:
        total = total + ref[...].astype(F32)
    refs[-1][...] = total.astype(BF16)


def add_all(parts, name):
    return call(
        add_kernel,
        name,
        list(parts),
        [None] * len(parts),
        [shape(parts[0].shape, BF16)],
        flops=parts[0].size * len(parts),
        moved=2 * parts[0].size * (len(parts) + 1),
    )[0]


def across_kernel(a_ref, b_ref, c_ref, d_ref, out_ref):
    here = a_ref[...].astype(F32) + b_ref[...].astype(F32)
    there = c_ref[...].astype(F32) + d_ref[...].astype(F32)
    out_ref[...] = (here + there).astype(BF16)


def sum_across(parts):
    return call(
        across_kernel,
        "sum_across",
        list(parts),
        [None] * 4,
        [shape((ROWS, SLICE), BF16)],
        flops=4 * ROWS * SLICE,
        moved=10 * ROWS * SLICE,
    )[0]


def finish_kernel(order_ref, *refs):
    parts, (q_ref, k_ref, v_ref, o_ref, small_ref, narrow) = refs[:Z], refs[Z:]
    for hop in range(Z):
        at = order_ref[hop]
        part = parts[hop][...].astype(F32)
        o_ref[:, columns_of(at)] = part[:, 0:QW]
        q_ref[:, columns_of(at)] = part[:, QW : 2 * QW]
        heads = pl.ds(pl.multiple_of(at * KW, KW), KW)
        k_ref[:, heads] = part[:, 2 * QW : 2 * QW + KW]
        v_ref[:, heads] = part[:, 2 * QW + KW : MAIN]
        narrow[at] = part[:, MAIN:]
    small_ref[...] = (narrow[0] + narrow[1] + narrow[2] + narrow[3]).T


def finish(order, parts):
    return call(
        finish_kernel,
        "finish",
        [order, *parts],
        [SCALARS] + [None] * Z,
        [
            shape((ROWS, D), F32),
            shape((ROWS, KEY_VALUE_HEADS * HEAD_DIM), F32),
            shape((ROWS, KEY_VALUE_HEADS * HEAD_DIM), F32),
            shape((ROWS, D), F32),
            shape((LANES, ROWS), F32),
        ],
        scratch=[pltpu.VMEM((Z, ROWS, LANES), F32)],
        flops=ROWS * SLICE * Z,
        moved=3 << 20,
    )


def unpack_kernel(share_ref, gate_ref, up_ref, down_ref):
    value = share_ref[0].astype(F32)
    gate_ref[0] = value[:, 0:H]
    up_ref[0] = value[:, H : 2 * H]
    down_ref[0] = value[:, 2 * H :]


def unpack(share):
    return pl.pallas_call(
        unpack_kernel,
        grid=(LOCAL,),
        in_specs=[per_expert(ROWS, 3 * H)],
        out_specs=[per_expert(ROWS, H)] * 3,
        out_shape=[shape((LOCAL, ROWS, H), F32)] * 3,
        compiler_params=params(),
        cost_estimate=cost(LOCAL * ROWS * 3 * H, 5 << 20),
        name="unpack",
    )(share)


def spread_tables(all_routes, me):
    lane = jnp.arange(LANES, dtype=jnp.int32)
    member = jnp.sum((all_routes[..., None] == lane).astype(F32), axis=2)
    mine = me * LOCAL + jnp.arange(LOCAL, dtype=jnp.int32)
    own = jnp.sum((all_routes[..., None] == mine).astype(F32), axis=2)
    earlier = (np.arange(T)[:, None] > np.arange(T)[None, :]).astype(np.float32)
    before = jnp.einsum(
        "ts,rse->rte", jnp.asarray(earlier, BF16), own.astype(BF16), preferred_element_type=F32
    )
    slots = jnp.where(own > 0.5, before.astype(jnp.int32), -1)
    slots = jnp.swapaxes(slots, 1, 2)[:, :, None, :]
    place = slots == jnp.arange(CAP, dtype=jnp.int32)[None, None, :, None]
    return member, place.astype(BF16).reshape(PEERS, SLOTS, T)


def body(
    tokens,
    cotangent,
    routes,
    norm_one,
    w_query,
    key_weight,
    value_weight,
    w_out,
    norm_two,
    w_router,
    w_gate,
    w_up,
    w_down,
):
    me = lax.axis_index("expert")
    place_in_group = lax.axis_index("fsdp")
    z = me % Z
    core = place_in_group % 2
    cosine, signed = (jnp.asarray(table) for table in rope_tables())

    own = pack(
        z.astype(jnp.int32)[None],
        w_out,
        w_query,
        key_weight,
        value_weight,
        w_router.T,
        norm_one[None, :],
        norm_two[None, :],
    )
    pair = jnp.stack([own, send_chip(own, LINE)])
    own = [send_chip(pair, hop) for hop in range(LINE)]
    other = [swap_core(value) for value in own]
    sources = jnp.stack([chip_at(place_in_group, hop, True) for hop in range(CHIPS)])
    order = jnp.concatenate([2 * sources + core, 2 * sources + 1 - core]).astype(jnp.int32)
    expert_pack = lax.all_gather(
        jnp.concatenate([w_gate, w_up, jnp.swapaxes(w_down, 1, 2)], axis=2),
        "fsdp",
        axis=1,
        tiled=True,
    )

    behind = jnp.stack([(z + Z - hop) % Z for hop in range(Z)]).astype(jnp.int32)
    ahead = jnp.stack([(z + hop) % Z for hop in range(Z)]).astype(jnp.int32)

    marks = jnp.pad(routes, ((0, 0), (0, LANES - TOPK))).astype(BF16)
    early = jnp.concatenate([cotangent, marks], axis=1)
    whole_row = jnp.concatenate([tokens, early], axis=1)
    xs = [send(whole_row, hop) for hop in (0, 1, 3)]
    xs.insert(2, send(after(whole_row, xs[1]), 2))
    w, gains, h1, qkv, ob = project(order, cosine, signed, own, other, xs)
    obs = [send(ob, hop) for hop in range(Z)]
    early_other = send(after(early, xs[3]), Z)
    early_other = after(early_other, *obs[1:])
    early_other = [send(early_other, hop) for hop in range(Z)]
    ob_full, *x1_columns = out_project(behind, w, obs)
    x1_pieces = [send(x1_columns[hop], hop, True) for hop in range(Z)]
    x1, h2 = residual(ahead, tokens, gains, x1_pieces)
    h2_other = send(h2, Z)
    h2_line = [send(h2, hop) for hop in range(Z)]
    h2_other = [send(h2_other, hop) for hop in range(Z)]

    all_routes = jnp.stack(
        [r[:, 2 * D : 2 * D + TOPK].astype(jnp.int32) for r in xs]
        + [r[:, D : D + TOPK].astype(jnp.int32) for r in early_other]
    )
    member, place = spread_tables(all_routes, me)
    row_expert = me * LOCAL + jnp.arange(SLOTS, dtype=jnp.int32) // CAP
    chosen = (row_expert[:, None] == jnp.arange(LANES, dtype=jnp.int32)[None, :]).astype(F32)
    dyr = spread_rows(place, xs, early_other)

    gates, gate0, b0 = gate_rows(0, w, member, chosen, place, h2_line)
    _, gate1, b1 = gate_rows(1, w, member, chosen, place, h2_other)
    b, slot_gate = (b0, b1), (gate0, gate1)
    weights = after(cut_out(ahead, after(w, x1)), b1)
    slot_gate = after(slot_gate, *weights)
    weights = [send(weights[hop], hop) for hop in range(Z)]
    gy, db, grad_pack = experts(me.astype(jnp.int32)[None], b, dyr, slot_gate, expert_pack)
    db_parts = collect(place, after(db, *weights[1:]), "collect_grads")
    grad_cross = [send(db_parts[Z + hop], hop, True) for hop in range(Z)]
    grad_line = after(db_parts[:Z], *grad_cross[1:])
    grad_line = [send(grad_line[hop], hop, True) for hop in range(Z)]
    grad_other = send(add_all(grad_cross, "line_grads"), Z)
    expert_share = lax.psum_scatter(
        after(grad_pack, *weights[1:]), "fsdp", scatter_dimension=1, tiled=True
    )
    results = collect(place, gy, "collect_results")
    grad_line = after(grad_line, results)
    dx1, dlogits, scaled, da = token_back(x1, cotangent, gates, w, gains, [*grad_line, grad_other])
    das = [send(da, hop) for hop in range(Z)]
    shadows = shadow(qkv, h2, dlogits, scaled, xs)
    results = after(results, *das[1:])
    results_cross = [send(results[Z + hop], hop, True) for hop in range(Z)]
    *returns, keep, give = head_back(
        behind,
        core.astype(jnp.int32)[None],
        qkv,
        h1,
        w,
        ob_full,
        shadows,
        cosine,
        signed,
        xs,
        das,
        weights,
        results[:Z],
    )
    dests = jnp.stack([chip_at(place_in_group, hop) for hop in range(CHIPS)]).astype(jnp.int32)
    parts = split(dests, keep, swap_core(after(give, *results_cross[1:])))
    lines = [send_chip(parts[hop], hop) for hop in range(LINE)]
    results_other = send(add_all(results_cross, "line_results"), Z)
    first, third = send(returns[1], 1, True), send(returns[3], 3, True)
    lines[0] = after(lines[0], first, third)
    second = send(after(returns[2], first, third), 2, True)
    returns = [returns[0], first, second, third]
    share = add_all(lines, "sum_lines")
    share = sum_across([share[0], *send_across(share)])
    share = after(share, second)
    shares = [send(share, hop) for hop in range(Z)]
    grad_gate, grad_up, grad_down = unpack(expert_share)
    grad_tokens = token_grad(tokens, gains, dx1, returns)
    mixed_out = mix(x1, returns, results_other)
    shares = after(shares, grad_tokens, mixed_out, grad_gate)
    grad_query, grad_key, grad_value, grad_out, narrow = finish(behind, shares)

    return (
        mixed_out,
        grad_tokens,
        narrow[E],
        grad_query,
        grad_key,
        grad_value,
        grad_out,
        narrow[E + 1],
        narrow[0:E].T,
        grad_gate,
        grad_up,
        jnp.swapaxes(grad_down, 1, 2),
    )


def solution(mesh):
    return jax.shard_map(
        body,
        mesh=mesh,
        in_specs=(
            P(("expert", "fsdp"), None),
            P(("expert", "fsdp"), None),
            P(("expert", "fsdp"), None),
            P("fsdp"),
            P("fsdp", None),
            P("fsdp", None),
            P("fsdp", None),
            P("fsdp", None),
            P("fsdp"),
            P("fsdp", None),
            P("expert", "fsdp", None),
            P("expert", "fsdp", None),
            P("expert", None, "fsdp"),
        ),
        out_specs=(
            P(("expert", "fsdp"), None),
            P(("expert", "fsdp"), None),
            P("fsdp"),
            P("fsdp", None),
            P("fsdp", None),
            P("fsdp", None),
            P("fsdp", None),
            P("fsdp"),
            P("fsdp", None),
            P("expert", "fsdp", None),
            P("expert", "fsdp", None),
            P("expert", None, "fsdp"),
        ),
        check_vma=False,
    )
```

time: 685 us -> 432 us (0.63)
  waiting for transfers between devices: 425 us -> 184 us
  starting transfers between devices: 101 us -> 74.6 us
  Pallas kernels: 100 us -> 125 us
  local copies, waits for them, and re-layouts: 25.8 us -> 15.2 us
    reduce_scatter x2 -> x1, waiting for transfers between devices: 158 us -> 0.01 us  [body(): lax.psum_scatter(after(grad_pack, *weights[1:]), 'fsdp', scatter_dimensio...]
    ppermute x42 -> x43, waiting for transfers between devices: 185 us -> 103 us  [send(): lax.ppermute(value, 'expert', [(i, peer(i, hop, back)) for i in range(PEE...]
    ppermute x0 -> x15, waiting for transfers between devices: none -> 80.8 us  [the longest x7 73.5 us: send_chip(): return lax.ppermute(value, 'fsdp', pairs)]
    all_gather x1, waiting for transfers between devices: 55.3 us -> 0.01 us  [body(): lax.all_gather(jnp.concatenate([w_gate, w_up, jnp.swapaxes(w_down, 1, 2)]...]
    ppermute x42 -> x43, starting transfers between devices: 101 us -> 58.4 us  [send(): lax.ppermute(value, 'expert', [(i, peer(i, hop, back)) for i in range(PEE...]
    all_gather x1 -> x0, waiting for transfers between devices: 26.1 us -> none  [body(): lax.all_gather(jnp.concatenate([w_query, key_weight, value_weight, w_out,...]
    pallas_call x8 -> x23, Pallas kernels: 100 us -> 125 us  [the longest x20 90.8 us: call(): pl.pallas_call(kernel, grid=(1,), in_specs=in_specs, out_specs=out_specs,...]
    ppermute x0 -> x15, starting transfers between devices: none -> 16.2 us  [the longest x7 10.8 us: send_chip(): return lax.ppermute(value, 'fsdp', pairs)]
  transfers between devices with their start and end apart: 46 -> 60, of which waited for: 21 -> 29; matrix products, arithmetic and copies ran while one was open for 3% -> 3% of each run, Pallas kernels for 6% -> 29%
where the time goes in v2:
time: 432 us; the launch traced here: 424 us
  waiting for transfers between devices  184 us (43%)
  Pallas kernels  125 us (29%)
  starting transfers between devices  74.6 us (17%)
  local copies, waits for them, and re-layouts  15.2 us (4%)
  between operations  15 us (3%)
  other arithmetic  9.75 us (2%)
    ppermute x43, waiting for transfers between devices, send(): lax.ppermute(value, 'expert', [(i, peer(i, hop, back)) for i in range(PEE...  103 us
    pallas_call x20, Pallas kernels, call(): pl.pallas_call(kernel, grid=(1,), in_specs=in_specs, out_specs=out_specs,...  90.8 us
    ppermute x7, waiting for transfers between devices, send_chip(): return lax.ppermute(value, 'fsdp', pairs)  73.5 us
    ppermute x43, starting transfers between devices, send(): lax.ppermute(value, 'expert', [(i, peer(i, hop, back)) for i in range(PEE...  58.4 us
    pallas_call x1, Pallas kernels, experts(): pl.pallas_call(expert_kernel, grid=(LOCAL,), in_specs=[SCALARS, per_exper...  27.9 us
    ppermute x7, starting transfers between devices, send_chip(): return lax.ppermute(value, 'fsdp', pairs)  10.8 us
  transfers between devices with their start and end apart: 60, of which 29 were waited for; matrix products, arithmetic and copies ran while one was open for 3% of the time, Pallas kernels for 29%

profile of v2, /device:TPU:0, one launch (start us, length us, event | category | flops | bytes accessed | tf_op | source)
XLA Modules:
  0.0 423.7 jit_solution(15872443245272749001)
XLA Ops:
  7.3 2.7 pad_maximum_fusion
  10.2 4.2 collective-permute-start.10
  19.2 4.6 %collective-permute-done = bf16[96,1152]{1,0:T(8,128)(2,1)S(1)} collective-permute-done((bf16[96,1152]{1,0:T(8,128)(2,1)}, bf16[96,1152]{1,0:T(8,128)(2,1)S(1)}, u32[]{:S(2)}, u32[]{:S(2)}) %collective-permute-start) | collective-permute-done | bytes 221216 | tf_op jit(solution)/shard_map/ppermute | solution.py:67
  24.8 3.2 collective-permute-start.3
  29.6 5.8 %collective-permute-done.8.refs_9_.refs_1_ = bf16[128,3200]{1,0:T(8,128)(2,1)} collective-permute-done((bf16[128,3200]{1,0:T(8,128)(2,1)S(1)}, bf16[128,3200]{1,0:T(8,128)(2,1)}, u32[]{:S(2)}, u32[]{:S(2)}) %collective-permute-start.8) | collective-permute-done | bytes 819232 | tf_op jit(solution)/shard_map/ppermute | solution.py:54
  36.2 11.3 %collective-permute-done.3.refs_3_ = bf16[2,96,1152]{2,1,0:T(8,128)(2,1)} collective-permute-done((bf16[2,96,1152]{2,1,0:T(8,128)(2,1)S(1)}, bf16[2,96,1152]{2,1,0:T(8,128)(2,1)}, u32[]{:S(2)}, u32[]{:S(2)}) %collective-permute-start.3) | collective-permute-done | bytes 442400 | tf_op jit(solution)/shard_map/ppermute | solution.py:67
  47.5 4.6 %collective-permute-done.2.refs_2_ = bf16[2,96,1152]{2,1,0:T(8,128)(2,1)} collective-permute-done((bf16[2,96,1152]{2,1,0:T(8,128)(2,1)S(1)}, bf16[2,96,1152]{2,1,0:T(8,128)(2,1)}, u32[]{:S(2)}, u32[]{:S(2)}) %collective-permute-start.2) | collective-permute-done | bytes 442400 | tf_op jit(solution)/shard_map/ppermute | solution.py:67
  52.1 14.0 %collective-permute-done.1.refs_1_ = bf16[2,96,1152]{2,1,0:T(8,128)(2,1)} collective-permute-done((bf16[2,96,1152]{2,1,0:T(8,128)(2,1)S(1)}, bf16[2,96,1152]{2,1,0:T(8,128)(2,1)}, u32[]{:S(2)}, u32[]{:S(2)}) %collective-permute-start.1) | collective-permute-done | bytes 442400 | tf_op jit(solution)/shard_map/ppermute | solution.py:67
  67.6 3.1 collective-permute-start.17
  70.7 8.6 %project.1 = (bf16[16,96,1152]{2,1,0:T(8,128)(2,1)}, f32[16,1536]{1,0:T(8,128)}, bf16[512,1536]{1,0:T(8,128)(2,1)}, bf16[512,640]{1,0:T(8,128)(2,1)}, bf16[512,384]{1,0:T(8,128)(2,1)}) custom-call(s32[16]{0:T(128)} %pad_add_fusion.1.order_ref, f32[128,128]{1,0:T(8,128)} %constant.297.clone.cos_ref, f32[128,128]{1,0:T(8,128)} %constant.298.clone.sin_ref, ...), custom_call_target="tpu_custom_call" | custom-call | flops 60397977600 | bytes 754974720 | tf_op jit(solution)/shard_map/project/pallas_call | solution.py:187
  79.3 2.9 collective-permute-start.13
  83.9 6.6 %collective-permute-done.17.refs_4_ = bf16[128,1664]{1,0:T(8,128)(2,1)S(1)} collective-permute-done((bf16[128,1664]{1,0:T(8,128)(2,1)S(1)}, bf16[128,1664]{1,0:T(8,128)(2,1)S(1)}, u32[]{:S(2)}, u32[]{:S(2)}) %collective-permute-start.17) | collective-permute-done | bytes 426016 | tf_op jit(solution)/shard_map/ppermute | solution.py:54
  90.5 8.7 %collective-permute-done.13.refs_3_ = bf16[512,384]{1,0:T(8,128)(2,1)S(1)} collective-permute-done((bf16[512,384]{1,0:T(8,128)(2,1)}, bf16[512,384]{1,0:T(8,128)(2,1)S(1)}, u32[]{:S(2)}, u32[]{:S(2)}) %collective-permute-start.13) | collective-permute-done | bytes 393248 | tf_op jit(solution)/shard_map/ppermute | solution.py:54
  99.3 3.3 collective-permute-done.11.refs_1_
  104.2 3.9 out_project.1
  108.2 3.5 collective-permute-start.14
  112.9 13.4 %collective-permute-done.14.refs_1_ = bf16[128,384]{1,0:T(8,128)(2,1)S(1)} collective-permute-done((bf16[128,384]{1,0:T(8,128)(2,1)}, bf16[128,384]{1,0:T(8,128)(2,1)S(1)}, u32[]{:S(2)}, u32[]{:S(2)}) %collective-permute-start.14) | collective-permute-done | bytes 98336 | tf_op jit(solution)/shard_map/ppermute | solution.py:54
  131.4 3.6 collective-permute-start.23
  135.0 2.5 cut_out.1
  139.9 5.0 %spread_rows.1 = bf16[5,8,32,1536]{3,2,1,0:T(8,128)(2,1)} custom-call(bf16[8,160,128]{2,1,0:T(8,128)(2,1)} %fusion.1.place_ref, bf16[128,3200]{1,0:T(8,128)(2,1)} %copy-done.7, bf16[128,3200]{1,0:T(8,128)(2,1)} %collective-permute-done.8.refs_9_.refs_1_, bf16[128,3200]{1,0:T(8,128)(2,1)} %collective-permute-done.9.refs_10_.refs_2_, ...), custom_call_target="tpu_custom_call" | custom-call | flops 30198988800 | bytes 503316480 | tf_op jit(solution)/shard_map/spread_rows/pallas_call | solution.py:187
  147.5 2.8 collective-permute-done.24.refs_0_
  150.4 3.9 collective-permute-start.27
  157.3 5.4 %gate_rows.2 = (f32[4,128,128]{2,1,0:T(8,128)}, f32[5,4,32,1]{3,2,1,0:T(8,128)}, bf16[5,4,32,1536]{3,2,1,0:T(8,128)(2,1)}) custom-call(bf16[16,96,1152]{2,1,0:T(8,128)(2,1)} %get-tuple-element.133.w_ref.small_ref, f32[8,128,128]{2,1,0:T(8,128)} %convert_reduce_fusion.member_ref, f32[160,128]{1,0:T(8,128)} %fusion.2.chosen_ref, ...), custom_call_target="tpu_custom_call" | custom-call | flops 15099494400 | bytes 314572800 | tf_op jit(solution)/shard_map/gate_rows/pallas_call | solution.py:187
  162.7 6.3 %collective-permute-done.27.refs_3_ = bf16[128,1536]{1,0:T(8,128)(2,1)S(1)} collective-permute-done((bf16[128,1536]{1,0:T(8,128)(2,1)S(1)}, bf16[128,1536]{1,0:T(8,128)(2,1)S(1)}, u32[]{:S(2)}, u32[]{:S(2)}) %collective-permute-start.27) | collective-permute-done | bytes 393248 | tf_op jit(solution)/shard_map/ppermute | solution.py:54
  169.0 4.3 %collective-permute-done.25.refs_1_ = bf16[128,1536]{1,0:T(8,128)(2,1)S(1)} collective-permute-done((bf16[128,1536]{1,0:T(8,128)(2,1)S(1)}, bf16[128,1536]{1,0:T(8,128)(2,1)S(1)}, u32[]{:S(2)}, u32[]{:S(2)}) %collective-permute-start.25) | collective-permute-done | bytes 393248 | tf_op jit(solution)/shard_map/ppermute | solution.py:54
  174.1 5.4 %gate_rows.3 = (f32[4,128,128]{2,1,0:T(8,128)}, f32[5,4,32,1]{3,2,1,0:T(8,128)}, bf16[5,4,32,1536]{3,2,1,0:T(8,128)(2,1)}) custom-call(bf16[16,96,1152]{2,1,0:T(8,128)(2,1)} %get-tuple-element.133.w_ref.small_ref, f32[8,128,128]{2,1,0:T(8,128)} %convert_reduce_fusion.member_ref, f32[160,128]{1,0:T(8,128)} %fusion.2.chosen_ref, ...), custom_call_target="tpu_custom_call" | custom-call | flops 15099494400 | bytes 314572800 | tf_op jit(solution)/shard_map/gate_rows/pallas_call | solution.py:187
  182.9 27.9 %experts.1 = (bf16[5,256,1536]{2,1,0:T(8,128)(2,1)}, bf16[5,256,1664]{2,1,0:T(8,128)(2,1)}, bf16[5,1536,1536]{2,1,0:T(8,128)(2,1)}) custom-call(s32[1]{0:T(128)} %bitcast.31.me_ref, bf16[5,128,1536]{2,1,0:T(8,128)(2,1)} %bitcast.76, bf16[5,128,1536]{2,1,0:T(8,128)(2,1)} %bitcast.77, bf16[5,256,1536]{2,1,0:T(8,128)(2,1)} %bitcast.75, f32[5,128,1]{2,1,0:T(8,128)} %bitcast.78, ...), custom_call_target="tpu_custom_call" | custom-call | flops 1087163596800 | bytes 3774873600 | tf_op jit(solution)/shard_map/experts/pallas_call | solution.py:457
  210.8 4.4 %collect_grads.1 = (bf16[128,1664]{1,0:T(8,128)(2,1)}, bf16[128,1664]{1,0:T(8,128)(2,1)}, bf16[128,1664]{1,0:T(8,128)(2,1)}, bf16[128,1664]{1,0:T(8,128)(2,1)}, ...) custom-call(bf16[8,160,128]{2,1,0:T(8,128)(2,1)} %fusion.1.place_ref, ...), custom_call_target="tpu_custom_call" | custom-call | flops 32715571200 | bytes 503316480 | tf_op jit(solution)/shard_map/collect_grads/pallas_call | solution.py:187
  219.6 8.6 %collective-permute-done.31.refs_1_ = bf16[128,1664]{1,0:T(8,128)(2,1)S(1)} collective-permute-done((bf16[128,1664]{1,0:T(8,128)(2,1)}, bf16[128,1664]{1,0:T(8,128)(2,1)S(1)}, u32[]{:S(2)}, u32[]{:S(2)}) %collective-permute-start.31) | collective-permute-done | bytes 426016 | tf_op jit(solution)/shard_map/ppermute | solution.py:54
  230.6 7.1 %collective-permute-done.33.refs_3_ = bf16[128,1664]{1,0:T(8,128)(2,1)S(1)} collective-permute-done((bf16[128,1664]{1,0:T(8,128)(2,1)}, bf16[128,1664]{1,0:T(8,128)(2,1)S(1)}, u32[]{:S(2)}, u32[]{:S(2)}) %collective-permute-start.33) | collective-permute-done | bytes 426016 | tf_op jit(solution)/shard_map/ppermute | solution.py:54
  244.9 4.3 %collect_results.1 = (bf16[128,1536]{1,0:T(8,128)(2,1)}, bf16[128,1536]{1,0:T(8,128)(2,1)}, bf16[128,1536]{1,0:T(8,128)(2,1)}, bf16[128,1536]{1,0:T(8,128)(2,1)}...) custom-call(bf16[8,160,128]{2,1,0:T(8,128)(2,1)} %fusion.1.place_ref, ...), custom_call_target="tpu_custom_call" | custom-call | flops 30198988800 | bytes 503316480 | tf_op jit(solution)/shard_map/collect_results/pallas_call | solution.py:187
  252.9 7.5 %collective-permute-done.36.refs_3_ = bf16[128,1664]{1,0:T(8,128)(2,1)S(1)} collective-permute-done((bf16[128,1664]{1,0:T(8,128)(2,1)}, bf16[128,1664]{1,0:T(8,128)(2,1)S(1)}, u32[]{:S(2)}, u32[]{:S(2)}) %collective-permute-start.36) | collective-permute-done | bytes 426016 | tf_op jit(solution)/shard_map/ppermute | solution.py:54
  262.2 3.9 token_back.1
  270.9 6.1 %shadow.1 = (f32[1536,128]{1,0:T(8,128)}, f32[512,1]{1,0:T(8,128)}, f32[8,384,128]{2,1,0:T(8,128)}) custom-call(bf16[512,640]{1,0:T(8,128)(2,1)} %get-tuple-element.122.qkv_ref, bf16[128,1536]{1,0:T(8,128)(2,1)} %get-tuple-element.125.refs_0_.h2_ref, bf16[128,128]{1,0:T(8,128)(2,1)} %get-tuple-element.171.dlogits_ref, ...), custom_call_target="tpu_custom_call" | custom-call | flops 18119393280 | bytes 377487360 | tf_op jit(solution)/shard_map/shadow/pallas_call | solution.py:187
  278.3 4.0 collective-permute-done.39.refs_6_
  282.3 4.6 %collective-permute-done.38.refs_5_ = bf16[128,1536]{1,0:T(8,128)(2,1)S(1)} collective-permute-done((bf16[128,1536]{1,0:T(8,128)(2,1)}, bf16[128,1536]{1,0:T(8,128)(2,1)S(1)}, u32[]{:S(2)}, u32[]{:S(2)}) %collective-permute-start.38) | collective-permute-done | bytes 393248 | tf_op jit(solution)/shard_map/ppermute | solution.py:54
  290.2 17.8 %head_back.1 = (bf16[128,3072]{1,0:T(8,128)(2,1)}, bf16[128,3072]{1,0:T(8,128)(2,1)}, bf16[128,3072]{1,0:T(8,128)(2,1)}, bf16[128,3072]{1,0:T(8,128)(2,1)}, bf16...) custom-call(s32[4]{0:T(128)} %pad_add_fusion.2.peers_ref.behind_ref.order_ref, s32[1]{0:T(128)} %bitcast.19.parity_ref, ...), custom_call_target="tpu_custom_call" | custom-call | flops 120795955200 | bytes 1006632960 | tf_op jit(solution)/shard_map/head_back/pallas_call | solution.py:187
  309.0 2.6 collective-permute-start.41
  313.7 3.5 split.1
  318.7 3.6 collective-permute-start.50
  322.3 6.3 %collective-permute-done.41.refs_2_.refs_1_ = bf16[128,3072]{1,0:T(8,128)(2,1)S(1)} collective-permute-done((bf16[128,3072]{1,0:T(8,128)(2,1)}, bf16[128,3072]{1,0:T(8,128)(2,1)S(1)}, u32[]{:S(2)}, u32[]{:S(2)}) %collective-permute-start.41) | collective-permute-done | bytes 786464 | tf_op jit(solution)/shard_map/ppermute | solution.py:54
  328.6 3.5 collective-permute-done.42.refs_4_.refs_3_
  332.1 38.9 %collective-permute-done.49.refs_1_ = bf16[2,96,1152]{2,1,0:T(8,128)(2,1)S(1)} collective-permute-done((bf16[2,96,1152]{2,1,0:T(8,128)(2,1)}, bf16[2,96,1152]{2,1,0:T(8,128)(2,1)S(1)}, u32[]{:S(2)}, u32[]{:S(2)}) %collective-permute-start.49) | collective-permute-done | bytes 442400 | tf_op jit(solution)/shard_map/ppermute | solution.py:67
  386.7 5.3 %collective-permute-done.53.c_ref = bf16[96,1152]{1,0:T(8,128)(2,1)S(1)} collective-permute-done((bf16[96,1152]{1,0:T(8,128)(2,1)S(1)}, bf16[96,1152]{1,0:T(8,128)(2,1)S(1)}, u32[]{:S(2)}, u32[]{:S(2)}) %collective-permute-start.53) | collective-permute-done | bytes 221216 | tf_op jit(solution)/shard_map/ppermute | solution.py:80
  394.8 2.9 collective-permute-start.57
  400.1 2.9 mix.1
  403.0 3.2 token_grad.1
  406.2 4.3 %unpack.1 = (f32[5,96,512]{2,1,0:T(8,128)}, f32[5,96,512]{2,1,0:T(8,128)}, f32[5,96,512]{2,1,0:T(8,128)}) custom-call(bf16[5,96,1536]{2,1,0:T(8,128)(2,1)} %reduce-scatter.2.cloned.1.call-done.share_ref), custom_call_target="tpu_custom_call" | custom-call | flops 44236800 | bytes 314572800 | tf_op jit(solution)/shard_map/unpack/pallas_call | solution.py:793
  (257 shorter events, 91.8 us)
Async XLA Ops:
  7.2 175.7 %all-gather.2.cloned.1.call-start = ((), (), s32[]{:S(2)}) async-start(), calls=%async_computation.1 | async-start | bytes 25067520 | tf_op jit(solution)/shard_map/all_gather | solution.py:856
  9.9 396.2 %reduce-scatter.2.cloned.1.call-start = ((), (), s32[]{:S(2)}) async-start(), calls=%async_computation.2 | async-start | bytes 25067520 | tf_op jit(solution)/shard_map/reduce_scatter | solution.py:904
  10.2 55.9 %collective-permute-start.10 = (bf16[128,3200]{1,0:T(8,128)(2,1)S(1)}, bf16[128,3200]{1,0:T(8,128)(2,1)S(1)}, u32[]{:S(2)}, u32[]{:S(2)}) collective-permute-start(bf16[128,3200]{1,0:T(8,128)(2,1)S(1)} %pad_maximum_fusion.1.refs_8_.refs_0_), channel_id=1, source_target_pairs={{0,48},{16,0},{32,16},{48,32},{64,112},{80,64},{96,80},{112,96},{1... | collective-permute-start | bytes 2457608 | tf_op jit(solution)/shard_map/ppermute | solution.py:54
  14.4 21.0 %collective-permute-start.8 = (bf16[128,3200]{1,0:T(8,128)(2,1)S(1)}, bf16[128,3200]{1,0:T(8,128)(2,1)}, u32[]{:S(2)}, u32[]{:S(2)}) collective-permute-start(bf16[128,3200]{1,0:T(8,128)(2,1)S(1)} %pad_maximum_fusion.1.refs_8_.refs_0_), channel_id=1, source_target_pairs={{0,16},{16,32},{32,48},{48,0},{64,80},{80,96},{96,112},{112,64},{1... | collective-permute-start | bytes 2457608 | tf_op jit(solution)/shard_map/ppermute | solution.py:54
  24.8 22.7 %collective-permute-start.3 = (bf16[2,96,1152]{2,1,0:T(8,128)(2,1)S(1)}, bf16[2,96,1152]{2,1,0:T(8,128)(2,1)}, u32[]{:S(2)}, u32[]{:S(2)}) collective-permute-start(bf16[2,96,1152]{2,1,0:T(8,128)(2,1)S(1)} %pad_maximum_fusion.2.refs_0_), channel_id=1, source_target_pairs={{0,6},{1,7},{2,0},{3,1},{4,2},{5,3},{6,4},{7,5},{8,14},{9,15},{10,... | collective-permute-start | bytes 1327112 | tf_op jit(solution)/shard_map/ppermute | solution.py:67
  28.0 24.1 %collective-permute-start.2 = (bf16[2,96,1152]{2,1,0:T(8,128)(2,1)S(1)}, bf16[2,96,1152]{2,1,0:T(8,128)(2,1)}, u32[]{:S(2)}, u32[]{:S(2)}) collective-permute-start(bf16[2,96,1152]{2,1,0:T(8,128)(2,1)S(1)} %pad_maximum_fusion.2.refs_0_), channel_id=1, source_target_pairs={{0,4},{1,5},{2,6},{3,7},{4,0},{5,1},{6,2},{7,3},{8,12},{9,13},{10,... | collective-permute-start | bytes 1327112 | tf_op jit(solution)/shard_map/ppermute | solution.py:67
  28.0 38.1 %collective-permute-start.1 = (bf16[2,96,1152]{2,1,0:T(8,128)(2,1)S(1)}, bf16[2,96,1152]{2,1,0:T(8,128)(2,1)}, u32[]{:S(2)}, u32[]{:S(2)}) collective-permute-start(bf16[2,96,1152]{2,1,0:T(8,128)(2,1)S(1)} %pad_maximum_fusion.2.refs_0_), channel_id=1, source_target_pairs={{0,2},{1,3},{2,4},{3,5},{4,6},{5,7},{6,0},{7,1},{8,10},{9,11},{10,... | collective-permute-start | bytes 1327112 | tf_op jit(solution)/shard_map/ppermute | solution.py:67
  35.4 35.2 %collective-permute-start.9 = (bf16[128,3200]{1,0:T(8,128)(2,1)S(1)}, bf16[128,3200]{1,0:T(8,128)(2,1)}, u32[]{:S(2)}, u32[]{:S(2)}) collective-permute-start(bf16[128,3200]{1,0:T(8,128)(2,1)S(1)} %pad_maximum_fusion.1.refs_8_.refs_0_), channel_id=1, source_target_pairs={{0,32},{16,48},{32,0},{48,16},{64,96},{80,112},{96,64},{112,80},{1... | collective-permute-start | bytes 2457608 | tf_op jit(solution)/shard_map/ppermute | solution.py:54
  47.5 20.1 %collective-permute-start.4 = (bf16[2,96,1152]{2,1,0:T(8,128)(2,1)S(1)}, bf16[2,96,1152]{2,1,0:T(8,128)(2,1)}, u32[]{:S(2)}, u32[]{:S(2)}) collective-permute-start(bf16[2,96,1152]{2,1,0:T(8,128)(2,1)S(1)} %pad_maximum_fusion.2.refs_0_), channel_id=1, source_target_pairs={{0,1},{1,0},{2,3},{3,2},{4,5},{5,4},{6,7},{7,6},{8,9},{9,8},{10,11... | collective-permute-start | bytes 1327112 | tf_op jit(solution)/shard_map/ppermute | solution.py:86
  52.1 18.5 %collective-permute-start.7 = (bf16[2,96,1152]{2,1,0:T(8,128)(2,1)}, bf16[2,96,1152]{2,1,0:T(8,128)(2,1)}, u32[]{:S(2)}, u32[]{:S(2)}) collective-permute-start(bf16[2,96,1152]{2,1,0:T(8,128)(2,1)} %collective-permute-done.3.refs_3_), channel_id=1, source_target_pairs={{0,1},{1,0},{2,3},{3,2},{4,5},{5,4},{6,7},{7,6},{8,9},{9,8},{10,11... | collective-permute-start | bytes 1327112 | tf_op jit(solution)/shard_map/ppermute | solution.py:86
  67.6 22.9 %collective-permute-start.17 = (bf16[128,1664]{1,0:T(8,128)(2,1)S(1)}, bf16[128,1664]{1,0:T(8,128)(2,1)S(1)}, u32[]{:S(2)}, u32[]{:S(2)}) collective-permute-start(bf16[128,1664]{1,0:T(8,128)(2,1)S(1)} %pad_maximum_fusion.3), channel_id=1, source_target_pairs={{0,64},{16,80},{32,96},{48,112},{64,0},{80,16},{96,32},{112,48},{1... | collective-permute-start | bytes 1277960 | tf_op jit(solution)/shard_map/ppermute | solution.py:54
  79.3 20.0 %collective-permute-start.13 = (bf16[512,384]{1,0:T(8,128)(2,1)}, bf16[512,384]{1,0:T(8,128)(2,1)S(1)}, u32[]{:S(2)}, u32[]{:S(2)}) collective-permute-start(bf16[512,384]{1,0:T(8,128)(2,1)} %get-tuple-element.116.refs_0_), channel_id=1, source_target_pairs={{0,48},{16,0},{32,16},{48,32},{64,112},{80,64},{96,80},{112,96},{1... | collective-permute-start | bytes 1179656 | tf_op jit(solution)/shard_map/ppermute | solution.py:54
  82.1 17.1 %collective-permute-start.12 = (bf16[512,384]{1,0:T(8,128)(2,1)}, bf16[512,384]{1,0:T(8,128)(2,1)S(1)}, u32[]{:S(2)}, u32[]{:S(2)}) collective-permute-start(bf16[512,384]{1,0:T(8,128)(2,1)} %get-tuple-element.116.refs_0_), channel_id=1, source_target_pairs={{0,32},{16,48},{32,0},{48,16},{64,96},{80,112},{96,64},{112,80},{1... | collective-permute-start | bytes 1179656 | tf_op jit(solution)/shard_map/ppermute | solution.py:54
  82.1 20.4 %collective-permute-start.11 = (bf16[512,384]{1,0:T(8,128)(2,1)}, bf16[512,384]{1,0:T(8,128)(2,1)S(1)}, u32[]{:S(2)}, u32[]{:S(2)}) collective-permute-start(bf16[512,384]{1,0:T(8,128)(2,1)} %get-tuple-element.116.refs_0_), channel_id=1, source_target_pairs={{0,16},{16,32},{32,48},{48,0},{64,80},{80,96},{96,112},{112,64},{1... | collective-permute-start | bytes 1179656 | tf_op jit(solution)/shard_map/ppermute | solution.py:54
  102.6 34.9 %collective-permute-start.20 = (bf16[128,1664]{1,0:T(8,128)(2,1)S(1)}, bf16[128,1664]{1,0:T(8,128)(2,1)S(1)}, u32[]{:S(2)}, u32[]{:S(2)}) collective-permute-start(bf16[128,1664]{1,0:T(8,128)(2,1)S(1)} %collective-permute-done.17.refs_4_), channel_id=1, source_target_pairs={{0,48},{16,0},{32,16},{48,32},{64,112},{80,64},{96,80},{112,96},{1... | collective-permute-start | bytes 1277960 | tf_op jit(solution)/shard_map/ppermute | solution.py:54
  103.5 34.2 %collective-permute-start.19 = (bf16[128,1664]{1,0:T(8,128)(2,1)S(1)}, bf16[128,1664]{1,0:T(8,128)(2,1)S(1)}, u32[]{:S(2)}, u32[]{:S(2)}) collective-permute-start(bf16[128,1664]{1,0:T(8,128)(2,1)S(1)} %collective-permute-done.17.refs_4_), channel_id=1, source_target_pairs={{0,32},{16,48},{32,0},{48,16},{64,96},{80,112},{96,64},{112,80},{1... | collective-permute-start | bytes 1277960 | tf_op jit(solution)/shard_map/ppermute | solution.py:54
  108.2 18.1 %collective-permute-start.14 = (bf16[128,384]{1,0:T(8,128)(2,1)}, bf16[128,384]{1,0:T(8,128)(2,1)S(1)}, u32[]{:S(2)}, u32[]{:S(2)}) collective-permute-start(bf16[128,384]{1,0:T(8,128)(2,1)} %get-tuple-element.118), channel_id=1, source_target_pairs={{0,48},{16,0},{32,16},{48,32},{64,112},{80,64},{96,80},{112,96},{1... | collective-permute-start | bytes 294920 | tf_op jit(solution)/shard_map/ppermute | solution.py:54
  111.7 14.6 %collective-permute-start.15 = (bf16[128,384]{1,0:T(8,128)(2,1)}, bf16[128,384]{1,0:T(8,128)(2,1)S(1)}, u32[]{:S(2)}, u32[]{:S(2)}) collective-permute-start(bf16[128,384]{1,0:T(8,128)(2,1)} %get-tuple-element.119), channel_id=1, source_target_pairs={{0,32},{16,48},{32,0},{48,16},{64,96},{80,112},{96,64},{112,80},{1... | collective-permute-start | bytes 294920 | tf_op jit(solution)/shard_map/ppermute | solution.py:54
  111.8 14.6 %collective-permute-start.16 = (bf16[128,384]{1,0:T(8,128)(2,1)}, bf16[128,384]{1,0:T(8,128)(2,1)S(1)}, u32[]{:S(2)}, u32[]{:S(2)}) collective-permute-start(bf16[128,384]{1,0:T(8,128)(2,1)} %get-tuple-element.120), channel_id=1, source_target_pairs={{0,16},{16,32},{32,48},{48,0},{64,80},{80,96},{96,112},{112,64},{1... | collective-permute-start | bytes 294920 | tf_op jit(solution)/shard_map/ppermute | solution.py:54
  129.3 21.0 %collective-permute-start.24 = (bf16[128,1536]{1,0:T(8,128)(2,1)}, bf16[128,1536]{1,0:T(8,128)(2,1)S(1)}, u32[]{:S(2)}, u32[]{:S(2)}) collective-permute-start(bf16[128,1536]{1,0:T(8,128)(2,1)} %get-tuple-element.125.refs_0_.h2_ref), channel_id=1, source_target_pairs={{0,64},{16,80},{32,96},{48,112},{64,0},{80,16},{96,32},{112,48},{1... | collective-permute-start | bytes 1179656 | tf_op jit(solution)/shard_map/ppermute | solution.py:54
  131.4 23.0 %collective-permute-start.23 = (bf16[128,1536]{1,0:T(8,128)(2,1)}, bf16[128,1536]{1,0:T(8,128)(2,1)S(1)}, u32[]{:S(2)}, u32[]{:S(2)}) collective-permute-start(bf16[128,1536]{1,0:T(8,128)(2,1)} %get-tuple-element.125.refs_0_.h2_ref), channel_id=1, source_target_pairs={{0,48},{16,0},{32,16},{48,32},{64,112},{80,64},{96,80},{112,96},{1... | collective-permute-start | bytes 1179656 | tf_op jit(solution)/shard_map/ppermute | solution.py:54
  137.5 17.7 %collective-permute-start.22 = (bf16[128,1536]{1,0:T(8,128)(2,1)S(1)}, bf16[128,1536]{1,0:T(8,128)(2,1)}, u32[]{:S(2)}, u32[]{:S(2)}) collective-permute-start(bf16[128,1536]{1,0:T(8,128)(2,1)S(1)} %copy-done.39), channel_id=1, source_target_pairs={{0,32},{16,48},{32,0},{48,16},{64,96},{80,112},{96,64},{112,80},{1... | collective-permute-start | bytes 1179656 | tf_op jit(solution)/shard_map/ppermute | solution.py:54
  137.7 19.6 %collective-permute-start.21 = (bf16[128,1536]{1,0:T(8,128)(2,1)S(1)}, bf16[128,1536]{1,0:T(8,128)(2,1)}, u32[]{:S(2)}, u32[]{:S(2)}) collective-permute-start(bf16[128,1536]{1,0:T(8,128)(2,1)S(1)} %copy-done.39), channel_id=1, source_target_pairs={{0,16},{16,32},{32,48},{48,0},{64,80},{80,96},{96,112},{112,64},{1... | collective-permute-start | bytes 1179656 | tf_op jit(solution)/shard_map/ppermute | solution.py:54
  150.4 18.6 %collective-permute-start.27 = (bf16[128,1536]{1,0:T(8,128)(2,1)S(1)}, bf16[128,1536]{1,0:T(8,128)(2,1)S(1)}, u32[]{:S(2)}, u32[]{:S(2)}) collective-permute-start(bf16[128,1536]{1,0:T(8,128)(2,1)S(1)} %collective-permute-done.24.refs_0_), channel_id=1, source_target_pairs={{0,48},{16,0},{32,16},{48,32},{64,112},{80,64},{96,80},{112,96},{1... | collective-permute-start | bytes 1179656 | tf_op jit(solution)/shard_map/ppermute | solution.py:54
  154.3 14.7 %collective-permute-start.26 = (bf16[128,1536]{1,0:T(8,128)(2,1)S(1)}, bf16[128,1536]{1,0:T(8,128)(2,1)S(1)}, u32[]{:S(2)}, u32[]{:S(2)}) collective-permute-start(bf16[128,1536]{1,0:T(8,128)(2,1)S(1)} %collective-permute-done.24.refs_0_), channel_id=1, source_target_pairs={{0,32},{16,48},{32,0},{48,16},{64,96},{80,112},{96,64},{112,80},{1... | collective-permute-start | bytes 1179656 | tf_op jit(solution)/shard_map/ppermute | solution.py:54
  154.4 18.9 %collective-permute-start.25 = (bf16[128,1536]{1,0:T(8,128)(2,1)S(1)}, bf16[128,1536]{1,0:T(8,128)(2,1)S(1)}, u32[]{:S(2)}, u32[]{:S(2)}) collective-permute-start(bf16[128,1536]{1,0:T(8,128)(2,1)S(1)} %collective-permute-done.24.refs_0_), channel_id=1, source_target_pairs={{0,16},{16,32},{32,48},{48,0},{64,80},{80,96},{96,112},{112,64},{1... | collective-permute-start | bytes 1179656 | tf_op jit(solution)/shard_map/ppermute | solution.py:54
  179.5 31.3 %collective-permute-start.28 = (bf16[384,384]{1,0:T(8,128)(2,1)}, bf16[384,384]{1,0:T(8,128)(2,1)}, u32[]{:S(2)}, u32[]{:S(2)}) collective-permute-start(bf16[384,384]{1,0:T(8,128)(2,1)} %get-tuple-element.139), channel_id=1, source_target_pairs={{0,16},{16,32},{32,48},{48,0},{64,80},{80,96},{96,112},{112,64},{1... | collective-permute-start | bytes 884744 | tf_op jit(solution)/shard_map/ppermute | solution.py:54
  179.5 31.3 %collective-permute-start.29 = (bf16[384,384]{1,0:T(8,128)(2,1)}, bf16[384,384]{1,0:T(8,128)(2,1)}, u32[]{:S(2)}, u32[]{:S(2)}) collective-permute-start(bf16[384,384]{1,0:T(8,128)(2,1)} %get-tuple-element.140), channel_id=1, source_target_pairs={{0,32},{16,48},{32,0},{48,16},{64,96},{80,112},{96,64},{112,80},{1... | collective-permute-start | bytes 884744 | tf_op jit(solution)/shard_map/ppermute | solution.py:54
  181.6 29.2 %collective-permute-start.30 = (bf16[384,384]{1,0:T(8,128)(2,1)}, bf16[384,384]{1,0:T(8,128)(2,1)}, u32[]{:S(2)}, u32[]{:S(2)}) collective-permute-start(bf16[384,384]{1,0:T(8,128)(2,1)} %get-tuple-element.141), channel_id=1, source_target_pairs={{0,48},{16,0},{32,16},{48,32},{64,112},{80,64},{96,80},{112,96},{1... | collective-permute-start | bytes 884744 | tf_op jit(solution)/shard_map/ppermute | solution.py:54
  216.1 14.5 %collective-permute-start.32 = (bf16[128,1664]{1,0:T(8,128)(2,1)}, bf16[128,1664]{1,0:T(8,128)(2,1)S(1)}, u32[]{:S(2)}, u32[]{:S(2)}) collective-permute-start(bf16[128,1664]{1,0:T(8,128)(2,1)} %get-tuple-element.151), channel_id=1, source_target_pairs={{0,32},{16,48},{32,0},{48,16},{64,96},{80,112},{96,64},{112,80},{1... | collective-permute-start | bytes 1277960 | tf_op jit(solution)/shard_map/ppermute | solution.py:54
  218.2 19.5 %collective-permute-start.33 = (bf16[128,1664]{1,0:T(8,128)(2,1)}, bf16[128,1664]{1,0:T(8,128)(2,1)S(1)}, u32[]{:S(2)}, u32[]{:S(2)}) collective-permute-start(bf16[128,1664]{1,0:T(8,128)(2,1)} %get-tuple-element.152), channel_id=1, source_target_pairs={{0,16},{16,32},{32,48},{48,0},{64,80},{80,96},{96,112},{112,64},{1... | collective-permute-start | bytes 1277960 | tf_op jit(solution)/shard_map/ppermute | solution.py:54
  238.4 14.5 %collective-permute-start.35 = (bf16[128,1664]{1,0:T(8,128)(2,1)}, bf16[128,1664]{1,0:T(8,128)(2,1)S(1)}, u32[]{:S(2)}, u32[]{:S(2)}) collective-permute-start(bf16[128,1664]{1,0:T(8,128)(2,1)} %get-tuple-element.155), channel_id=1, source_target_pairs={{0,32},{16,48},{32,0},{48,16},{64,96},{80,112},{96,64},{112,80},{1... | collective-permute-start | bytes 1277960 | tf_op jit(solution)/shard_map/ppermute | solution.py:54
  240.5 20.0 %collective-permute-start.36 = (bf16[128,1664]{1,0:T(8,128)(2,1)}, bf16[128,1664]{1,0:T(8,128)(2,1)S(1)}, u32[]{:S(2)}, u32[]{:S(2)}) collective-permute-start(bf16[128,1664]{1,0:T(8,128)(2,1)} %get-tuple-element.156), channel_id=1, source_target_pairs={{0,16},{16,32},{32,48},{48,0},{64,80},{80,96},{96,112},{112,64},{1... | collective-permute-start | bytes 1277960 | tf_op jit(solution)/shard_map/ppermute | solution.py:54
  243.3 18.0 %collective-permute-start.37 = (bf16[128,1664]{1,0:T(8,128)(2,1)}, bf16[128,1664]{1,0:T(8,128)(2,1)S(1)}, u32[]{:S(2)}, u32[]{:S(2)}) collective-permute-start(bf16[128,1664]{1,0:T(8,128)(2,1)} %line_grads.1), channel_id=1, source_target_pairs={{0,64},{16,80},{32,96},{48,112},{64,0},{80,16},{96,32},{112,48},{1... | collective-permute-start | bytes 1277960 | tf_op jit(solution)/shard_map/ppermute | solution.py:54
  268.5 13.8 %collective-permute-start.39 = (bf16[128,1536]{1,0:T(8,128)(2,1)}, bf16[128,1536]{1,0:T(8,128)(2,1)S(1)}, u32[]{:S(2)}, u32[]{:S(2)}) collective-permute-start(bf16[128,1536]{1,0:T(8,128)(2,1)} %get-tuple-element.176.refs_4_), channel_id=1, source_target_pairs={{0,32},{16,48},{32,0},{48,16},{64,96},{80,112},{96,64},{112,80},{1... | collective-permute-start | bytes 1179656 | tf_op jit(solution)/shard_map/ppermute | solution.py:54
  269.3 17.5 %collective-permute-start.38 = (bf16[128,1536]{1,0:T(8,128)(2,1)}, bf16[128,1536]{1,0:T(8,128)(2,1)S(1)}, u32[]{:S(2)}, u32[]{:S(2)}) collective-permute-start(bf16[128,1536]{1,0:T(8,128)(2,1)} %get-tuple-element.176.refs_4_), channel_id=1, source_target_pairs={{0,16},{16,32},{32,48},{48,0},{64,80},{80,96},{96,112},{112,64},{1... | collective-permute-start | bytes 1179656 | tf_op jit(solution)/shard_map/ppermute | solution.py:54
  286.9 21.2 %collective-permute-start.44 = (bf16[128,1536]{1,0:T(8,128)(2,1)S(1)}, bf16[128,1536]{1,0:T(8,128)(2,1)S(1)}, u32[]{:S(2)}, u32[]{:S(2)}) collective-permute-start(bf16[128,1536]{1,0:T(8,128)(2,1)S(1)} %copy-done.43), channel_id=1, source_target_pairs={{0,48},{16,0},{32,16},{48,32},{64,112},{80,64},{96,80},{112,96},{1... | collective-permute-start | bytes 1179656 | tf_op jit(solution)/shard_map/ppermute | solution.py:54
  287.7 20.3 %collective-permute-start.45 = (bf16[128,1536]{1,0:T(8,128)(2,1)S(1)}, bf16[128,1536]{1,0:T(8,128)(2,1)S(1)}, u32[]{:S(2)}, u32[]{:S(2)}) collective-permute-start(bf16[128,1536]{1,0:T(8,128)(2,1)S(1)} %copy-done.41), channel_id=1, source_target_pairs={{0,32},{16,48},{32,0},{48,16},{64,96},{80,112},{96,64},{112,80},{1... | collective-permute-start | bytes 1179656 | tf_op jit(solution)/shard_map/ppermute | solution.py:54
  289.6 18.5 %collective-permute-start.46 = (bf16[128,1536]{1,0:T(8,128)(2,1)S(1)}, bf16[128,1536]{1,0:T(8,128)(2,1)S(1)}, u32[]{:S(2)}, u32[]{:S(2)}) collective-permute-start(bf16[128,1536]{1,0:T(8,128)(2,1)S(1)} %copy-done.40), channel_id=1, source_target_pairs={{0,16},{16,32},{32,48},{48,0},{64,80},{80,96},{96,112},{112,64},{1... | collective-permute-start | bytes 1179656 | tf_op jit(solution)/shard_map/ppermute | solution.py:54
  309.0 19.6 %collective-permute-start.41 = (bf16[128,3072]{1,0:T(8,128)(2,1)}, bf16[128,3072]{1,0:T(8,128)(2,1)S(1)}, u32[]{:S(2)}, u32[]{:S(2)}) collective-permute-start(bf16[128,3072]{1,0:T(8,128)(2,1)} %get-tuple-element.182), channel_id=1, source_target_pairs={{0,48},{16,0},{32,16},{48,32},{64,112},{80,64},{96,80},{112,96},{1... | collective-permute-start | bytes 2359304 | tf_op jit(solution)/shard_map/ppermute | solution.py:54
  311.6 20.5 %collective-permute-start.42 = (bf16[128,3072]{1,0:T(8,128)(2,1)}, bf16[128,3072]{1,0:T(8,128)(2,1)S(1)}, u32[]{:S(2)}, u32[]{:S(2)}) collective-permute-start(bf16[128,3072]{1,0:T(8,128)(2,1)} %get-tuple-element.184), channel_id=1, source_target_pairs={{0,16},{16,32},{32,48},{48,0},{64,80},{80,96},{96,112},{112,64},{1... | collective-permute-start | bytes 2359304 | tf_op jit(solution)/shard_map/ppermute | solution.py:54
  317.1 53.9 %collective-permute-start.49 = (bf16[2,96,1152]{2,1,0:T(8,128)(2,1)}, bf16[2,96,1152]{2,1,0:T(8,128)(2,1)S(1)}, u32[]{:S(2)}, u32[]{:S(2)}) collective-permute-start(bf16[2,96,1152]{2,1,0:T(8,128)(2,1)} %get-tuple-element.196), channel_id=1, source_target_pairs={{0,2},{1,3},{2,4},{3,5},{4,6},{5,7},{6,0},{7,1},{8,10},{9,11},{10,... | collective-permute-start | bytes 1327112 | tf_op jit(solution)/shard_map/ppermute | solution.py:67
  318.7 52.4 %collective-permute-start.50 = (bf16[2,96,1152]{2,1,0:T(8,128)(2,1)}, bf16[2,96,1152]{2,1,0:T(8,128)(2,1)S(1)}, u32[]{:S(2)}, u32[]{:S(2)}) collective-permute-start(bf16[2,96,1152]{2,1,0:T(8,128)(2,1)} %get-tuple-element.197), channel_id=1, source_target_pairs={{0,4},{1,5},{2,6},{3,7},{4,0},{5,1},{6,2},{7,3},{8,12},{9,13},{10,... | collective-permute-start | bytes 1327112 | tf_op jit(solution)/shard_map/ppermute | solution.py:67
  322.3 48.8 %collective-permute-start.51 = (bf16[2,96,1152]{2,1,0:T(8,128)(2,1)}, bf16[2,96,1152]{2,1,0:T(8,128)(2,1)S(1)}, u32[]{:S(2)}, u32[]{:S(2)}) collective-permute-start(bf16[2,96,1152]{2,1,0:T(8,128)(2,1)} %get-tuple-element.198), channel_id=1, source_target_pairs={{0,6},{1,7},{2,0},{3,1},{4,2},{5,3},{6,4},{7,5},{8,14},{9,15},{10,... | collective-permute-start | bytes 1327112 | tf_op jit(solution)/shard_map/ppermute | solution.py:67
  332.1 62.7 %collective-permute-start.43 = (bf16[128,3072]{1,0:T(8,128)(2,1)}, bf16[128,3072]{1,0:T(8,128)(2,1)S(1)}, u32[]{:S(2)}, u32[]{:S(2)}) collective-permute-start(bf16[128,3072]{1,0:T(8,128)(2,1)} %get-tuple-element.185), channel_id=1, source_target_pairs={{0,32},{16,48},{32,0},{48,16},{64,96},{80,112},{96,64},{112,80},{1... | collective-permute-start | bytes 2359304 | tf_op jit(solution)/shard_map/ppermute | solution.py:54
  378.9 13.1 %collective-permute-start.53 = (bf16[96,1152]{1,0:T(8,128)(2,1)S(1)}, bf16[96,1152]{1,0:T(8,128)(2,1)S(1)}, u32[]{:S(2)}, u32[]{:S(2)}) collective-permute-start(bf16[96,1152]{1,0:T(8,128)(2,1)S(1)} %get-tuple-element.215.a_ref), channel_id=1, source_target_pairs={{0,64},{1,65},{2,66},{3,67},{4,68},{5,69},{6,70},{7,71},{8,72},{9,... | collective-permute-start | bytes 663560 | tf_op jit(solution)/shard_map/ppermute | solution.py:80
  383.3 16.1 %collective-permute-start.47 = (bf16[128,1536]{1,0:T(8,128)(2,1)}, bf16[128,1536]{1,0:T(8,128)(2,1)S(1)}, u32[]{:S(2)}, u32[]{:S(2)}) collective-permute-start(bf16[128,1536]{1,0:T(8,128)(2,1)} %line_results.1), channel_id=1, source_target_pairs={{0,64},{16,80},{32,96},{48,112},{64,0},{80,16},{96,32},{112,48},{1... | collective-permute-start | bytes 1179656 | tf_op jit(solution)/shard_map/ppermute | solution.py:54
  394.8 15.7 %collective-permute-start.57 = (bf16[96,1152]{1,0:T(8,128)(2,1)}, bf16[96,1152]{1,0:T(8,128)(2,1)S(1)}, u32[]{:S(2)}, u32[]{:S(2)}) collective-permute-start(bf16[96,1152]{1,0:T(8,128)(2,1)} %sum_across.1.refs_0_), channel_id=1, source_target_pairs={{0,48},{16,0},{32,16},{48,32},{64,112},{80,64},{96,80},{112,96},{1... | collective-permute-start | bytes 663560 | tf_op jit(solution)/shard_map/ppermute | solution.py:54
  (66 other events, 589.3 us)
Sparse Core Ops, SparseCore 0:
  10.1 153.1 all-gather.1
  210.9 153.0 reduce-scatter.1
